TPU v7x, 32 devices: a whole 2x2x4 slice. The times are simulated.
32 devices in a mesh: grp: 4 (over y, x), pen: 8 (over z, core).
Axes of the slice: x: 2, y: 2, z: 4, core: 2. Of those that a mesh axis runs over, the one named last changes fastest.
Arguments:
- flow_fields: float32 [4, 4, 1536, 1536], P(None, 'grp', 'pen'), may hold values from -6 to 6
- marker_cells: int32 [4, 8, 1024, 8], P('grp', 'pen'), may hold values from 0 to 294911
- marker_weights: float32 [4, 8, 1024, 8], P('grp', 'pen'), may hold values from 0.05 to 0.3
- solid_blocks: int32 [4, 1536, 12], P('grp', 'pen'), may hold values 0 or 1
Outputs:
- velocity_next: float32 [3, 4, 1536, 1536], P(None, 'grp', 'pen')
- poisson_source: float32 [4, 1536, 1536], P(None, 'pen', 'grp')
Inputs may be any that keep to these rules, and one draw needn't show every extreme that they name: `marker_cells`: each entry numbers a cell of the device's own home block of 294912 cells, first dimension slowest, third fastest.
All inputs are finite; a program needn't handle non-finite values. No bound on the sum of `solid_blocks` on one device may be relied on, other than what follows from the above.
Results may differ from a plain program's by a relative error of at most 0.0003.
Values sent between devices are 32-bit elements; how exact they have to be, the bound alone decides.
No kernel may reach another device: no remote copies, remote signals or barrier semaphores. Data moves between devices by JAX's collectives and lax.ppermute only.
A program may use at most 128 MiB of HBM per device.

v0:
```python
import math

import jax
import jax.numpy as jnp
from jax import lax
from jax.sharding import PartitionSpec as P


def compact(line_data):
    length = line_data.shape[0]
    padded = jnp.pad(line_data, ((2, 2), (0, 0)))
    source = 14.0 / 9.0 * 0.5 * (padded[3:-1] - padded[1:-3]) + 1.0 / 9.0 * 0.25 * (
        padded[4:] - padded[:-4]
    )
    lower_band = jnp.full((length,), 1.0 / 3.0, dtype=line_data.dtype).at[0].set(0.0)
    upper_band = jnp.full((length,), 1.0 / 3.0, dtype=line_data.dtype).at[length - 1].set(0.0)
    middle_band = jnp.ones((length,), dtype=line_data.dtype)
    return lax.linalg.tridiagonal_solve(lower_band, middle_band, upper_band, source)


def compact_along(block_data, axis):
    reordered = jnp.moveaxis(block_data, axis, 0)
    shaped = reordered.shape
    result = compact(reordered.reshape(shaped[0], -1)).reshape(shaped)
    return jnp.moveaxis(result, 0, axis)


def circulant_block(lag_block, block_width, length):
    out_rows = lax.iota(jnp.int32, block_width)
    in_columns = lax.iota(jnp.int32, block_width)
    offset = (lag_block * block_width + out_rows[:, None] - in_columns[None, :]) % length
    phases = math.pi / length * offset.astype(jnp.float32)
    parity = (1 - 2 * (offset % 2)).astype(jnp.float32)
    nonzero = offset != 0
    sine_values = jnp.where(nonzero, jnp.sin(phases), 1.0)
    return jnp.where(nonzero, math.pi / length * parity * jnp.cos(phases) / sine_values, 0.0)


def spectral_along(block_data, axis):
    reordered = jnp.moveaxis(block_data, axis, -1)
    shaped = reordered.shape
    length = shaped[-1]
    block_width = math.gcd(length, 384)
    block_count = length // block_width
    line_blocks = reordered.reshape(-1, block_count, block_width)
    result = jnp.zeros_like(line_blocks)
    for lag_block in range(block_count):
        table_block = circulant_block(lag_block, block_width, length)
        shifted = jnp.roll(line_blocks, lag_block, axis=1)
        result = result + jnp.einsum(
            "xas,rs->xar",
            shifted,
            table_block,
            precision=lax.Precision.HIGHEST,
            preferred_element_type=jnp.float32,
        )
    return jnp.moveaxis(result.reshape(shaped), -1, axis)


def terms_for(fields, slopes, direction):
    carried = -fields[direction][None] * slopes[:3]
    return carried.at[direction].add(-slopes[3])


def body(flow_fields, marker_cells, marker_weights, solid_blocks):
    slopes_z = spectral_along(flow_fields, 3)
    tendency = terms_for(flow_fields, slopes_z, 2)
    pencil = lax.all_to_all(flow_fields, "pen", split_axis=3, concat_axis=2, tiled=True)
    slopes = spectral_along(pencil, 2)
    returned = jnp.concatenate([terms_for(pencil, slopes, 1), slopes[1][None]], axis=0)
    second_part = lax.all_to_all(returned, "pen", split_axis=2, concat_axis=3, tiled=True)
    tendency = tendency + second_part[:3]
    pencil = lax.all_to_all(flow_fields, "grp", split_axis=3, concat_axis=1, tiled=True)
    slopes = compact_along(pencil, 1)
    returned = jnp.concatenate([terms_for(pencil, slopes, 0), slopes[0][None]], axis=0)
    first_part = lax.all_to_all(returned, "grp", split_axis=1, concat_axis=3, tiled=True)
    tendency = tendency + first_part[:3]
    divergence = slopes_z[2] + second_part[3] + first_part[3]
    poisson_source = lax.all_to_all(divergence, "grp", split_axis=2, concat_axis=0, tiled=True)
    provisional = flow_fields[:3] + 0.1 * tendency
    shaped = provisional.shape
    flattened = provisional.reshape(3, -1)
    cells_index = marker_cells[0, 0].reshape(-1)
    weights = marker_weights[0, 0]
    gathered = flattened[:, cells_index].reshape(3, weights.shape[0], weights.shape[1])
    sampled = jnp.sum(gathered * weights[None], axis=2)
    spread = (sampled[..., None] * weights[None]).reshape(3, -1)
    correction = jnp.zeros_like(flattened).at[:, cells_index].add(spread).reshape(shaped)
    block_cells = flow_fields.shape[3] // solid_blocks.shape[2]
    solid = jnp.repeat(solid_blocks, block_cells, axis=2).astype(jnp.float32)
    velocity_next = (1.0 - solid)[None] * (provisional - correction)
    return (velocity_next, poisson_source)


def solution(mesh):
    return jax.shard_map(
        body,
        mesh=mesh,
        in_specs=(
            P(None, "grp", "pen", None),
            P("grp", "pen", None, None),
            P("grp", "pen", None, None),
            P("grp", "pen", None),
        ),
        out_specs=(P(None, "grp", "pen", None), P(None, "pen", "grp")),
        check_vma=False,
    )
```

profile of v0, /device:TPU:9, one launch (start us, length us, event | category | flops | bytes accessed | tf_op | source)
XLA Modules:
  0.0 1550.9 jit_solution(8500824506663920362)
XLA Ops:
  0.6 7.0 copy.195
  12.9 6.2 reshape.340
  19.1 63.2 %all-to-all-done.2 = f32[4,1,192,1536]{2,0,1,3:T(4,128)} async-done(((f32[4,1,192,1536]{2,0,1,3:T(4,128)}), f32[4,1,192,1536]{2,0,1,3:T(4,128)}, u32[]{:S(2)}, u32[]{:S(2)}) %all-to-all-start.2) | async-done | bytes 4718624 | tf_op jit(solution)/shard_map/all_to_all | solution.py:73
  82.3 6.4 all-to-all-start
  88.7 7.2 copy.237
  106.7 7.3 copy.214
  114.0 28.0 %fusion.181 = (f32[294912]{0:T(1024)S(1)}, f32[294912]{0:T(1024)S(1)}, f32[294912]{0:T(1024)}, f32[1,294912]{1,0:T(1,128)S(1)}) fusion(f32[4,294912]{1,0:T(4,128)} %fusion.3), kind=kLoop, calls=%fused_computation.231 | loop fusion | flops 4423680 | bytes 9437184 | tf_op jit(solution)/shard_map/eval_jaxpr/sub | solution.py:18
  152.8 71.3 %all-to-all-done = f32[4,1,192,1536]{2,0,1,3:T(4,128)} async-done(((f32[4,1,192,1536]{2,0,1,3:T(4,128)}), f32[4,1,192,1536]{2,0,1,3:T(4,128)}, u32[]{:S(2)}, u32[]{:S(2)}) %all-to-all-start) | async-done | bytes 4718624 | tf_op jit(solution)/shard_map/all_to_all | solution.py:68
  229.0 9.1 copy.264
  238.1 7.6 all_to_all.64
  245.7 6.6 reshape.341
  252.3 8.0 fusion.184
  265.6 12.8 fusion.18
  278.5 13.0 fusion.22
  291.5 7.6 copy.233
  302.0 13.1 fusion.89
  315.1 13.2 fusion.31
  328.3 6.6 copy.209
  334.9 6.4 reshape.342
  352.0 7.1 copy.210
  359.0 8.8 all-to-all-start.1
  367.9 9.5 fusion.187
  389.7 11.0 fusion.6
  400.7 12.9 fusion.10
  413.6 13.0 fusion.91
  426.6 14.9 fusion.33
  479.3 23.5 %all-to-all-done.1 = f32[4,1,1536,192]{3,0,1,2:T(4,128)} async-done(((f32[4,1,1536,192]{3,0,1,2:T(4,128)}), f32[4,1,1536,192]{3,0,1,2:T(4,128)}, u32[]{:S(2)}, u32[]{:S(2)}) %all-to-all-start.1) | async-done | bytes 4718624 | tf_op jit(solution)/shard_map/all_to_all | solution.py:71
  502.9 6.4 copy.265
  528.0 6.7 slice_add_fusion
  539.3 129.2 %gather_fusion = f32[8192,3]{0,1:T(4,128)} fusion(f32[3,294912]{1,0:T(4,128)} %bitcast.124, s32[8192]{0:T(1024)} %broadcast_clamp_fusion), kind=kCustom, calls=%fused_computation | custom fusion | bytes 229376 | tf_op jit(solution)/shard_map/gather | solution.py:85
  681.9 858.1 %scatter_fusion = f32[3,294912]{1,0:T(4,128)} fusion(f32[3,294912]{1,0:T(4,128)} %broadcast_in_dim.54, s32[8192]{0:T(1024)} %bitcast.158, f32[8192,3]{0,1:T(4,128)} %multiply_bitcast_fusion), kind=kCustom, calls=%fused_computation.1 | custom fusion | flops 24576 | bytes 327680 | tf_op jit(solution)/shard_map/scatter-add | solution.py:88
  1539.9 5.8 fusion.35
  (120 shorter events, 141.9 us)
Async XLA Ops:
  7.6 74.6 %all-to-all-start.2 = ((f32[4,1,192,1536]{2,0,1,3:T(4,128)}), f32[4,1,192,1536]{2,0,1,3:T(4,128)}, u32[]{:S(2)}, u32[]{:S(2)}) async-start(f32[4,1,192,1536]{2,0,1,3:T(4,128)} %copy.195), calls=%async_computation.2 | async-start | bytes 12582912 | tf_op jit(solution)/shard_map/all_to_all | solution.py:73
  82.3 141.8 %all-to-all-start = ((f32[4,1,192,1536]{2,0,1,3:T(4,128)}), f32[4,1,192,1536]{2,0,1,3:T(4,128)}, u32[]{:S(2)}, u32[]{:S(2)}) async-start(f32[4,1,192,1536]{2,0,1,3:T(4,128)} %copy.195), calls=%async_computation | async-start | bytes 12582912 | tf_op jit(solution)/shard_map/all_to_all | solution.py:68
  224.1 135.0 %all-to-all-start.3 = ((f32[4,4,192,384]{3,2,0,1:T(8,128)}), f32[4,4,192,384]{3,2,0,1:T(8,128)}, u32[]{:S(2)}, u32[]{:S(2)}) async-start(f32[4,4,192,384]{3,2,0,1:T(8,128)} %pad_maximum_fusion.1), calls=%async_computation.3 | async-start | bytes 9437184 | tf_op jit(solution)/shard_map/all_to_all | solution.py:76
  252.3 8.1 copy-start
  299.1 2.7 copy-start.3
  299.1 15.9 %slice-start.8 = ((s8[4718592]{0:T(1024)(128)(4,1)}), s8[4194304]{0:T(1024)(128)(4,1)S(1)}, s32[]{:S(2)}) async-start(s8[4718592]{0:T(1024)(128)(4,1)} %bitcast.153), calls=%async_computation.13 | async-start | bytes 8388608
  301.8 13.2 slice-start.6
  301.9 13.2 slice-start.9
  302.0 13.1 slice-start.7
  343.9 4.5 slice-start.2
  345.4 3.6 slice-start.3
  359.0 22.7 %slice-start = ((s8[4718592]{0:T(1024)(128)(4,1)}), s8[524288]{0:T(1024)(128)(4,1)S(1)}, s32[]{:S(2)}) async-start(s8[4718592]{0:T(1024)(128)(4,1)} %bitcast.125), calls=%async_computation.5 | async-start | bytes 1048576
  359.0 143.8 %all-to-all-start.1 = ((f32[4,1,1536,192]{3,0,1,2:T(4,128)}), f32[4,1,1536,192]{3,0,1,2:T(4,128)}, u32[]{:S(2)}, u32[]{:S(2)}) async-start(f32[4,1,1536,192]{3,0,1,2:T(4,128)} %copy.210), calls=%async_computation.1 | async-start | bytes 12582912 | tf_op jit(solution)/shard_map/all_to_all | solution.py:71
  367.9 13.9 slice-start.1
  383.7 2.2 slice-start.4
  385.5 2.2 slice-start.5
  387.7 2.0 copy-start.4
  460.3 7.1 copy-start.1
  461.9 2.9 copy-start.6
  464.9 0.6 copy-start.5
  467.5 2.3 copy-start.2
  518.1 1027.7 %all-to-all-start.4 = ((f32[1,192,1536]{1,0,2:T(1,128)}), f32[1,192,1536]{1,0,2:T(1,128)}, u32[]{:S(2)}, u32[]{:S(2)}) async-start(f32[1,192,1536]{1,0,2:T(1,128)} %copy.222), calls=%async_computation.4 | async-start | bytes 3145728 | tf_op jit(solution)/shard_map/all_to_all | solution.py:79
where the time goes:
time: 1580 us; the launch traced here: 1550 us
  other arithmetic  933 us (59%)
  local copies, waits for them, and re-layouts  325 us (21%)
  waiting for transfers between devices  158 us (10%)
  matrix products  104 us (7%)
  starting transfers between devices  30 us (2%)
    scatter-add x1, other arithmetic, body(): jnp.zeros_like(flattened).at[:, cells_index].add(spread).reshape(shaped)  858 us
    gather x1, local copies, waits for them, and re-layouts, body(): flattened[:, cells_index].reshape(3, weights.shape[0], weights.shape[1])  129 us
    dot_general x8, matrix products, spectral_along(): jnp.einsum('xas,rs->xar', shifted, table_block, precision=lax.Precision.H...  104 us
    all_to_all x1, waiting for transfers between devices, body(): lax.all_to_all(flow_fields, 'pen', split_axis=3, concat_axis=2, tiled=True)  71.3 us
    all_to_all x1, waiting for transfers between devices, body(): lax.all_to_all(flow_fields, 'grp', split_axis=3, concat_axis=1, tiled=True)  63.2 us
    unnamed x55, local copies, waits for them, and re-layouts  37.1 us
  transfers between devices with their start and end apart: 5, of which 3 were waited for; matrix products, arithmetic and copies ran while one was open for 85% of the time, Pallas kernels for 0%

commit v1 on v0

v1 whole, which is shorter than its diff:
```python
import functools
import math

import jax
import jax.numpy as jnp
import ml_dtypes
import numpy as np
from jax import lax
from jax.experimental import pallas as pl
from jax.experimental.pallas import tpu as pltpu
from jax.sharding import PartitionSpec as P

LANES = 128
CHUNK = 256
FIELD_ORDER = (1, 3, 0, 2)
ANY = pl.BlockSpec(memory_space=pl.ANY)
SMEM = pl.BlockSpec(memory_space=pltpu.SMEM)
VMEM = pl.BlockSpec(memory_space=pltpu.VMEM)
BF = jnp.bfloat16
F32 = jnp.float32


def split_table(length):
    half = length // 2
    lag = np.arange(length)
    row = np.zeros(length)
    row[1:] = math.pi / length * (1 - 2 * (lag[1:] % 2)) / np.tan(math.pi * lag[1:] / length)
    row[half] = 0.0
    offset = np.arange(half)[:, None] - np.arange(half)[None, :]
    same, other = row[offset % length], row[(offset + half) % length]
    table = np.stack([(same + other) / 2, (same - other) / 2])
    high = table.astype(ml_dtypes.bfloat16)
    low = (table - high.astype(np.float64)).astype(ml_dtypes.bfloat16)
    return high, low


def compact_matrix(length):
    eye = np.eye(length)
    off = lambda k: np.eye(length, k=k)
    left = eye + (off(1) + off(-1)) / 3
    right = 7 / 9 * (off(1) - off(-1)) + 1 / 36 * (off(2) - off(-2))
    return np.linalg.solve(left, right).astype(np.float32)


def two_terms(value):
    high = value.astype(BF)
    return high, (value - high.astype(F32)).astype(BF)


def dot(a, b):
    return jnp.dot(a, b, preferred_element_type=F32)


def dot_t(a, b):
    return lax.dot_general(a, b, (((1,), (1,)), ((), ())), preferred_element_type=F32)


def params(mib, **more):
    return pltpu.CompilerParams(vmem_limit_bytes=mib * 2**20, **more)


def cost(flops, moved):
    return pl.CostEstimate(flops=int(flops), bytes_accessed=int(moved), transcendentals=0)


class Plan:
    def __init__(self, pens, rows, depth):
        self.pens, self.rows, self.depth = pens, rows, depth
        self.tiles = depth // LANES
        self.pairs = len(FIELD_ORDER) * self.tiles
        self.rounds = -(-self.pairs // pens)
        first = min(-(-2 * self.tiles // pens), self.rounds)
        self.stages = [list(range(first))]
        if first < self.rounds:
            self.stages.append(list(range(first, self.rounds)))

    def place(self, round_, pen):
        pair = jnp.minimum(round_ * self.pens + pen, self.pairs - 1)
        slot, tile = pair // self.tiles, pair % self.tiles
        field = jnp.int32(FIELD_ORDER[0])
        for i, f in enumerate(FIELD_ORDER[1:], 1):
            field = jnp.where(slot == i, f, field)
        return field, pl.multiple_of(tile * LANES, LANES)


def run_copies(copies):
    for c in copies:
        c.start()
    for c in copies:
        c.wait()


def pack_lines(plan, rounds, me, flow):
    n = plan.pens

    def kernel(me_ref, flow_ref, *rest):
        outs, sems = rest[:-1], rest[-1]
        copies = []
        for s in range(1, n):
            pen = lax.rem(me_ref[0] + s, n)
            for k, r in enumerate(rounds):
                field, z = plan.place(r, pen)
                copies.append(pltpu.make_async_copy(
                    flow_ref.at[field, 0, :, pl.ds(z, LANES)], outs[s - 1].at[k], sems.at[len(copies)]))
        run_copies(copies)

    shape = jax.ShapeDtypeStruct((len(rounds), plan.rows, LANES), F32)
    size = 4 * len(rounds) * plan.rows * LANES * n
    return pl.pallas_call(
        kernel, out_shape=[shape] * (n - 1), in_specs=[SMEM, ANY], out_specs=[ANY] * (n - 1),
        scratch_shapes=[pltpu.SemaphoreType.DMA(((n - 1) * len(rounds),))],
        compiler_params=params(4), cost_estimate=cost(0, 2 * size), name="pack_lines",
    )(me, flow)


def line_slopes(plan, rounds, groups, me, flow, received, tables):
    n, rows = plan.pens, plan.rows
    length, half, count = n * rows, n * rows // 2, len(rounds)
    wide = count * LANES
    block = math.gcd(half, 256)

    def kernel(me_ref, flow_ref, high_ref, low_ref, *rest):
        ins = rest[: n - 1]
        outs = rest[n - 1 : n - 1 + n * len(groups)]
        lines, result, x_high, x_low, in_sems, out_sems = rest[n - 1 + n * len(groups) :]
        mine = me_ref[0]
        copies = []
        for s in range(1, n):
            pen = lax.rem(mine + n - s, n)
            at = pl.ds(pl.multiple_of(pen * rows, 8), rows)
            copies.append(pltpu.make_async_copy(ins[s - 1], lines.at[:, at, :], in_sems.at[len(copies)]))
        at = pl.ds(pl.multiple_of(mine * rows, 8), rows)
        for k, r in enumerate(rounds):
            field, z = plan.place(r, mine)
            copies.append(pltpu.make_async_copy(
                flow_ref.at[field, 0, :, pl.ds(z, LANES)], lines.at[k, at, :], in_sems.at[len(copies)]))
        run_copies(copies)

        @pl.loop(0, half // block)
        def _(b):
            upper = pl.ds(pl.multiple_of(b * block, block), block)
            lower = pl.ds(pl.multiple_of(b * block + half, block), block)
            for k in range(count):
                to = pl.ds(k * LANES, LANES)
                first, second = lines[k, upper, :], lines[k, lower, :]
                for part, value in enumerate((first + second, first - second)):
                    h, l = two_terms(value)
                    x_high[part, upper, to] = h
                    x_low[part, upper, to] = l

        @pl.loop(0, half // block)
        def _(b):
            upper = pl.ds(pl.multiple_of(b * block, block), block)
            lower = pl.ds(pl.multiple_of(b * block + half, block), block)
            parts = []
            for part in range(2):
                t_high, t_low = high_ref[part, upper, :], low_ref[part, upper, :]
                h, l = x_high[part], x_low[part]
                parts.append(dot(t_high, h) + (dot(t_high, l) + dot(t_low, h)))
            top, bottom = parts[0] + parts[1], parts[0] - parts[1]
            for k in range(count):
                result[k, upper, :] = top[:, k * LANES : (k + 1) * LANES]
                result[k, lower, :] = bottom[:, k * LANES : (k + 1) * LANES]

        copies = []
        for g, group in enumerate(groups):
            at_k = pl.ds(rounds.index(group[0]), len(group))
            for s in range(n):
                pen = lax.rem(mine + s, n)
                at = pl.ds(pl.multiple_of(pen * rows, 8), rows)
                copies.append(pltpu.make_async_copy(
                    result.at[at_k, at, :], outs[g * n + s], out_sems.at[len(copies)]))
        run_copies(copies)

    shapes = [jax.ShapeDtypeStruct((len(g), rows, LANES), F32) for g in groups for _ in range(n)]
    out = pl.pallas_call(
        kernel, out_shape=shapes,
        in_specs=[SMEM, ANY, VMEM, VMEM] + [ANY] * (n - 1), out_specs=[ANY] * len(shapes),
        scratch_shapes=[
            pltpu.VMEM((count, length, LANES), F32), pltpu.VMEM((count, length, LANES), F32),
            pltpu.VMEM((2, half, wide), BF), pltpu.VMEM((2, half, wide), BF),
            pltpu.SemaphoreType.DMA((n - 1 + count,)), pltpu.SemaphoreType.DMA((len(shapes),)),
        ],
        compiler_params=params(32),
        cost_estimate=cost(12 * half * half * wide, 8 * count * length * LANES + 8 * half * half),
        name="line_slopes",
    )(me, flow, *tables, *received)
    return [out[g * n : (g + 1) * n] for g in range(len(groups))]


def depth_terms(flow, tables):
    fields, _, rows, depth = flow.shape
    half = depth // 2
    step = math.gcd(rows, 48)

    def kernel(flow_ref, high_ref, low_ref, base_ref, slope_ref):
        value = flow_ref[:, 0].reshape(fields * step, depth)
        parts = []
        for part, x in enumerate((value[:, :half] + value[:, half:], value[:, :half] - value[:, half:])):
            h, l = two_terms(x)
            parts.append(dot(h, high_ref[part]) + (dot(l, high_ref[part]) + dot(h, low_ref[part])))
        minus = jnp.concatenate([parts[0] + parts[1], parts[0] - parts[1]], axis=1)
        rows_of = lambda f: minus[f * step : (f + 1) * step]
        speed = flow_ref[2, 0]
        for i in range(3):
            term = speed * rows_of(i)
            if i == 2:
                term = term + rows_of(3)
                slope_ref[...] = -rows_of(2)
            base_ref[i] = flow_ref[i, 0] + 0.1 * term

    whole = pl.BlockSpec((2, half, half), lambda r: (0, 0, 0), pipeline_mode=pl.Buffered(1))
    size = 4 * fields * rows * depth
    return pl.pallas_call(
        kernel, grid=(rows // step,),
        out_shape=[jax.ShapeDtypeStruct((3, rows, depth), F32), jax.ShapeDtypeStruct((rows, depth), F32)],
        in_specs=[pl.BlockSpec((fields, 1, step, depth), lambda r: (0, 0, r, 0)), whole, whole],
        out_specs=[pl.BlockSpec((3, step, depth), lambda r: (0, r, 0)), pl.BlockSpec((step, depth), lambda r: (r, 0))],
        compiler_params=params(40), cost_estimate=cost(12 * fields * rows * half * half, 2 * size + 8 * half * half),
        name="depth_terms",
    )(flow, *tables)


def slab_terms(coefficients, planes):
    n = len(planes)
    fields, rows, width = planes[0].shape
    step = math.gcd(rows, 48)

    def kernel(c_ref, *refs):
        ins, outs, slopes = refs[:n], refs[n : 2 * n], refs[2 * n]
        for to in range(n):
            speed = ins[(n - to) % n][0]
            for f in range(fields):
                slope = c_ref[to, 0] * ins[0][f]
                for s in range(1, n):
                    slope = slope + c_ref[to, s] * ins[s][f]
                if f == 0:
                    slopes[to] = slope
                if f < 3:
                    outs[to][f] = speed * slope
                else:
                    outs[to][0] += slope

    size = 4 * n * fields * rows * width
    out = pl.pallas_call(
        kernel, grid=(rows // step,),
        out_shape=[jax.ShapeDtypeStruct((3, rows, width), F32)] * n + [jax.ShapeDtypeStruct((n, rows, width), F32)],
        in_specs=[SMEM] + [pl.BlockSpec((fields, step, width), lambda r: (0, r, 0))] * n,
        out_specs=[pl.BlockSpec((3, step, width), lambda r: (0, r, 0))] * n
        + [pl.BlockSpec((n, step, width), lambda r: (0, r, 0))],
        compiler_params=params(32), cost_estimate=cost(n * size, 2 * size), name="slab_terms",
    )(coefficients, *planes)
    return out[:n], out[n]


def solve_layout(me, slopes, parts):
    n = len(parts)

    def kernel(me_ref, slopes_ref, *refs):
        out = refs[n]
        for s in range(n):
            out[lax.rem(me_ref[0] + n - s, n)] = refs[s][...] + slopes_ref[(n - s) % n]

    return pl.pallas_call(
        kernel, out_shape=jax.ShapeDtypeStruct(slopes.shape, F32), in_specs=[SMEM] + [VMEM] * (n + 1), out_specs=VMEM,
        compiler_params=params(16), cost_estimate=cost(slopes.size, 12 * slopes.size), name="solve_layout",
    )(me, slopes, *parts)


def marker_order(cells, weights, rows, depth):
    markers, stencil = weights.shape
    tiles, entries = depth // LANES, markers * stencil
    chunks = entries // CHUNK
    marker = lax.iota(jnp.int32, entries) // stencil
    flat = cells.reshape(-1)
    row, z = flat // depth, flat % depth
    place = (z // LANES * rows + row) * LANES + z % LANES
    weight = weights.reshape(-1)
    if rows * depth * markers < 2**31:
        key, weight = lax.sort((place * markers + marker, weight), num_keys=1)
        place, marker = key // markers, key % markers
    else:
        place, marker, weight = lax.sort((place, marker, weight), num_keys=1)
    shape = (chunks, 1, CHUNK)
    tile_row, lane = place // LANES, place % LANES
    tile = (tile_row // rows).reshape(chunks, CHUNK)
    first, last = tile[:, 0], tile[:, -1]
    end = jnp.cumsum(last - first + 1)
    start = end - (last - first + 1)
    pairs = chunks + tiles
    index = lax.iota(jnp.int32, pairs)
    chunk = jnp.minimum(jnp.sum((end[None, :] <= index[:, None]).astype(jnp.int32), axis=1), chunks - 1)
    pick = chunk[:, None] == lax.iota(jnp.int32, chunks)[None, :]
    at = jnp.sum(jnp.where(pick, (first - start)[None, :], 0), axis=1) + index
    at = jnp.where(index < end[-1], at, tiles)
    return chunk, at, tile_row.reshape(shape), lane.reshape(shape), marker.reshape(shape), weight.reshape(shape)


def home_step(plan, component, me, flow, base, across, slope_z, groups, order, solid, out):
    n, rows, depth, tiles = plan.pens, plan.rows, plan.depth, plan.tiles
    wanted = (1, 3) if component == 1 else (component,)
    slots = [FIELD_ORDER.index(f) for f in wanted]
    used = {r for slot in slots for r in range(slot * tiles // n, ((slot + 1) * tiles - 1) // n + 1)}
    low, span = min(used), max(used) - min(used) + 1
    sources = [(group, k, r, s) for group, _ in groups for k, r in enumerate(group) if r in used for s in range(n)]
    buffers = [b for group, bs in groups if used & set(group) for b in bs]
    starts, total = {}, 0
    for group, bs in groups:
        if used & set(group):
            starts[tuple(group)] = total
            total += n
    chunk_of, tile_of, *entries = order
    pairs = chunk_of.shape[0]
    chunks = entries[0].shape[0]
    markers = chunks * CHUNK // 8
    with_div = component == 1
    marker_rows = plan.marker_rows

    def kernel(me_ref, chunk_ref, tile_ref, flow_ref, base_ref, across_ref, slope_ref, row_ref, lane_ref, marker_ref,
               weight_ref, solid_ref, *rest):
        bufs = rest[:total]
        rest = rest[total:]
        if out is not None:
            rest = rest[1:]
        out_ref, rest = rest[0], rest[1:]
        if with_div:
            div_ref, rest = rest[0], rest[1:]
        slopes, speed, value, cross, third, prov, terms, sems = rest
        mine = me_ref[0]
        copies = []

        def copy(src, dst):
            copies.append(pltpu.make_async_copy(src, dst, sems.at[len(copies)]))

        copy(flow_ref.at[1, 0], speed)
        copy(base_ref.at[component], value)
        copy(across_ref.at[component], cross)
        if with_div:
            copy(slope_ref, third)
        for group, k, r, s in sources:
            pen = lax.rem(mine + n - s, n)
            copy(bufs[starts[tuple(group)] + s].at[k], slopes.at[(r - low) * n + pen])
        run_copies(copies)
        for t in range(tiles):
            z = slice(t * LANES, (t + 1) * LANES)
            own = slopes[slots[0] * tiles - low * n + t]
            term = cross[:, z] + speed[:, z] * own
            if with_div:
                term = term + slopes[slots[1] * tiles - low * n + t]
                third[:, z] = third[:, z] + own
            result = value[:, z] - 0.1 * term
            prov[t] = result
            h, l = two_terms(result)
            terms[t, :, :LANES] = h
            terms[t, :, LANES:] = l
        if with_div:
            divergence = pltpu.make_async_copy(third, div_ref, sems.at[0])
            divergence.start()

        row_at = lax.broadcasted_iota(jnp.int32, (rows, CHUNK), 0)
        lane_at = lax.broadcasted_iota(jnp.int32, (LANES, CHUNK), 0)
        marker_at = lax.broadcasted_iota(jnp.int32, (marker_rows, CHUNK), 0)
        one, zero = jnp.ones((), BF), jnp.zeros((), BF)

        def entry(i):
            c, t = chunk_ref[i], tile_ref[i]
            row = row_ref[c] - t * rows
            m = marker_ref[c]
            lanes = jnp.where(lane_at == lane_ref[c], 1.0, 0.0).astype(BF)
            low_part = jnp.where(lane_at == m % LANES, 1.0, 0.0).astype(BF)
            return c, jnp.minimum(t, tiles - 1), row_at == row, lanes, marker_at == m // LANES, low_part

        def gather(i, total):
            c, t, rows_hit, lanes, marker_hit, low_part = entry(i)
            both = dot(terms[t], jnp.concatenate([lanes, lanes], axis=0))
            found = jnp.sum(jnp.where(rows_hit, both, 0.0), axis=0, keepdims=True) * weight_ref[c]
            h, l = two_terms(jnp.where(marker_hit, found, 0.0))
            return total + (dot_t(h, low_part) + dot_t(l, low_part))

        sampled = lax.fori_loop(0, pairs, gather, jnp.zeros((marker_rows, LANES), F32), unroll=2)
        s_high, s_low = two_terms(sampled)

        def scatter(i, carry):
            c, t, rows_hit, lanes, marker_hit, low_part = entry(i)
            spread = dot(s_high, low_part) + dot(s_low, low_part)
            spread = jnp.sum(jnp.where(marker_hit, spread, 0.0), axis=0, keepdims=True) * weight_ref[c]
            h, l = two_terms(jnp.where(rows_hit, spread, 0.0))
            prov[t] -= dot_t(h, lanes) + dot_t(l, lanes)
            return carry

        lax.fori_loop(0, pairs, scatter, 0, unroll=2)
        fluid = 1.0 - solid_ref[...].astype(F32)
        for t in range(tiles):
            z = slice(t * LANES, (t + 1) * LANES)
            b = t * LANES // (depth // solid.shape[1])
            value[:, z] = fluid[:, b : b + 1] * prov[t]
        if with_div:
            divergence.wait()
        last = pltpu.make_async_copy(value, out_ref.at[component, 0], sems.at[1])
        last.start()
        last.wait()

    shapes = [jax.ShapeDtypeStruct((3, 1, rows, depth), F32)]
    if with_div:
        shapes.append(jax.ShapeDtypeStruct((rows, depth), F32))
    operands = [me, chunk_of, tile_of, flow, base, across, slope_z, *entries, solid, *buffers]
    specs = [SMEM] * 3 + [ANY] * 4 + [VMEM] * (len(entries) + 1) + [ANY] * total
    aliases = {}
    if out is not None:
        aliases = {len(operands): 0}
        operands.append(out)
        specs.append(ANY)
    block = pltpu.VMEM((rows, depth), F32)
    result = pl.pallas_call(
        kernel, out_shape=shapes, in_specs=specs, out_specs=[ANY] * len(shapes), input_output_aliases=aliases,
        scratch_shapes=[
            pltpu.VMEM((span * n, rows, LANES), F32), block, block, block, block,
            pltpu.VMEM((tiles, rows, LANES), F32), pltpu.VMEM((tiles, rows, 2 * LANES), BF),
            pltpu.SemaphoreType.DMA((4 + len(sources),)),
        ],
        compiler_params=params(32),
        cost_estimate=cost(pairs * 16 * rows * CHUNK * LANES, 20 * rows * depth), name="home_step",
    )(*operands)
    return result


def body(flow, marker_cells, marker_weights, solid_blocks, *, pens, grps):
    _, planes, rows, depth = flow.shape
    assert planes == 1 and depth % LANES == 0 and rows % 8 == 0
    width = depth // grps
    plan = Plan(pens, rows, depth)
    plan.marker_rows = -(-marker_weights.shape[2] // LANES // 8) * 8
    pen, grp = lax.axis_index("pen"), lax.axis_index("grp")
    pen_at, grp_at = jnp.full((1,), pen, jnp.int32), jnp.full((1,), grp, jnp.int32)
    tables = [jnp.asarray(t) for t in split_table(pens * rows)]
    tables_z = tables if depth == pens * rows else [jnp.asarray(t) for t in split_table(depth)]

    shifts = sorted(range(1, pens), key=lambda s: abs(2 * s - pens))

    def around(axis, n, s, value):
        return lax.ppermute(value, axis, [(i, (i + s) % n) for i in range(n)])

    def send_lines(blocks):
        got = {s: around("pen", pens, s, blocks[s - 1]) for s in shifts}
        return [got[s] for s in range(1, pens)]

    arrived = [send_lines(pack_lines(plan, rounds, pen_at, flow)) for rounds in plan.stages]
    fields = flow[:, 0]
    lines_x = [lax.dynamic_slice_in_dim(fields, lax.rem(grp + s, grps) * width, width, 2) for s in range(grps)]
    lines_x = [lines_x[0]] + [around("grp", grps, s, lines_x[s]) for s in range(1, grps)]
    base, slope_z = depth_terms(flow, tables_z)
    order = marker_order(marker_cells[0, 0], marker_weights[0, 0], rows, depth)
    matrix = jnp.asarray(compact_matrix(grps))
    at = lax.iota(jnp.int32, grps)
    relative = matrix[(grp + at) % grps][:, (grp - at) % grps]
    terms_x, slopes_x = slab_terms(relative, lines_x)
    across = jnp.zeros((3, rows, depth), F32)
    for s in range(grps):
        block = terms_x[s] if s == 0 else around("grp", grps, s, terms_x[s])
        across = lax.dynamic_update_slice_in_dim(across, block, lax.rem(grp + grps - s, grps) * width, 2)
    groups = []
    for number, rounds in enumerate(plan.stages):
        cut = [rounds] if number == 0 or len(rounds) == 1 else [rounds[:-1], rounds[-1:]]
        slopes = line_slopes(plan, rounds, cut, pen_at, flow, arrived[number], tables)
        for group, blocks in zip(cut, slopes):
            groups.append((group, [blocks[0]] + send_lines(blocks[1:])))

    step = functools.partial(home_step, plan, me=pen_at, flow=flow, base=base, across=across, slope_z=slope_z,
                             groups=groups, order=order, solid=solid_blocks[0])
    out, divergence = step(1, out=None)
    parts = [lax.dynamic_slice_in_dim(divergence, lax.rem(grp + s, grps) * width, width, 1) for s in range(grps)]
    parts = [parts[0]] + [around("grp", grps, s, parts[s]) for s in range(1, grps)]
    (out,) = step(0, out=out)
    poisson = solve_layout(grp_at, slopes_x, parts)
    (out,) = step(2, out=out)
    return out, poisson


def solution(mesh):
    return jax.shard_map(
        functools.partial(body, pens=mesh.shape["pen"], grps=mesh.shape["grp"]),
        mesh=mesh,
        in_specs=(
            P(None, "grp", "pen", None),
            P("grp", "pen", None, None),
            P("grp", "pen", None, None),
            P("grp", "pen", None),
        ),
        out_specs=(P(None, "grp", "pen", None), P(None, "pen", "grp")),
        check_vma=False,
    )
```

time: 1580 us -> 319 us (0.20); the launches traced: 1550 us -> 316 us
  other arithmetic: 933 us -> 10.1 us
  local copies, waits for them, and re-layouts: 325 us -> 43.7 us
  Pallas kernels: 0 us -> 108 us
  matrix products: 104 us -> 0 us
  waiting for transfers between devices: 158 us -> 94.3 us
  starting transfers between devices: 30 us -> 58.4 us
    scatter-add x4 -> x0, other arithmetic: 861 us -> none  [the longest x1 858 us: body(): jnp.zeros_like(flattened).at[:, cells_index].add(spread).reshape(shaped)]
    all_to_all x5 -> x0, waiting for transfers between devices: 158 us -> none  [the longest x1 71.3 us: body(): lax.all_to_all(flow_fields, 'pen', split_axis=3, concat_axis=2, tiled=True)]
    gather x1 -> x4, local copies, waits for them, and re-layouts: 129 us -> 1.31 us  [body(): relative = matrix[(grp + at) % grps][:, (grp - at) % grps]]
    pallas_call x0 -> x10, Pallas kernels: none -> 108 us  [the longest x3 77.9 us: home_step(): pl.pallas_call(kernel, out_shape=shapes, in_specs=specs, out_specs=[ANY]...]
    dot_general x8 -> x0, matrix products: 104 us -> none  [spectral_along(): jnp.einsum('xas,rs->xar', shifted, table_block, precision=lax.Precision.H...]
    ppermute x0 -> x44, waiting for transfers between devices: none -> 94.3 us  [around(): return lax.ppermute(value, axis, [(i, (i + s) % n) for i in range(n)])]
    ppermute x0 -> x44, starting transfers between devices: none -> 58.4 us  [around(): return lax.ppermute(value, axis, [(i, (i + s) % n) for i in range(n)])]
    slice x15 -> x1, local copies, waits for them, and re-layouts: 48 us -> 1.21 us  [marker_order(): at = jnp.where(index < end[-1], at, tiles)]
  transfers between devices with their start and end apart: 5 -> 44, of which waited for: 3 -> 9; matrix products, arithmetic and copies ran while one was open for 85% -> 6% of each run, Pallas kernels for 0% -> 34%
where the time goes in v1:
time: 319 us; the launch traced here: 316 us
  Pallas kernels  108 us (34%)
  waiting for transfers between devices  94.3 us (30%)
  starting transfers between devices  58.4 us (18%)
  local copies, waits for them, and re-layouts  43.7 us (14%)
  other arithmetic  10.1 us (3%)
    ppermute x44, waiting for transfers between devices, around(): return lax.ppermute(value, axis, [(i, (i + s) % n) for i in range(n)])  94.3 us
    pallas_call x3, Pallas kernels, home_step(): pl.pallas_call(kernel, out_shape=shapes, in_specs=specs, out_specs=[ANY]...  77.9 us
    ppermute x44, starting transfers between devices, around(): return lax.ppermute(value, axis, [(i, (i + s) % n) for i in range(n)])  58.4 us
    unnamed x88, local copies, waits for them, and re-layouts  30.4 us
    pallas_call x2, Pallas kernels, line_slopes(): pl.pallas_call(kernel, out_shape=shapes, in_specs=[SMEM, ANY, VMEM, VMEM]...  15 us
    sort x1, other arithmetic, marker_order(): key, weight = lax.sort((place * markers + marker, weight), num_keys=1)  6.9 us
    pallas_call x1, Pallas kernels, depth_terms(): pl.pallas_call(kernel, grid=(rows // step,), out_shape=[jax.ShapeDtypeStr...  6.83 us
  transfers between devices with their start and end apart: 44, of which 9 were waited for; matrix products, arithmetic and copies ran while one was open for 6% of the time, Pallas kernels for 34%

profile of v1, /device:TPU:9, one launch (start us, length us, event | category | flops | bytes accessed | tf_op | source)
XLA Modules:
  0.0 316.2 jit_solution(1668260148474750257)
XLA Ops:
  0.7 4.6 %dynamic-slice_bitcast_fusion = (f32[4,192,384]{2,1,0:T(8,128)}, f32[4,192,384]{2,1,0:T(8,128)}, f32[4,192,384]{2,1,0:T(8,128)}, f32[4,192,384]{2,1,0:T(8,128)}) fusion(f32[4,1,192,1536]{3,2,1,0:T(8,128)} %flow_ref.15, s32[]{:T(128)S(6)} %select_n.130, s32[]{:T(128)S(6)} %select_n.129, s32[]{:T(128)S(6)} %select_n.128, s32[]{:T(128)S(6)} %select_n.127), kind=kLoop, calls=%fused_computation.2 | loop fusion | bytes 9437200 | tf_op jit(solution)/shard_map/dynamic_slice | solution.py:449
  8.9 2.3 copy-done
  12.7 2.7 collective-permute-start.27
  16.8 2.3 copy-done.1
  23.9 6.9 %sort.23 = (s32[8192]{0:T(1024)S(1)}, f32[8192]{0:T(1024)}, s32[8192]{0:T(1024)}) sort(s32[8192]{0:T(1024)S(1)} %fusion.5, f32[8192]{0:T(1024)S(1)} %reshape_squeeze.4, s32[8192]{0:T(1024)S(1)} %iota.26), dimensions={0}, to_apply=%region_0.1 | sort | flops 106496 | bytes 196608 | tf_op jit(solution)/shard_map/sort | solution.py:280
  35.9 12.1 %collective-permute-done.29.rest_2_ = f32[3,192,128]{2,1,0:T(8,128)S(1)} collective-permute-done((f32[3,192,128]{2,1,0:T(8,128)S(1)}, f32[3,192,128]{2,1,0:T(8,128)S(1)}, u32[]{:S(2)}, u32[]{:S(2)}) %collective-permute-start.29) | collective-permute-done | bytes 294944 | tf_op jit(solution)/shard_map/ppermute | solution.py:441
  48.7 5.1 %collective-permute-start.31 = (f32[3,192,128]{2,1,0:T(8,128)}, f32[3,192,128]{2,1,0:T(8,128)S(1)}, u32[]{:S(2)}, u32[]{:S(2)}) collective-permute-start(f32[3,192,128]{2,1,0:T(8,128)} %get-tuple-element.88), channel_id=1, source_target_pairs={{0,5},{1,6},{2,7},{3,0},{4,1},{5,2},{6,3},{7,4},{8,13},{9,14},{10,... | collective-permute-start | bytes 884744 | tf_op jit(solution)/shard_map/ppermute | solution.py:441
  53.8 2.3 copy-done.2
  59.5 6.8 %depth_terms.1 = (f32[3,192,1536]{2,1,0:T(8,128)S(1)}, f32[192,1536]{1,0:T(8,128)S(1)}) custom-call(f32[4,1,192,1536]{3,2,1,0:T(8,128)S(1)} %copy-done.2, bf16[2,768,768]{2,1,0:T(8,128)(2,1)S(1)} %copy-done.4, bf16[2,768,768]{2,1,0:T(8,128)(2,1)S(1)} %copy-done.6), custom_call_target="tpu_custom_call" | custom-call | flops 5435817984 | bytes 14155776 | tf_op jit(solution)/shard_map/depth_terms/pallas_call | solution.py:214
  68.9 6.7 %collective-permute-done.10.rest_4_ = f32[3,192,128]{2,1,0:T(8,128)S(1)} collective-permute-done((f32[3,192,128]{2,1,0:T(8,128)S(1)}, f32[3,192,128]{2,1,0:T(8,128)S(1)}, u32[]{:S(2)}, u32[]{:S(2)}) %collective-permute-start.10) | collective-permute-done | bytes 294944 | tf_op jit(solution)/shard_map/ppermute | solution.py:441
  76.3 6.1 %collective-permute-start.12 = (f32[3,192,128]{2,1,0:T(8,128)}, f32[3,192,128]{2,1,0:T(8,128)}, u32[]{:S(2)}, u32[]{:S(2)}) collective-permute-start(f32[3,192,128]{2,1,0:T(8,128)} %get-tuple-element.67), channel_id=1, source_target_pairs={{0,7},{1,0},{2,1},{3,2},{4,3},{5,4},{6,5},{7,6},{8,15},{9,8},{10,9... | collective-permute-start | bytes 884744 | tf_op jit(solution)/shard_map/ppermute | solution.py:441
  84.9 4.5 %collective-permute-start.8 = (f32[3,192,128]{2,1,0:T(8,128)}, f32[3,192,128]{2,1,0:T(8,128)}, u32[]{:S(2)}, u32[]{:S(2)}) collective-permute-start(f32[3,192,128]{2,1,0:T(8,128)} %get-tuple-element.63), channel_id=1, source_target_pairs={{0,3},{1,4},{2,5},{3,6},{4,7},{5,0},{6,1},{7,2},{8,11},{9,12},{10,... | collective-permute-start | bytes 884744 | tf_op jit(solution)/shard_map/ppermute | solution.py:441
  92.1 4.8 %slab_terms.1 = (f32[3,192,384]{2,1,0:T(8,128)S(1)}, f32[3,192,384]{2,1,0:T(8,128)}, f32[3,192,384]{2,1,0:T(8,128)}, f32[3,192,384]{2,1,0:T(8,128)}, f32[4,192,384]{2,1,0:T(8,128)S(1)}) custom-call(f32[4,4]{1,0:T(4,128)S(1)} %bitcast.44, f32[4,192,384]{2,1,0:T(8,128)S(1)} %copy-done.10, f32[4,192,384]{2,1,0:T(8,128)} %collective-permute-done.refs_1_, ...), custom_call_target="tpu_custom_call" | custom-call | flops 18874368 | bytes 9437184 | tf_op jit(solution)/shard_map/slab_terms/pallas_call | solution.py:245
  101.3 23.2 %collective-permute-done.8.rest_2_ = f32[3,192,128]{2,1,0:T(8,128)} collective-permute-done((f32[3,192,128]{2,1,0:T(8,128)}, f32[3,192,128]{2,1,0:T(8,128)}, u32[]{:S(2)}, u32[]{:S(2)}) %collective-permute-start.8) | collective-permute-done | bytes 294944 | tf_op jit(solution)/shard_map/ppermute | solution.py:441
  124.7 4.0 %collective-permute-done.9.rest_3_ = f32[3,192,128]{2,1,0:T(8,128)} collective-permute-done((f32[3,192,128]{2,1,0:T(8,128)}, f32[3,192,128]{2,1,0:T(8,128)}, u32[]{:S(2)}, u32[]{:S(2)}) %collective-permute-start.9) | collective-permute-done | bytes 294944 | tf_op jit(solution)/shard_map/ppermute | solution.py:441
  131.7 2.3 copy-done.3
  139.3 8.8 %line_slopes.2 = (f32[2,192,128]{2,1,0:T(8,128)S(1)}, f32[2,192,128]{2,1,0:T(8,128)S(1)}, f32[2,192,128]{2,1,0:T(8,128)S(1)}, f32[2,192,128]{2,1,0:T(8,128)S(1)}...) custom-call(s32[1]{0:T(128)} %bitcast.me_ref, ...), custom_call_target="tpu_custom_call" | custom-call | flops 2717908992 | bytes 9437184 | tf_op jit(solution)/shard_map/line_slopes/pallas_call | solution.py:176
  150.1 6.2 %line_slopes.3 = (f32[3,192,128]{2,1,0:T(8,128)S(1)}, f32[3,192,128]{2,1,0:T(8,128)S(1)}, f32[3,192,128]{2,1,0:T(8,128)S(1)}, f32[3,192,128]{2,1,0:T(8,128)S(1)}...) custom-call(s32[1]{0:T(128)} %bitcast.me_ref, ...), custom_call_target="tpu_custom_call" | custom-call | flops 2717908992 | bytes 9437184 | tf_op jit(solution)/shard_map/line_slopes/pallas_call | solution.py:176
  156.3 2.0 collective-permute-start.34
  159.6 5.0 %collective-permute-done.34.rest_1_ = f32[3,192,128]{2,1,0:T(8,128)S(1)} collective-permute-done((f32[3,192,128]{2,1,0:T(8,128)S(1)}, f32[3,192,128]{2,1,0:T(8,128)S(1)}, u32[]{:S(2)}, u32[]{:S(2)}) %collective-permute-start.34) | collective-permute-done | bytes 294944 | tf_op jit(solution)/shard_map/ppermute | solution.py:441
  165.1 11.9 %collective-permute-done.35.rest_2_ = f32[3,192,128]{2,1,0:T(8,128)S(1)} collective-permute-done((f32[3,192,128]{2,1,0:T(8,128)S(1)}, f32[3,192,128]{2,1,0:T(8,128)S(1)}, u32[]{:S(2)}, u32[]{:S(2)}) %collective-permute-start.35) | collective-permute-done | bytes 294944 | tf_op jit(solution)/shard_map/ppermute | solution.py:441
  177.0 3.3 %collective-permute-start.39 = (f32[3,192,128]{2,1,0:T(8,128)S(1)}, f32[3,192,128]{2,1,0:T(8,128)S(1)}, u32[]{:S(2)}, u32[]{:S(2)}) collective-permute-start(f32[3,192,128]{2,1,0:T(8,128)S(1)} %get-tuple-element.97), channel_id=1, source_target_pairs={{0,6},{1,7},{2,0},{3,1},{4,2},{5,3},{6,4},{7,5},{8,14},{9,15},{10,... | collective-permute-start | bytes 884744 | tf_op jit(solution)/shard_map/ppermute | solution.py:441
  184.8 21.9 %collective-permute-done.36.rest_3_ = f32[3,192,128]{2,1,0:T(8,128)S(1)} collective-permute-done((f32[3,192,128]{2,1,0:T(8,128)S(1)}, f32[3,192,128]{2,1,0:T(8,128)S(1)}, u32[]{:S(2)}, u32[]{:S(2)}) %collective-permute-start.36) | collective-permute-done | bytes 294944 | tf_op jit(solution)/shard_map/ppermute | solution.py:441
  206.7 3.4 %collective-permute-start.15 = (f32[2,192,128]{2,1,0:T(8,128)S(1)}, f32[2,192,128]{2,1,0:T(8,128)S(1)}, u32[]{:S(2)}, u32[]{:S(2)}) collective-permute-start(f32[2,192,128]{2,1,0:T(8,128)S(1)} %get-tuple-element.71), channel_id=1, source_target_pairs={{0,3},{1,4},{2,5},{3,6},{4,7},{5,0},{6,1},{7,2},{8,11},{9,12},{10,... | collective-permute-start | bytes 589832 | tf_op jit(solution)/shard_map/ppermute | solution.py:441
  210.1 9.3 %collective-permute-done.37.rest_4_ = f32[3,192,128]{2,1,0:T(8,128)S(1)} collective-permute-done((f32[3,192,128]{2,1,0:T(8,128)S(1)}, f32[3,192,128]{2,1,0:T(8,128)S(1)}, u32[]{:S(2)}, u32[]{:S(2)}) %collective-permute-start.37) | collective-permute-done | bytes 294944 | tf_op jit(solution)/shard_map/ppermute | solution.py:441
  219.3 2.8 collective-permute-start.16
  224.1 27.2 %home_step.3 = (f32[3,1,192,1536]{3,2,1,0:T(8,128)}, f32[192,1536]{1,0:T(8,128)S(1)}) custom-call(s32[1]{0:T(128)} %bitcast.me_ref, s32[44]{0:T(128)S(1)} %broadcast_minimum_fusion.chunk_ref, s32[44]{0:T(128)S(1)} %compare_select_fusion.6.tile_ref, f32[4,1,192,1536]{3,2,1,0:T(8,128)S(1)} %copy-done.3, f32[3,192,1536]{2,1,0:T(8,128)S(1)} %get-tuple-element.54.base_ref, ...), custom_call_target="tpu_custom_call" | custom-call | flops 4429185024 | bytes 5898240 | tf_op jit(solution)/shard_map/home_step/pallas_call | solution.py:414
  253.2 3.3 %collective-permute-start.22 = (f32[1,192,128]{2,1,0:T(8,128)S(1)}, f32[1,192,128]{2,1,0:T(8,128)S(1)}, u32[]{:S(2)}, u32[]{:S(2)}) collective-permute-start(f32[1,192,128]{2,1,0:T(8,128)S(1)} %get-tuple-element.79), channel_id=1, source_target_pairs={{0,3},{1,4},{2,5},{3,6},{4,7},{5,0},{6,1},{7,2},{8,11},{9,12},{10,... | collective-permute-start | bytes 294920 | tf_op jit(solution)/shard_map/ppermute | solution.py:441
  258.1 25.3 %home_step.4.rest_16_ = f32[3,1,192,1536]{3,2,1,0:T(8,128)} custom-call(s32[1]{0:T(128)} %bitcast.me_ref, s32[44]{0:T(128)S(1)} %broadcast_minimum_fusion.chunk_ref, s32[44]{0:T(128)S(1)} %compare_select_fusion.6.tile_ref, f32[4,1,192,1536]{3,2,1,0:T(8,128)S(1)} %copy-done.3, ...), custom_call_target="tpu_custom_call", output_to_operand_aliasing={{}: (20, {})} | custom-call | flops 4429185024 | bytes 5898240 | tf_op jit(solution)/shard_map/home_step/pallas_call | solution.py:414
  283.4 2.1 collective-permute-start.25
  287.1 2.2 collective-permute-start.43
  289.6 25.4 %home_step.5 = f32[3,1,192,1536]{3,2,1,0:T(8,128)} custom-call(s32[1]{0:T(128)} %bitcast.me_ref, s32[44]{0:T(128)S(1)} %broadcast_minimum_fusion.chunk_ref, s32[44]{0:T(128)S(1)} %compare_select_fusion.6.tile_ref, f32[4,1,192,1536]{3,2,1,0:T(8,128)S(1)} %copy-done.3, ...), custom_call_target="tpu_custom_call", output_to_operand_aliasing={{}: (28, {})} | custom-call | flops 4429185024 | bytes 5898240 | tf_op jit(solution)/shard_map/home_step/pallas_call | solution.py:414
  (191 shorter events, 58.1 us)
Async XLA Ops:
  5.3 78.4 %collective-permute-start = (f32[4,192,384]{2,1,0:T(8,128)}, f32[4,192,384]{2,1,0:T(8,128)}, u32[]{:S(2)}, u32[]{:S(2)}) collective-permute-start(f32[4,192,384]{2,1,0:T(8,128)} %get-tuple-element.108), channel_id=1, source_target_pairs={{0,8},{8,16},{16,24},{24,0},{1,9},{9,17},{17,25},{25,1},{2,10},{10... | collective-permute-start | bytes 3538952 | tf_op jit(solution)/shard_map/ppermute | solution.py:441
  6.5 78.4 %collective-permute-start.1 = (f32[4,192,384]{2,1,0:T(8,128)}, f32[4,192,384]{2,1,0:T(8,128)}, u32[]{:S(2)}, u32[]{:S(2)}) collective-permute-start(f32[4,192,384]{2,1,0:T(8,128)} %get-tuple-element.107), channel_id=1, source_target_pairs={{0,16},{8,24},{16,0},{24,8},{1,17},{9,25},{17,1},{25,9},{2,18},{10... | collective-permute-start | bytes 3538952 | tf_op jit(solution)/shard_map/ppermute | solution.py:441
  7.8 81.7 %collective-permute-start.2 = (f32[4,192,384]{2,1,0:T(8,128)}, f32[4,192,384]{2,1,0:T(8,128)}, u32[]{:S(2)}, u32[]{:S(2)}) collective-permute-start(f32[4,192,384]{2,1,0:T(8,128)} %get-tuple-element.106), channel_id=1, source_target_pairs={{0,24},{8,0},{16,8},{24,16},{1,25},{9,1},{17,9},{25,17},{2,26},{10... | collective-permute-start | bytes 3538952 | tf_op jit(solution)/shard_map/ppermute | solution.py:441
  12.7 18.8 %collective-permute-start.27 = (f32[3,192,128]{2,1,0:T(8,128)S(1)}, f32[3,192,128]{2,1,0:T(8,128)S(1)}, u32[]{:S(2)}, u32[]{:S(2)}) collective-permute-start(f32[3,192,128]{2,1,0:T(8,128)S(1)} %get-tuple-element.84), channel_id=1, source_target_pairs={{0,1},{1,2},{2,3},{3,4},{4,5},{5,6},{6,7},{7,0},{8,9},{9,10},{10,1... | collective-permute-start | bytes 884744 | tf_op jit(solution)/shard_map/ppermute | solution.py:441
  34.5 32.8 %collective-permute-start.30 = (f32[3,192,128]{2,1,0:T(8,128)}, f32[3,192,128]{2,1,0:T(8,128)S(1)}, u32[]{:S(2)}, u32[]{:S(2)}) collective-permute-start(f32[3,192,128]{2,1,0:T(8,128)} %get-tuple-element.87), channel_id=1, source_target_pairs={{0,4},{1,5},{2,6},{3,7},{4,0},{5,1},{6,2},{7,3},{8,12},{9,13},{10,... | collective-permute-start | bytes 884744 | tf_op jit(solution)/shard_map/ppermute | solution.py:441
  48.7 19.4 %collective-permute-start.31 = (f32[3,192,128]{2,1,0:T(8,128)}, f32[3,192,128]{2,1,0:T(8,128)S(1)}, u32[]{:S(2)}, u32[]{:S(2)}) collective-permute-start(f32[3,192,128]{2,1,0:T(8,128)} %get-tuple-element.88), channel_id=1, source_target_pairs={{0,5},{1,6},{2,7},{3,0},{4,1},{5,2},{6,3},{7,4},{8,13},{9,14},{10,... | collective-permute-start | bytes 884744 | tf_op jit(solution)/shard_map/ppermute | solution.py:441
  76.3 22.5 %collective-permute-start.12 = (f32[3,192,128]{2,1,0:T(8,128)}, f32[3,192,128]{2,1,0:T(8,128)}, u32[]{:S(2)}, u32[]{:S(2)}) collective-permute-start(f32[3,192,128]{2,1,0:T(8,128)} %get-tuple-element.67), channel_id=1, source_target_pairs={{0,7},{1,0},{2,1},{3,2},{4,3},{5,4},{6,5},{7,6},{8,15},{9,8},{10,9... | collective-permute-start | bytes 884744 | tf_op jit(solution)/shard_map/ppermute | solution.py:441
  84.9 39.6 %collective-permute-start.8 = (f32[3,192,128]{2,1,0:T(8,128)}, f32[3,192,128]{2,1,0:T(8,128)}, u32[]{:S(2)}, u32[]{:S(2)}) collective-permute-start(f32[3,192,128]{2,1,0:T(8,128)} %get-tuple-element.63), channel_id=1, source_target_pairs={{0,3},{1,4},{2,5},{3,6},{4,7},{5,0},{6,1},{7,2},{8,11},{9,12},{10,... | collective-permute-start | bytes 884744 | tf_op jit(solution)/shard_map/ppermute | solution.py:441
  89.5 39.2 %collective-permute-start.9 = (f32[3,192,128]{2,1,0:T(8,128)}, f32[3,192,128]{2,1,0:T(8,128)}, u32[]{:S(2)}, u32[]{:S(2)}) collective-permute-start(f32[3,192,128]{2,1,0:T(8,128)} %get-tuple-element.64), channel_id=1, source_target_pairs={{0,4},{1,5},{2,6},{3,7},{4,0},{5,1},{6,2},{7,3},{8,12},{9,13},{10,... | collective-permute-start | bytes 884744 | tf_op jit(solution)/shard_map/ppermute | solution.py:441
  98.8 49.3 %collective-permute-start.32 = (f32[3,192,128]{2,1,0:T(8,128)}, f32[3,192,128]{2,1,0:T(8,128)}, u32[]{:S(2)}, u32[]{:S(2)}) collective-permute-start(f32[3,192,128]{2,1,0:T(8,128)} %get-tuple-element.89), channel_id=1, source_target_pairs={{0,6},{1,7},{2,0},{3,1},{4,2},{5,3},{6,4},{7,5},{8,14},{9,15},{10,... | collective-permute-start | bytes 884744 | tf_op jit(solution)/shard_map/ppermute | solution.py:441
  100.1 48.2 %collective-permute-start.33 = (f32[3,192,128]{2,1,0:T(8,128)}, f32[3,192,128]{2,1,0:T(8,128)}, u32[]{:S(2)}, u32[]{:S(2)}) collective-permute-start(f32[3,192,128]{2,1,0:T(8,128)} %get-tuple-element.90), channel_id=1, source_target_pairs={{0,7},{1,0},{2,1},{3,2},{4,3},{5,4},{6,5},{7,6},{8,15},{9,8},{10,9... | collective-permute-start | bytes 884744 | tf_op jit(solution)/shard_map/ppermute | solution.py:441
  101.0 76.0 %collective-permute-start.3 = (f32[3,192,384]{2,1,0:T(8,128)}, f32[3,192,384]{2,1,0:T(8,128)}, u32[]{:S(2)}, u32[]{:S(2)}) collective-permute-start(f32[3,192,384]{2,1,0:T(8,128)} %get-tuple-element.56), channel_id=1, source_target_pairs={{0,8},{8,16},{16,24},{24,0},{1,9},{9,17},{17,25},{25,1},{2,10},{10... | collective-permute-start | bytes 2654216 | tf_op jit(solution)/shard_map/ppermute | solution.py:441
  124.5 52.5 %collective-permute-start.4 = (f32[3,192,384]{2,1,0:T(8,128)}, f32[3,192,384]{2,1,0:T(8,128)}, u32[]{:S(2)}, u32[]{:S(2)}) collective-permute-start(f32[3,192,384]{2,1,0:T(8,128)} %get-tuple-element.57), channel_id=1, source_target_pairs={{0,16},{8,24},{16,0},{24,8},{1,17},{9,25},{17,1},{25,9},{2,18},{10... | collective-permute-start | bytes 2654216 | tf_op jit(solution)/shard_map/ppermute | solution.py:441
  128.7 51.6 %collective-permute-start.5 = (f32[3,192,384]{2,1,0:T(8,128)}, f32[3,192,384]{2,1,0:T(8,128)}, u32[]{:S(2)}, u32[]{:S(2)}) collective-permute-start(f32[3,192,384]{2,1,0:T(8,128)} %get-tuple-element.58), channel_id=1, source_target_pairs={{0,24},{8,0},{16,8},{24,16},{1,25},{9,1},{17,9},{25,17},{2,26},{10... | collective-permute-start | bytes 2654216 | tf_op jit(solution)/shard_map/ppermute | solution.py:441
  164.5 42.2 %collective-permute-start.36 = (f32[3,192,128]{2,1,0:T(8,128)S(1)}, f32[3,192,128]{2,1,0:T(8,128)S(1)}, u32[]{:S(2)}, u32[]{:S(2)}) collective-permute-start(f32[3,192,128]{2,1,0:T(8,128)S(1)} %get-tuple-element.94), channel_id=1, source_target_pairs={{0,3},{1,4},{2,5},{3,6},{4,7},{5,0},{6,1},{7,2},{8,11},{9,12},{10,... | collective-permute-start | bytes 884744 | tf_op jit(solution)/shard_map/ppermute | solution.py:441
  177.0 42.3 %collective-permute-start.37 = (f32[3,192,128]{2,1,0:T(8,128)S(1)}, f32[3,192,128]{2,1,0:T(8,128)S(1)}, u32[]{:S(2)}, u32[]{:S(2)}) collective-permute-start(f32[3,192,128]{2,1,0:T(8,128)S(1)} %get-tuple-element.95), channel_id=1, source_target_pairs={{0,4},{1,5},{2,6},{3,7},{4,0},{5,1},{6,2},{7,3},{8,12},{9,13},{10,... | collective-permute-start | bytes 884744 | tf_op jit(solution)/shard_map/ppermute | solution.py:441
  177.0 45.1 %collective-permute-start.38 = (f32[3,192,128]{2,1,0:T(8,128)S(1)}, f32[3,192,128]{2,1,0:T(8,128)S(1)}, u32[]{:S(2)}, u32[]{:S(2)}) collective-permute-start(f32[3,192,128]{2,1,0:T(8,128)S(1)} %get-tuple-element.96), channel_id=1, source_target_pairs={{0,5},{1,6},{2,7},{3,0},{4,1},{5,2},{6,3},{7,4},{8,13},{9,14},{10,... | collective-permute-start | bytes 884744 | tf_op jit(solution)/shard_map/ppermute | solution.py:441
  177.0 45.1 %collective-permute-start.39 = (f32[3,192,128]{2,1,0:T(8,128)S(1)}, f32[3,192,128]{2,1,0:T(8,128)S(1)}, u32[]{:S(2)}, u32[]{:S(2)}) collective-permute-start(f32[3,192,128]{2,1,0:T(8,128)S(1)} %get-tuple-element.97), channel_id=1, source_target_pairs={{0,6},{1,7},{2,0},{3,1},{4,2},{5,3},{6,4},{7,5},{8,14},{9,15},{10,... | collective-permute-start | bytes 884744 | tf_op jit(solution)/shard_map/ppermute | solution.py:441
  180.3 41.9 %collective-permute-start.40 = (f32[3,192,128]{2,1,0:T(8,128)S(1)}, f32[3,192,128]{2,1,0:T(8,128)S(1)}, u32[]{:S(2)}, u32[]{:S(2)}) collective-permute-start(f32[3,192,128]{2,1,0:T(8,128)S(1)} %get-tuple-element.98), channel_id=1, source_target_pairs={{0,7},{1,0},{2,1},{3,2},{4,3},{5,4},{6,5},{7,6},{8,15},{9,8},{10,9... | collective-permute-start | bytes 884744 | tf_op jit(solution)/shard_map/ppermute | solution.py:441
  206.7 44.7 %collective-permute-start.15 = (f32[2,192,128]{2,1,0:T(8,128)S(1)}, f32[2,192,128]{2,1,0:T(8,128)S(1)}, u32[]{:S(2)}, u32[]{:S(2)}) collective-permute-start(f32[2,192,128]{2,1,0:T(8,128)S(1)} %get-tuple-element.71), channel_id=1, source_target_pairs={{0,3},{1,4},{2,5},{3,6},{4,7},{5,0},{6,1},{7,2},{8,11},{9,12},{10,... | collective-permute-start | bytes 589832 | tf_op jit(solution)/shard_map/ppermute | solution.py:441
  219.3 33.7 %collective-permute-start.16 = (f32[2,192,128]{2,1,0:T(8,128)S(1)}, f32[2,192,128]{2,1,0:T(8,128)S(1)}, u32[]{:S(2)}, u32[]{:S(2)}) collective-permute-start(f32[2,192,128]{2,1,0:T(8,128)S(1)} %get-tuple-element.72), channel_id=1, source_target_pairs={{0,4},{1,5},{2,6},{3,7},{4,0},{5,1},{6,2},{7,3},{8,12},{9,13},{10,... | collective-permute-start | bytes 589832 | tf_op jit(solution)/shard_map/ppermute | solution.py:441
  222.1 31.1 %collective-permute-start.17 = (f32[2,192,128]{2,1,0:T(8,128)S(1)}, f32[2,192,128]{2,1,0:T(8,128)S(1)}, u32[]{:S(2)}, u32[]{:S(2)}) collective-permute-start(f32[2,192,128]{2,1,0:T(8,128)S(1)} %get-tuple-element.73), channel_id=1, source_target_pairs={{0,5},{1,6},{2,7},{3,0},{4,1},{5,2},{6,3},{7,4},{8,13},{9,14},{10,... | collective-permute-start | bytes 589832 | tf_op jit(solution)/shard_map/ppermute | solution.py:441
  222.2 34.3 %collective-permute-start.18 = (f32[2,192,128]{2,1,0:T(8,128)S(1)}, f32[2,192,128]{2,1,0:T(8,128)S(1)}, u32[]{:S(2)}, u32[]{:S(2)}) collective-permute-start(f32[2,192,128]{2,1,0:T(8,128)S(1)} %get-tuple-element.74), channel_id=1, source_target_pairs={{0,6},{1,7},{2,0},{3,1},{4,2},{5,3},{6,4},{7,5},{8,14},{9,15},{10,... | collective-permute-start | bytes 589832 | tf_op jit(solution)/shard_map/ppermute | solution.py:441
  222.2 34.3 %collective-permute-start.19 = (f32[2,192,128]{2,1,0:T(8,128)S(1)}, f32[2,192,128]{2,1,0:T(8,128)S(1)}, u32[]{:S(2)}, u32[]{:S(2)}) collective-permute-start(f32[2,192,128]{2,1,0:T(8,128)S(1)} %get-tuple-element.75), channel_id=1, source_target_pairs={{0,7},{1,0},{2,1},{3,2},{4,3},{5,4},{6,5},{7,6},{8,15},{9,8},{10,9... | collective-permute-start | bytes 589832 | tf_op jit(solution)/shard_map/ppermute | solution.py:441
  251.4 32.0 %collective-permute-start.20 = (f32[1,192,128]{2,1,0:T(8,128)S(1)}, f32[1,192,128]{2,1,0:T(8,128)S(1)}, u32[]{:S(2)}, u32[]{:S(2)}) collective-permute-start(f32[1,192,128]{2,1,0:T(8,128)S(1)} %get-tuple-element.77), channel_id=1, source_target_pairs={{0,1},{1,2},{2,3},{3,4},{4,5},{5,6},{6,7},{7,0},{8,9},{9,10},{10,1... | collective-permute-start | bytes 294920 | tf_op jit(solution)/shard_map/ppermute | solution.py:441
  253.1 32.4 %collective-permute-start.21 = (f32[1,192,128]{2,1,0:T(8,128)S(1)}, f32[1,192,128]{2,1,0:T(8,128)S(1)}, u32[]{:S(2)}, u32[]{:S(2)}) collective-permute-start(f32[1,192,128]{2,1,0:T(8,128)S(1)} %get-tuple-element.78), channel_id=1, source_target_pairs={{0,2},{1,3},{2,4},{3,5},{4,6},{5,7},{6,0},{7,1},{8,10},{9,11},{10,... | collective-permute-start | bytes 294920 | tf_op jit(solution)/shard_map/ppermute | solution.py:441
  253.2 32.4 %collective-permute-start.22 = (f32[1,192,128]{2,1,0:T(8,128)S(1)}, f32[1,192,128]{2,1,0:T(8,128)S(1)}, u32[]{:S(2)}, u32[]{:S(2)}) collective-permute-start(f32[1,192,128]{2,1,0:T(8,128)S(1)} %get-tuple-element.79), channel_id=1, source_target_pairs={{0,3},{1,4},{2,5},{3,6},{4,7},{5,0},{6,1},{7,2},{8,11},{9,12},{10,... | collective-permute-start | bytes 294920 | tf_op jit(solution)/shard_map/ppermute | solution.py:441
  256.5 30.4 %collective-permute-start.23 = (f32[1,192,128]{2,1,0:T(8,128)S(1)}, f32[1,192,128]{2,1,0:T(8,128)S(1)}, u32[]{:S(2)}, u32[]{:S(2)}) collective-permute-start(f32[1,192,128]{2,1,0:T(8,128)S(1)} %get-tuple-element.80), channel_id=1, source_target_pairs={{0,4},{1,5},{2,6},{3,7},{4,0},{5,1},{6,2},{7,3},{8,12},{9,13},{10,... | collective-permute-start | bytes 294920 | tf_op jit(solution)/shard_map/ppermute | solution.py:441
  256.5 30.6 %collective-permute-start.24 = (f32[1,192,128]{2,1,0:T(8,128)S(1)}, f32[1,192,128]{2,1,0:T(8,128)S(1)}, u32[]{:S(2)}, u32[]{:S(2)}) collective-permute-start(f32[1,192,128]{2,1,0:T(8,128)S(1)} %get-tuple-element.81), channel_id=1, source_target_pairs={{0,5},{1,6},{2,7},{3,0},{4,1},{5,2},{6,3},{7,4},{8,13},{9,14},{10,... | collective-permute-start | bytes 294920 | tf_op jit(solution)/shard_map/ppermute | solution.py:441
  285.6 29.3 %collective-permute-start.41 = (f32[192,384]{1,0:T(8,128)S(1)}, f32[192,384]{1,0:T(8,128)S(1)}, u32[]{:S(2)}, u32[]{:S(2)}) collective-permute-start(f32[192,384]{1,0:T(8,128)S(1)} %get-tuple-element.112), channel_id=1, source_target_pairs={{0,8},{8,16},{16,24},{24,0},{1,9},{9,17},{17,25},{25,1},{2,10},{10... | collective-permute-start | bytes 884744 | tf_op jit(solution)/shard_map/ppermute | solution.py:441
  286.9 28.1 %collective-permute-start.42 = (f32[192,384]{1,0:T(8,128)S(1)}, f32[192,384]{1,0:T(8,128)S(1)}, u32[]{:S(2)}, u32[]{:S(2)}) collective-permute-start(f32[192,384]{1,0:T(8,128)S(1)} %get-tuple-element.111), channel_id=1, source_target_pairs={{0,16},{8,24},{16,0},{24,8},{1,17},{9,25},{17,1},{25,9},{2,18},{10... | collective-permute-start | bytes 884744 | tf_op jit(solution)/shard_map/ppermute | solution.py:441
  287.1 27.9 %collective-permute-start.43 = (f32[192,384]{1,0:T(8,128)S(1)}, f32[192,384]{1,0:T(8,128)S(1)}, u32[]{:S(2)}, u32[]{:S(2)}) collective-permute-start(f32[192,384]{1,0:T(8,128)S(1)} %get-tuple-element.110), channel_id=1, source_target_pairs={{0,24},{8,0},{16,8},{24,16},{1,25},{9,1},{17,9},{25,17},{2,26},{10... | collective-permute-start | bytes 884744 | tf_op jit(solution)/shard_map/ppermute | solution.py:441
  (55 other events, 745.4 us)

commit v2 on v1

v2 whole, which is shorter than its diff:
```python
import functools
import math

import jax
import jax.numpy as jnp
import ml_dtypes
import numpy as np
from jax import lax
from jax.experimental import pallas as pl
from jax.experimental.pallas import tpu as pltpu
from jax.sharding import PartitionSpec as P

LANES = 128
CHUNK = 256
CORES = 2
UNROLL = 11
FIELD_ORDER = (1, 3, 0, 2)
ANY = pl.BlockSpec(memory_space=pl.ANY)
HBM = pl.BlockSpec(memory_space=pltpu.HBM)
SMEM = pl.BlockSpec(memory_space=pltpu.SMEM)
VMEM = pl.BlockSpec(memory_space=pltpu.VMEM)
BF = jnp.bfloat16
F32 = jnp.float32


def split_table(length):
    half = length // 2
    lag = np.arange(length)
    row = np.zeros(length)
    row[1:] = math.pi / length * (1 - 2 * (lag[1:] % 2)) / np.tan(math.pi * lag[1:] / length)
    row[half] = 0.0
    offset = np.arange(half)[:, None] - np.arange(half)[None, :]
    same, other = row[offset % length], row[(offset + half) % length]
    table = np.stack([(same + other) / 2, (same - other) / 2])
    high = table.astype(ml_dtypes.bfloat16)
    low = (table - high.astype(np.float64)).astype(ml_dtypes.bfloat16)
    return high, low


def compact_matrix(length):
    eye = np.eye(length)
    off = lambda k: np.eye(length, k=k)
    left = eye + (off(1) + off(-1)) / 3
    right = 7 / 9 * (off(1) - off(-1)) + 1 / 36 * (off(2) - off(-2))
    return np.linalg.solve(left, right).astype(np.float32)


def two_terms(value):
    high = value.astype(BF)
    return high, (value - high.astype(F32)).astype(BF)


def dot(a, b):
    return jnp.dot(a, b, preferred_element_type=F32)


def dot_t(a, b):
    return lax.dot_general(a, b, (((1,), (1,)), ((), ())), preferred_element_type=F32)


def params():
    return pltpu.CompilerParams(vmem_limit_bytes=60 * 2**20)


def cost(flops, moved):
    return pl.CostEstimate(flops=int(flops) // 100, bytes_accessed=int(moved) // 100, transcendentals=0)


class Plan:
    def __init__(self, pens, rows, depth):
        self.pens, self.chips, self.rows, self.depth = pens, pens // CORES, rows, depth
        self.tiles = depth // LANES
        self.pairs = len(FIELD_ORDER) * self.tiles
        self.rounds = -(-self.pairs // self.chips)
        first = min(-(-2 * self.tiles // self.chips), self.rounds)
        self.stages = [list(range(first))]
        if first < self.rounds:
            self.stages.append(list(range(first, self.rounds)))

    def place(self, round_, chip):
        pair = jnp.minimum(round_ * self.chips + chip, self.pairs - 1)
        slot, tile = pair // self.tiles, pair % self.tiles
        field = jnp.int32(FIELD_ORDER[0])
        for i, f in enumerate(FIELD_ORDER[1:], 1):
            field = jnp.where(slot == i, f, field)
        return field, pl.multiple_of(tile * LANES, LANES)


def run_copies(copies):
    for c in copies:
        c.start()
    for c in copies:
        c.wait()


def pack_lines(plan, me, flow):
    n, stages = plan.chips, plan.stages
    fields, _, rows, depth = flow.shape

    def kernel(me_ref, flow_ref, *rest):
        outs, (held, in_sems, out_sems) = rest[:-3], rest[-3:]
        loads = [pltpu.make_async_copy(flow_ref.at[f, 0], held.at[f], in_sems.at[f]) for f in FIELD_ORDER]
        for c in loads:
            c.start()
        copies = []
        for i, rounds in enumerate(stages):
            last = min((rounds[-1] * n + n - 1) // plan.tiles, fields - 1)
            while len(loads) > fields - 1 - last:
                loads.pop(0).wait()
            for s in range(n):
                chip = lax.rem(me_ref[0] // CORES + s, n)
                for k, r in enumerate(rounds):
                    field, z = plan.place(r, chip)
                    c = pltpu.make_async_copy(held.at[field, :, pl.ds(z, LANES)], outs[i * n + s].at[k], out_sems.at[len(copies)])
                    c.start()
                    copies.append(c)
        for c in copies:
            c.wait()

    shapes = [jax.ShapeDtypeStruct((len(rounds), rows, LANES), F32) for rounds in stages for _ in range(n)]
    out = pl.pallas_call(
        kernel, out_shape=shapes, in_specs=[SMEM, HBM], out_specs=[HBM] * len(shapes),
        scratch_shapes=[pltpu.VMEM((fields, rows, depth), F32), pltpu.SemaphoreType.DMA((fields,)),
                        pltpu.SemaphoreType.DMA((n * plan.rounds,))],
        compiler_params=params(), cost_estimate=cost(0, 2 * flow.size), name="pack_lines",
    )(me, flow)
    return [out[i * n : (i + 1) * n] for i in range(len(stages))]


def line_slopes(plan, rounds, groups, me, received, other, tables):
    n, rows = plan.chips, plan.rows
    length, half, count = plan.pens * rows, plan.pens * rows // 2, len(rounds)
    wide = count * LANES
    block = math.gcd(half, 256)

    def kernel(me_ref, high_ref, low_ref, *rest):
        ins, others = rest[:n], rest[n : 2 * n]
        outs = rest[2 * n : 2 * n + n * len(groups)]
        lines, result, x_high, x_low, in_sems, out_sems = rest[2 * n + n * len(groups) :]
        chip, core = me_ref[0] // CORES, me_ref[0] % CORES
        copies = []
        for refs, c in ((ins, core), (others, 1 - core)):
            for s in range(n):
                pen = lax.rem(chip + n - s, n) * CORES + c
                at = pl.ds(pl.multiple_of(pen * rows, 8), rows)
                copies.append(pltpu.make_async_copy(refs[s], lines.at[:, at, :], in_sems.at[len(copies)]))
        run_copies(copies)

        @pl.loop(0, half // block)
        def _(b):
            upper = pl.ds(pl.multiple_of(b * block, block), block)
            lower = pl.ds(pl.multiple_of(b * block + half, block), block)
            for k in range(count):
                to = pl.ds(k * LANES, LANES)
                first, second = lines[k, upper, :], lines[k, lower, :]
                for part, value in enumerate((first + second, first - second)):
                    h, l = two_terms(value)
                    x_high[part, upper, to] = h
                    x_low[part, upper, to] = l

        for home in range(n // 2):
            at = pl.ds(pl.multiple_of((home * CORES + core) * rows, 16), rows)
            parts = []
            for part in range(2):
                t_high, t_low = high_ref[part, at, :], low_ref[part, at, :]
                h, l = x_high[part], x_low[part]
                parts.append(dot(t_high, h) + (dot(t_high, l) + dot(t_low, h)))
            top, bottom = parts[0] + parts[1], parts[0] - parts[1]
            for k in range(count):
                result[home, k] = top[:, k * LANES : (k + 1) * LANES]
                result[home + n // 2, k] = bottom[:, k * LANES : (k + 1) * LANES]

        copies = []
        for g, group in enumerate(groups):
            at_k = pl.ds(rounds.index(group[0]), len(group))
            for s in range(n):
                home = lax.rem(chip + s, n)
                copies.append(pltpu.make_async_copy(result.at[home, at_k], outs[g * n + s], out_sems.at[len(copies)]))
        run_copies(copies)

    shapes = [jax.ShapeDtypeStruct((len(g), rows, LANES), F32) for g in groups for _ in range(n)]
    out = pl.pallas_call(
        kernel, out_shape=shapes,
        in_specs=[SMEM, VMEM, VMEM] + [HBM] * (2 * n), out_specs=[ANY] * len(shapes),
        scratch_shapes=[
            pltpu.VMEM((count, length, LANES), F32), pltpu.VMEM((n, count, rows, LANES), F32),
            pltpu.VMEM((2, half, wide), BF), pltpu.VMEM((2, half, wide), BF),
            pltpu.SemaphoreType.DMA((2 * n,)), pltpu.SemaphoreType.DMA((len(shapes),)),
        ],
        compiler_params=params(),
        cost_estimate=cost(6 * half * half * wide, 6 * count * length * LANES + 8 * half * half),
        name="line_slopes",
    )(me, *tables, *received, *other)
    return [out[g * n : (g + 1) * n] for g in range(len(groups))]


def depth_terms(flow, tables):
    fields, _, rows, depth = flow.shape
    half = depth // 2
    step = math.gcd(rows, 48)

    def kernel(flow_ref, high_ref, low_ref, base_ref, slope_ref):
        value = flow_ref[:, 0].reshape(fields * step, depth)
        parts = []
        for part, x in enumerate((value[:, :half] + value[:, half:], value[:, :half] - value[:, half:])):
            h, l = two_terms(x)
            parts.append(dot(h, high_ref[part]) + (dot(l, high_ref[part]) + dot(h, low_ref[part])))
        minus = jnp.concatenate([parts[0] + parts[1], parts[0] - parts[1]], axis=1)
        rows_of = lambda f: minus[f * step : (f + 1) * step]
        speed = flow_ref[2, 0]
        for i in range(3):
            term = speed * rows_of(i)
            if i == 2:
                term = term + rows_of(3)
                slope_ref[...] = -rows_of(2)
            base_ref[i] = flow_ref[i, 0] + 0.1 * term

    whole = pl.BlockSpec((2, half, half), lambda r: (0, 0, 0), pipeline_mode=pl.Buffered(1))
    size = 4 * fields * rows * depth
    return pl.pallas_call(
        kernel, grid=(rows // step,),
        out_shape=[jax.ShapeDtypeStruct((3, rows, depth), F32), jax.ShapeDtypeStruct((rows, depth), F32)],
        in_specs=[pl.BlockSpec((fields, 1, step, depth), lambda r: (0, 0, r, 0)), whole, whole],
        out_specs=[pl.BlockSpec((3, step, depth), lambda r: (0, r, 0)), pl.BlockSpec((step, depth), lambda r: (r, 0))],
        compiler_params=params(), cost_estimate=cost(12 * fields * rows * half * half, 2 * size + 8 * half * half),
        name="depth_terms",
    )(flow, *tables)


def slab_terms(coefficients, planes):
    n, fields, rows, width = planes.shape
    step = math.gcd(rows, 48)

    def kernel(in_ref, out_ref, slope_ref):
        for i in range(n):
            for f in range(fields):
                slope = sum(float(coefficients[i, j]) * in_ref[j, f] for j in range(n))
                if f == 0:
                    slope_ref[i] = slope
                if f < 3:
                    out_ref[i, f] = in_ref[i, 0] * slope
                else:
                    out_ref[i, 0] += slope

    size = 4 * n * fields * rows * width
    block = lambda *lead: pl.BlockSpec((*lead, step, width), lambda r: (0,) * len(lead) + (r, 0))
    return pl.pallas_call(
        kernel, grid=(rows // step,),
        out_shape=[jax.ShapeDtypeStruct((n, 3, rows, width), F32), jax.ShapeDtypeStruct((n, rows, width), F32)],
        in_specs=[block(n, fields)], out_specs=[block(n, 3), block(n)],
        compiler_params=params(), cost_estimate=cost(n * size, 2 * size), name="slab_terms",
    )(planes)


def marker_order(cells, weights, rows, depth):
    markers, stencil = weights.shape
    tiles, entries = depth // LANES, markers * stencil
    chunks = entries // CHUNK
    marker = lax.iota(jnp.int32, entries) // stencil
    flat = cells.reshape(-1)
    row, z = flat // depth, flat % depth
    place = (z // LANES * rows + row) * LANES + z % LANES
    weight = weights.reshape(-1)
    if rows * depth * markers < 2**31:
        key, weight = lax.sort((place * markers + marker, weight), num_keys=1)
        place, marker = key // markers, key % markers
    else:
        place, marker, weight = lax.sort((place, marker, weight), num_keys=1)
    shape = (chunks, 1, CHUNK)
    tile_row, lane = place // LANES, place % LANES
    tile = (tile_row // rows).reshape(chunks, CHUNK)
    first, last = tile[:, 0], tile[:, -1]
    end = jnp.cumsum(last - first + 1)
    start = end - (last - first + 1)
    pairs = chunks + tiles
    index = lax.iota(jnp.int32, pairs)
    chunk = jnp.minimum(jnp.sum((end[None, :] <= index[:, None]).astype(jnp.int32), axis=1), chunks - 1)
    pick = chunk[:, None] == lax.iota(jnp.int32, chunks)[None, :]
    at = jnp.sum(jnp.where(pick, (first - start)[None, :], 0), axis=1) + index
    at = jnp.where(index < end[-1], at, tiles)
    return chunk, at, tile_row.reshape(shape), lane.reshape(shape), marker.reshape(shape), weight.reshape(shape)


def home_slopes(plan, slot, groups):
    n, tiles = plan.chips, plan.tiles
    low, high = slot * tiles // n, ((slot + 1) * tiles - 1) // n
    wanted, buffers = [], []
    for group, blocks in groups:
        if any(low <= r <= high for r in group):
            wanted += [(len(buffers) + s, k, r, s) for k, r in enumerate(group) if low <= r <= high for s in range(n)]
            buffers += blocks

    def copies(me, refs, slopes, sems, first):
        return [pltpu.make_async_copy(
            refs[b].at[k], slopes.at[(r - low) * n + lax.rem(me // CORES + n - s, n)], sems.at[first + i])
            for i, (b, k, r, s) in enumerate(wanted)]

    return buffers, (high - low + 1) * n, len(wanted), slot * tiles - low * n, copies


def home_divergence(plan, parts, me, slope_z, groups):
    rows, depth, tiles = plan.rows, plan.depth, plan.tiles
    buffers, span, count, skip, copies_of = home_slopes(plan, FIELD_ORDER.index(1), groups)

    def kernel(me_ref, slope_ref, *rest):
        refs, (out_ref, slopes, third, sems) = rest[: len(buffers)], rest[len(buffers) :]
        copies = copies_of(me_ref[0], refs, slopes, sems, 1)
        run_copies([pltpu.make_async_copy(slope_ref, third, sems.at[0])] + copies)
        for t in range(tiles):
            z = slice(t * LANES, (t + 1) * LANES)
            third[:, z] = third[:, z] + slopes[skip + t]
        width = depth // parts
        for g in range(parts):
            out_ref[g] = third[:, g * width : (g + 1) * width]

    return pl.pallas_call(
        kernel, out_shape=jax.ShapeDtypeStruct((parts, rows, depth // parts), F32),
        in_specs=[SMEM] + [HBM] * (1 + len(buffers)), out_specs=VMEM,
        scratch_shapes=[pltpu.VMEM((span, rows, LANES), F32), pltpu.VMEM((rows, depth), F32),
                        pltpu.SemaphoreType.DMA((1 + count,))],
        compiler_params=params(), cost_estimate=cost(0, 12 * rows * depth), name="home_divergence",
    )(me, slope_z, *buffers)


def home_step(plan, component, me, flow, base, across, groups, order, solid, out):
    rows, depth, tiles = plan.rows, plan.depth, plan.tiles
    wanted = (1, 3) if component == 1 else (component,)
    sources = [home_slopes(plan, FIELD_ORDER.index(f), groups) for f in wanted]
    buffers = [b for source in sources for b in source[0]]
    total = len(buffers)
    chunk_of, tile_of, *entries = order
    pairs = chunk_of.shape[0]
    chunks = entries[0].shape[0]
    marker_rows = plan.marker_rows

    def kernel(me_ref, chunk_ref, tile_ref, flow_ref, base_ref, across_ref, row_ref, lane_ref, marker_ref,
               weight_ref, solid_ref, *rest):
        bufs = rest[:total]
        rest = rest[total:]
        if out is not None:
            rest = rest[1:]
        out_ref, speed, value, cross, prov, terms, sems, *slopes = rest
        copies = [
            pltpu.make_async_copy(flow_ref.at[1, 0], speed, sems.at[0]),
            pltpu.make_async_copy(base_ref.at[component], value, sems.at[1]),
            pltpu.make_async_copy(across_ref.at[component], cross, sems.at[2]),
        ]
        used = 0
        for (held, _, count, _, copies_of), ref in zip(sources, slopes):
            copies += copies_of(me_ref[0], bufs[used : used + len(held)], ref, sems, len(copies))
            used += len(held)
        run_copies(copies)
        for t in range(tiles):
            z = slice(t * LANES, (t + 1) * LANES)
            term = cross[:, z] + speed[:, z] * slopes[0][sources[0][3] + t]
            if component == 1:
                term = term + slopes[1][sources[1][3] + t]
            result = value[:, z] - 0.1 * term
            prov[t] = result
            h, l = two_terms(result)
            terms[t, :, :LANES] = h
            terms[t, :, LANES:] = l

        row_at = lax.broadcasted_iota(jnp.int32, (rows, CHUNK), 0)
        lane_at = lax.broadcasted_iota(jnp.int32, (LANES, CHUNK), 0)
        marker_at = lax.broadcasted_iota(jnp.int32, (marker_rows, CHUNK), 0)
        one, zero = jnp.ones((), BF), jnp.zeros((), BF)

        def entry(i):
            c, t = chunk_ref[i], tile_ref[i]
            m = marker_ref[c]
            low_part = jnp.where(lane_at == m % LANES, 1.0, 0.0).astype(BF)
            return c, jnp.minimum(t, tiles - 1), row_at == row_ref[c] - t * rows, lane_at == lane_ref[c], marker_at == m // LANES, low_part

        def gather(i, total):
            c, t, rows_hit, lanes_hit, marker_hit, low_part = entry(i)
            lanes = jnp.where(lanes_hit, 1.0, 0.0).astype(BF)
            both = dot(terms[t], jnp.concatenate([lanes, lanes], axis=0))
            found = jnp.sum(jnp.where(rows_hit, both, 0.0), axis=0, keepdims=True) * weight_ref[c]
            h, l = two_terms(jnp.where(marker_hit, found, 0.0))
            return total + dot_t(jnp.concatenate([h, l], axis=0), low_part)

        sampled = lax.fori_loop(0, pairs, gather, jnp.zeros((2 * marker_rows, LANES), F32), unroll=UNROLL)
        sampled = jnp.concatenate(two_terms(sampled[:marker_rows] + sampled[marker_rows:]), axis=0)

        def scatter(i, carry):
            c, t, rows_hit, lanes_hit, marker_hit, low_part = entry(i)
            spread = dot(sampled, low_part)
            spread = spread[:marker_rows] + spread[marker_rows:]
            spread = jnp.sum(jnp.where(marker_hit, spread, 0.0), axis=0, keepdims=True) * weight_ref[c]
            h, l = two_terms(spread)
            value = [jnp.where(lanes_hit, x.astype(F32), 0.0).astype(BF) for x in (h, l)]
            both = dot_t(jnp.where(rows_hit, 1.0, 0.0).astype(BF), jnp.concatenate(value, axis=0))
            prov[t] -= both[:, :LANES] + both[:, LANES:]
            return carry

        lax.fori_loop(0, pairs, scatter, 0, unroll=UNROLL)
        fluid = 1.0 - solid_ref[...].astype(F32)
        for t in range(tiles):
            z = slice(t * LANES, (t + 1) * LANES)
            b = t * LANES // (depth // solid.shape[1])
            value[:, z] = fluid[:, b : b + 1] * prov[t]
        last = pltpu.make_async_copy(value, out_ref.at[component, 0], sems.at[0])
        last.start()
        last.wait()

    operands = [me, chunk_of, tile_of, flow, base, across, *entries, solid, *buffers]
    specs = [SMEM] * 3 + [HBM] * 3 + [VMEM] * (len(entries) + 1) + [HBM] * total
    aliases = {}
    if out is not None:
        aliases = {len(operands): 0}
        operands.append(out)
        specs.append(HBM)
    block = pltpu.VMEM((rows, depth), F32)
    return pl.pallas_call(
        kernel, out_shape=jax.ShapeDtypeStruct((3, 1, rows, depth), F32), in_specs=specs, out_specs=HBM,
        input_output_aliases=aliases,
        scratch_shapes=[
            block, block, block, pltpu.VMEM((tiles, rows, LANES), F32), pltpu.VMEM((tiles, rows, 2 * LANES), BF),
            pltpu.SemaphoreType.DMA((3 + sum(source[2] for source in sources),)),
            *[pltpu.VMEM((source[1], rows, LANES), F32) for source in sources],
        ],
        compiler_params=params(),
        cost_estimate=cost(pairs * 16 * rows * CHUNK * LANES, 20 * rows * depth), name="home_step",
    )(*operands)


def body(flow, marker_cells, marker_weights, solid_blocks, *, pens, grps):
    _, planes, rows, depth = flow.shape
    assert planes == 1 and depth % LANES == 0 and rows % 8 == 0
    width = depth // grps
    plan = Plan(pens, rows, depth)
    plan.marker_rows = -(-marker_weights.shape[2] // LANES // 8) * 8
    pen_at = jnp.full((1,), lax.axis_index("pen"), jnp.int32)
    tables = [jnp.asarray(t) for t in split_table(pens * rows)]
    tables_z = tables if depth == pens * rows else [jnp.asarray(t) for t in split_table(depth)]

    def after(value, *others):
        return lax.optimization_barrier((value, others))[0]

    chips = plan.chips
    shifts = sorted(range(1, chips), key=lambda s: abs(2 * s - chips))

    def send_lines(blocks):
        got = {0: blocks[0]}
        for s in shifts:
            got[s] = lax.ppermute(blocks[s], "pen", [(i, (i + CORES * s) % pens) for i in range(pens)])
        return [got[s] for s in range(chips)]

    def swap(blocks):
        def other(value):
            return lax.ppermute(value, "pen", [(i, i ^ 1) for i in range(pens)])

        joined = other(jnp.concatenate(blocks[1:], axis=0))
        return [other(blocks[0])] + jnp.split(joined, chips - 1, axis=0)

    def cut_depth(value):
        return jnp.moveaxis(value.reshape(*value.shape[:-1], grps, width), -2, 0)

    def exchange(value):
        return lax.all_to_all(value, "grp", 0, 0, tiled=True)

    def slopes_of(rounds, cut, lines):
        return line_slopes(plan, rounds, cut, pen_at, lines, swap(lines), tables)

    first, second = plan.stages
    middle = -(-len(second) // 2)
    cut = [second[:middle], second[middle:]] if len(second) > 1 else [second]
    together = lax.optimization_barrier

    packed = pack_lines(plan, pen_at, flow)
    lines = send_lines(packed[0])
    lines_x = exchange(cut_depth(after(flow, packed)[:, 0]))
    order = marker_order(*after((marker_cells[0, 0], marker_weights[0, 0]), packed), rows, depth)
    lines, order, packed = together((lines, order, packed))
    lines_2 = send_lines(packed[1])
    (slopes,) = slopes_of(first, [first], lines)
    terms_x, slopes_x = slab_terms(compact_matrix(grps), after(lines_x, slopes))
    across = exchange(terms_x)
    lines_2, slopes, slopes_x = together((lines_2, slopes, slopes_x))
    back = send_lines(slopes)
    slopes = slopes_of(second, cut, lines_2)
    base, slope_z = depth_terms(after(flow, slopes), tables_z)
    across = jnp.moveaxis(after(across, base), 0, 2).reshape(3, rows, depth)
    back, slopes, across, base, slope_z = together((back, slopes, across, base, slope_z))
    groups = [(first, back)]
    step = functools.partial(home_step, plan, me=pen_at, flow=flow, base=base, across=across, order=order, solid=solid_blocks[0])
    back = send_lines(slopes[0])
    poisson = exchange(home_divergence(plan, grps, pen_at, slope_z, groups))
    out = step(1, groups=groups, out=None)
    slopes, back, out, poisson = together((slopes, back, out, poisson))
    groups = groups + [(cut[0], back)]
    if len(cut) > 1:
        back = send_lines(slopes[1])
    out = step(0, groups=groups, out=out)
    if len(cut) > 1:
        back, out = together((back, out))
        groups = groups + [(cut[1], back)]
    out = step(2, groups=groups, out=out)
    return out, poisson + slopes_x


def solution(mesh):
    return jax.shard_map(
        functools.partial(body, pens=mesh.shape["pen"], grps=mesh.shape["grp"]),
        mesh=mesh,
        in_specs=(
            P(None, "grp", "pen", None),
            P("grp", "pen", None, None),
            P("grp", "pen", None, None),
            P("grp", "pen", None),
        ),
        out_specs=(P(None, "grp", "pen", None), P(None, "pen", "grp")),
        check_vma=False,
    )
```

time: 319 us -> 257 us (0.81)
  starting transfers between devices: 58.4 us -> 30.9 us
  local copies, waits for them, and re-layouts: 43.7 us -> 22.3 us
  Pallas kernels: 108 us -> 91.3 us
    ppermute x44 -> x19, starting transfers between devices: 58.4 us -> 18.4 us  [the longest x15 17 us: send_lines(): lax.ppermute(blocks[s], 'pen', [(i, (i + CORES * s) % pens) for i in rang...]
    unnamed x88 -> x37, local copies, waits for them, and re-layouts: 30.4 us -> 3.88 us
    pallas_call x8 -> x7, Pallas kernels: 96.8 us -> 75.4 us  [the longest x3 48 us: home_step(): pl.pallas_call(kernel, out_shape=jax.ShapeDtypeStruct((3, 1, rows, depth)...]
    all_to_all x0 -> x3, starting transfers between devices: none -> 12.5 us  [exchange(): return lax.all_to_all(value, 'grp', 0, 0, tiled=True)]
    another operation x2 -> x3, local copies, waits for them, and re-layouts: 0.26 us -> 11.2 us  [the longest x2 11.2 us: cut_depth(): return jnp.moveaxis(value.reshape(*value.shape[:-1], grps, width), -2, 0)]
    dynamic_slice x2 -> x0, local copies, waits for them, and re-layouts: 4.76 us -> none  [the longest x1 4.63 us: body(): lax.dynamic_slice_in_dim(fields, lax.rem(grp + s, grps) * width, width, 2)]
    dynamic_update_slice x4 -> x0, local copies, waits for them, and re-layouts: 3.94 us -> none  [body(): lax.dynamic_update_slice_in_dim(across, block, lax.rem(grp + grps - s, gr...]
    pallas_call x1, Pallas kernels: 6.83 us -> 10.2 us  [depth_terms(): pl.pallas_call(kernel, grid=(rows // step,), out_shape=[jax.ShapeDtypeStr...]
  transfers between devices with their start and end apart: 44 -> 22, of which waited for: 9 -> 9; matrix products, arithmetic and copies ran while one was open for 6% -> 12% of each run, Pallas kernels for 34% -> 27%
where the time goes in v2:
time: 257 us; the launch traced here: 254 us
  waiting for transfers between devices  96.6 us (38%)
  Pallas kernels  91.3 us (36%)
  starting transfers between devices  30.9 us (12%)
  local copies, waits for them, and re-layouts  22.3 us (9%)
  other arithmetic  12.2 us (5%)
    ppermute x15, waiting for transfers between devices, send_lines(): lax.ppermute(blocks[s], 'pen', [(i, (i + CORES * s) % pens) for i in rang...  95.3 us
    pallas_call x3, Pallas kernels, home_step(): pl.pallas_call(kernel, out_shape=jax.ShapeDtypeStruct((3, 1, rows, depth)...  48 us
    pallas_call x2, Pallas kernels, line_slopes(): pl.pallas_call(kernel, out_shape=shapes, in_specs=[SMEM, VMEM, VMEM] + [H...  20.2 us
    ppermute x15, starting transfers between devices, send_lines(): lax.ppermute(blocks[s], 'pen', [(i, (i + CORES * s) % pens) for i in rang...  17 us
    all_to_all x3, starting transfers between devices, exchange(): return lax.all_to_all(value, 'grp', 0, 0, tiled=True)  12.5 us
    another operation x2, local copies, waits for them, and re-layouts, cut_depth(): return jnp.moveaxis(value.reshape(*value.shape[:-1], grps, width), -2, 0)  11.2 us
    pallas_call x1, Pallas kernels, depth_terms(): pl.pallas_call(kernel, grid=(rows // step,), out_shape=[jax.ShapeDtypeStr...  10.2 us
    sort x1, other arithmetic, marker_order(): key, weight = lax.sort((place * markers + marker, weight), num_keys=1)  6.89 us
  transfers between devices with their start and end apart: 22, of which 9 were waited for; matrix products, arithmetic and copies ran while one was open for 12% of the time, Pallas kernels for 27%

profile of v2, /device:TPU:9, one launch (start us, length us, event | category | flops | bytes accessed | tf_op | source)
XLA Modules:
  0.0 254.5 jit_solution(1482820213266897265)
XLA Ops:
  0.6 4.2 %pack_lines.1 = (f32[6,192,128]{2,1,0:T(8,128)}, f32[6,192,128]{2,1,0:T(8,128)}, f32[6,192,128]{2,1,0:T(8,128)}, f32[6,192,128]{2,1,0:T(8,128)}, f32[6,192,128]{...) custom-call(s32[1]{0:T(128)} %bitcast.me_ref, f32[4,1,192,1536]{3,2,1,0:T(8,128)} %flow_ref.8), custom_call_target="tpu_custom_call" | custom-call | bytes 23592 | tf_op jit(solution)/shard_map/pack_lines/pallas_call | solution.py:121
  7.3 1.4 collective-permute-start.2
  8.7 6.2 %reshape_squeeze.3 = f32[4,192,4,384]{3,2,1,0:T(4,128)} reshape(f32[4,1,192,1536]{3,2,1,0:T(8,128)} %flow_ref.8) | data formatting | bytes 9437184 | tf_op jit(solution)/shard_map/reshape;squeeze | solution.py:458
  14.9 5.0 %copy.36 = f32[4,192,4,384]{3,1,0,2:T(8,128)} copy(f32[4,192,4,384]{3,2,1,0:T(4,128)} %reshape_squeeze.3) | data formatting | bytes 9437184 | tf_op jit(solution)/shard_map/reshape;squeeze | solution.py:458
  19.9 5.1 %all-to-all-start = ((f32[4,4,192,384]{3,2,1,0:T(8,128)}), f32[4,4,192,384]{3,2,1,0:T(8,128)}, u32[]{:S(2)}, u32[]{:S(2)}) async-start(f32[4,4,192,384]{3,2,1,0:T(8,128)} %bitcast.20), calls=%async_computation | async-start | bytes 9437184 | tf_op jit(solution)/shard_map/all_to_all | solution.py:461
  27.1 6.9 %sort.23 = (s32[8192]{0:T(1024)S(1)}, f32[8192]{0:T(1024)}, s32[8192]{0:T(1024)}) sort(s32[8192]{0:T(1024)S(1)} %fusion.5, f32[8192]{0:T(1024)S(1)} %reshape.61, s32[8192]{0:T(1024)S(1)} %iota.19), dimensions={0}, to_apply=%region_0.1 | sort | flops 106496 | bytes 196608 | tf_op jit(solution)/shard_map/sort | solution.py:265
  37.0 19.5 %collective-permute-done.1.rest_2_ = f32[6,192,128]{2,1,0:T(8,128)S(1)} collective-permute-done((f32[6,192,128]{2,1,0:T(8,128)}, f32[6,192,128]{2,1,0:T(8,128)S(1)}, u32[]{:S(2)}, u32[]{:S(2)}) %collective-permute-start.1) | collective-permute-done | bytes 589856 | tf_op jit(solution)/shard_map/ppermute | solution.py:447
  56.4 2.8 %collective-permute-done.2.rest_3_ = f32[6,192,128]{2,1,0:T(8,128)S(1)} collective-permute-done((f32[6,192,128]{2,1,0:T(8,128)}, f32[6,192,128]{2,1,0:T(8,128)S(1)}, u32[]{:S(2)}, u32[]{:S(2)}) %collective-permute-start.2) | collective-permute-done | bytes 589856 | tf_op jit(solution)/shard_map/ppermute | solution.py:447
  61.0 1.5 collective-permute-start.4
  62.5 1.5 collective-permute-start.5
  66.1 10.1 %line_slopes.2 = (f32[6,192,128]{2,1,0:T(8,128)}, f32[6,192,128]{2,1,0:T(8,128)}, f32[6,192,128]{2,1,0:T(8,128)}, f32[6,192,128]{2,1,0:T(8,128)}) custom-call(s32[1]{0:T(128)} %bitcast.me_ref, bf16[2,768,768]{2,1,0:T(8,128)(2,1)} %constant.110.clone.high_ref, bf16[2,768,768]{2,1,0:T(8,128)(2,1)} %constant.111.clone.low_ref, ...), custom_call_target="tpu_custom_call" | custom-call | flops 27179088 | bytes 117964 | tf_op jit(solution)/shard_map/line_slopes/pallas_call | solution.py:182
  77.5 5.7 %slab_terms.1 = (f32[4,3,192,384]{3,2,1,0:T(8,128)}, f32[4,192,384]{2,1,0:T(8,128)}) custom-call(f32[4,4,192,384]{3,2,1,0:T(8,128)} %all-to-all-done.in_ref), custom_call_target="tpu_custom_call" | custom-call | flops 188743 | bytes 94371 | tf_op jit(solution)/shard_map/slab_terms/pallas_call | solution.py:247
  83.2 3.7 %all-to-all-start.1 = ((f32[4,3,192,384]{3,2,1,0:T(8,128)}), f32[4,3,192,384]{3,2,1,0:T(8,128)S(1)}, u32[]{:S(2)}, u32[]{:S(2)}) async-start(f32[4,3,192,384]{3,2,1,0:T(8,128)} %get-tuple-element.134), calls=%async_computation.1 | async-start | bytes 7077888 | tf_op jit(solution)/shard_map/all_to_all | solution.py:461
  86.9 25.1 %collective-permute-done.4.rest_2_ = f32[6,192,128]{2,1,0:T(8,128)} collective-permute-done((f32[6,192,128]{2,1,0:T(8,128)}, f32[6,192,128]{2,1,0:T(8,128)}, u32[]{:S(2)}, u32[]{:S(2)}) %collective-permute-start.4) | collective-permute-done | bytes 589856 | tf_op jit(solution)/shard_map/ppermute | solution.py:447
  112.0 2.5 collective-permute-done.5.rest_3_
  114.6 1.6 pad_maximum_fusion.1
  116.8 1.5 collective-permute-start.8
  118.3 2.6 %collective-permute-start.9 = (f32[6,192,128]{2,1,0:T(8,128)}, f32[6,192,128]{2,1,0:T(8,128)}, u32[]{:S(2)}, u32[]{:S(2)}) collective-permute-start(f32[6,192,128]{2,1,0:T(8,128)} %get-tuple-element.120), channel_id=1, source_target_pairs={{0,4},{1,5},{2,6},{3,7},{4,0},{5,1},{6,2},{7,3},{8,12},{9,13},{10,... | collective-permute-start | bytes 1769480 | tf_op jit(solution)/shard_map/ppermute | solution.py:447
  122.9 10.1 %line_slopes.3 = (f32[3,192,128]{2,1,0:T(8,128)}, f32[3,192,128]{2,1,0:T(8,128)}, f32[3,192,128]{2,1,0:T(8,128)}, f32[3,192,128]{2,1,0:T(8,128)}, f32[3,192,128]...) custom-call(s32[1]{0:T(128)} %bitcast.me_ref, ...), custom_call_target="tpu_custom_call" | custom-call | flops 27179088 | bytes 117964 | tf_op jit(solution)/shard_map/line_slopes/pallas_call | solution.py:182
  133.0 10.2 %depth_terms.1 = (f32[3,192,1536]{2,1,0:T(8,128)}, f32[192,1536]{1,0:T(8,128)}) custom-call(f32[4,1,192,1536]{3,2,1,0:T(8,128)} %flow_ref.8, bf16[2,768,768]{2,1,0:T(8,128)(2,1)} %constant.110.clone.high_ref, bf16[2,768,768]{2,1,0:T(8,128)(2,1)} %constant.111.clone.low_ref), custom_call_target="tpu_custom_call" | custom-call | flops 54358180 | bytes 141557 | tf_op jit(solution)/shard_map/depth_terms/pallas_call | solution.py:220
  143.3 2.3 copy.34
  145.6 23.8 %collective-permute-done.9.rest_2_.rest_6_ = f32[6,192,128]{2,1,0:T(8,128)} collective-permute-done((f32[6,192,128]{2,1,0:T(8,128)}, f32[6,192,128]{2,1,0:T(8,128)}, u32[]{:S(2)}, u32[]{:S(2)}) %collective-permute-start.9) | collective-permute-done | bytes 589856 | tf_op jit(solution)/shard_map/ppermute | solution.py:447
  169.3 3.0 %home_divergence.1 = f32[4,192,384]{2,1,0:T(8,128)} custom-call(s32[1]{0:T(128)} %bitcast.me_ref, f32[192,1536]{1,0:T(8,128)} %get-tuple-element.157.slope_ref, f32[6,192,128]{2,1,0:T(8,128)} %get-tuple-element.153.rest_0_.rest_4_, f32[6,192,128]{2,1,0:T(8,128)} %collective-permute-done.8.rest_1_.rest_5_, ...), custom_call_target="tpu_custom_call" | custom-call | bytes 35389 | tf_op jit(solution)/shard_map/home_divergence/pallas_call | solution.py:316
  172.4 3.7 %all-to-all-start.2 = ((f32[4,192,384]{2,1,0:T(8,128)}), f32[4,192,384]{2,1,0:T(8,128)S(1)}, u32[]{:S(2)}, u32[]{:S(2)}) async-start(f32[4,192,384]{2,1,0:T(8,128)} %home_divergence.1), calls=%async_computation.2 | async-start | bytes 2359296 | tf_op jit(solution)/shard_map/all_to_all | solution.py:461
  176.1 3.4 %collective-permute-start.14 = (f32[3,192,128]{2,1,0:T(8,128)}, f32[3,192,128]{2,1,0:T(8,128)S(1)}, u32[]{:S(2)}, u32[]{:S(2)}) collective-permute-start(f32[3,192,128]{2,1,0:T(8,128)} %get-tuple-element.146), channel_id=1, source_target_pairs={{0,4},{1,5},{2,6},{3,7},{4,0},{5,1},{6,2},{7,3},{8,12},{9,13},{10,... | collective-permute-start | bytes 884744 | tf_op jit(solution)/shard_map/ppermute | solution.py:447
  181.4 16.4 %home_step.3.rest_4_ = f32[3,1,192,1536]{3,2,1,0:T(8,128)} custom-call(s32[1]{0:T(128)} %bitcast.me_ref, s32[44]{0:T(128)} %copy-done.16, s32[44]{0:T(128)} %compare_select_fusion.tile_ref, f32[4,1,192,1536]{3,2,1,0:T(8,128)} %flow_ref.8, f32[3,192,1536]{2,1,0:T(8,128)} %get-tuple-element.139.base_ref, f32[3,192,1536]{2,1,0:T(8,128)} %bitcast.17, ...), custom_call_target="tpu_custom_call" | custom-call | flops 44291848 | bytes 58982 | tf_op jit(solution)/shard_map/home_step/pallas_call | solution.py:415
  197.9 3.0 %collective-permute-done.14.rest_2_ = f32[3,192,128]{2,1,0:T(8,128)S(1)} collective-permute-done((f32[3,192,128]{2,1,0:T(8,128)}, f32[3,192,128]{2,1,0:T(8,128)S(1)}, u32[]{:S(2)}, u32[]{:S(2)}) %collective-permute-start.14) | collective-permute-done | bytes 294944 | tf_op jit(solution)/shard_map/ppermute | solution.py:447
  200.9 11.6 %collective-permute-done.15.rest_3_ = f32[3,192,128]{2,1,0:T(8,128)S(1)} collective-permute-done((f32[3,192,128]{2,1,0:T(8,128)S(1)}, f32[3,192,128]{2,1,0:T(8,128)S(1)}, u32[]{:S(2)}, u32[]{:S(2)}) %collective-permute-start.15) | collective-permute-done | bytes 294944 | tf_op jit(solution)/shard_map/ppermute | solution.py:447
  212.5 1.4 collective-permute-start.18
  215.0 15.8 %home_step.4.rest_4_ = f32[3,1,192,1536]{3,2,1,0:T(8,128)} custom-call(s32[1]{0:T(128)} %bitcast.me_ref, s32[44]{0:T(128)} %copy-done.16, s32[44]{0:T(128)} %compare_select_fusion.tile_ref, f32[4,1,192,1536]{3,2,1,0:T(8,128)} %flow_ref.8, f32[3,192,1536]{2,1,0:T(8,128)} %get-tuple-element.139.base_ref, ...), custom_call_target="tpu_custom_call", output_to_operand_aliasing={{}: (15, {})} | custom-call | flops 44291848 | bytes 58982 | tf_op jit(solution)/shard_map/home_step/pallas_call | solution.py:415
  230.9 7.0 %collective-permute-done.17.rest_2_ = f32[3,192,128]{2,1,0:T(8,128)S(1)} collective-permute-done((f32[3,192,128]{2,1,0:T(8,128)}, f32[3,192,128]{2,1,0:T(8,128)S(1)}, u32[]{:S(2)}, u32[]{:S(2)}) %collective-permute-start.17) | collective-permute-done | bytes 294944 | tf_op jit(solution)/shard_map/ppermute | solution.py:447
  238.5 15.8 %home_step.5 = f32[3,1,192,1536]{3,2,1,0:T(8,128)} custom-call(s32[1]{0:T(128)} %bitcast.me_ref, s32[44]{0:T(128)} %copy-done.16, s32[44]{0:T(128)} %compare_select_fusion.tile_ref, f32[4,1,192,1536]{3,2,1,0:T(8,128)} %flow_ref.8, f32[3,192,1536]{2,1,0:T(8,128)} %get-tuple-element.139.base_ref, ...), custom_call_target="tpu_custom_call", output_to_operand_aliasing={{}: (15, {})} | custom-call | flops 44291848 | bytes 58982 | tf_op jit(solution)/shard_map/home_step/pallas_call | solution.py:415
  (90 shorter events, 19.0 us)
Async XLA Ops:
  4.9 32.1 %collective-permute-start = (f32[6,192,128]{2,1,0:T(8,128)}, f32[6,192,128]{2,1,0:T(8,128)S(1)}, u32[]{:S(2)}, u32[]{:S(2)}) collective-permute-start(f32[6,192,128]{2,1,0:T(8,128)} %get-tuple-element.90), channel_id=1, source_target_pairs={{0,2},{1,3},{2,4},{3,5},{4,6},{5,7},{6,0},{7,1},{8,10},{9,11},{10,... | collective-permute-start | bytes 1769480 | tf_op jit(solution)/shard_map/ppermute | solution.py:447
  6.2 50.2 %collective-permute-start.1 = (f32[6,192,128]{2,1,0:T(8,128)}, f32[6,192,128]{2,1,0:T(8,128)S(1)}, u32[]{:S(2)}, u32[]{:S(2)}) collective-permute-start(f32[6,192,128]{2,1,0:T(8,128)} %get-tuple-element.91), channel_id=1, source_target_pairs={{0,4},{1,5},{2,6},{3,7},{4,0},{5,1},{6,2},{7,3},{8,12},{9,13},{10,... | collective-permute-start | bytes 1769480 | tf_op jit(solution)/shard_map/ppermute | solution.py:447
  7.3 52.0 %collective-permute-start.2 = (f32[6,192,128]{2,1,0:T(8,128)}, f32[6,192,128]{2,1,0:T(8,128)S(1)}, u32[]{:S(2)}, u32[]{:S(2)}) collective-permute-start(f32[6,192,128]{2,1,0:T(8,128)} %get-tuple-element.92), channel_id=1, source_target_pairs={{0,6},{1,7},{2,0},{3,1},{4,2},{5,3},{6,4},{7,5},{8,14},{9,15},{10,... | collective-permute-start | bytes 1769480 | tf_op jit(solution)/shard_map/ppermute | solution.py:447
  19.9 5.1 %copy-start.13 = (s32[1,1,1024,8]{2,3,1,0:T(8,128)S(1)}, s32[1,1,1024,8]{2,3,1,0:T(8,128)}, u32[]{:S(2)}) copy-start(s32[1,1,1024,8]{2,3,1,0:T(8,128)} %param.7) | copy-start | bytes 98308
  19.9 57.6 %all-to-all-start = ((f32[4,4,192,384]{3,2,1,0:T(8,128)}), f32[4,4,192,384]{3,2,1,0:T(8,128)}, u32[]{:S(2)}, u32[]{:S(2)}) async-start(f32[4,4,192,384]{3,2,1,0:T(8,128)} %bitcast.20), calls=%async_computation | async-start | bytes 9437184 | tf_op jit(solution)/shard_map/all_to_all | solution.py:461
  35.1 24.3 %copy-start.16 = (s32[44]{0:T(128)}, s32[44]{0:T(128)S(1)}, u32[]{:S(2)}) copy-start(s32[44]{0:T(128)S(1)} %broadcast_minimum_fusion.chunk_ref) | copy-start | bytes 532
  37.0 22.5 %copy-start = (f32[6,192,128]{2,1,0:T(8,128)}, f32[6,192,128]{2,1,0:T(8,128)S(1)}, u32[]{:S(2)}) copy-start(f32[6,192,128]{2,1,0:T(8,128)S(1)} %collective-permute-done.rest_1_) | copy-start | bytes 1769476
  56.4 3.0 %copy-start.1 = (f32[6,192,128]{2,1,0:T(8,128)}, f32[6,192,128]{2,1,0:T(8,128)S(1)}, u32[]{:S(2)}) copy-start(f32[6,192,128]{2,1,0:T(8,128)S(1)} %collective-permute-done.1.rest_2_) | copy-start | bytes 1769476
  60.1 3.8 %collective-permute-start.7 = (f32[18,192,128]{2,1,0:T(8,128)S(1)}, f32[18,192,128]{2,1,0:T(8,128)S(1)}, u32[]{:S(2)}, u32[]{:S(2)}) collective-permute-start(f32[18,192,128]{2,1,0:T(8,128)S(1)} %pad_maximum_fusion), channel_id=1, source_target_pairs={{0,1},{1,0},{2,3},{3,2},{4,5},{5,4},{6,7},{7,6},{8,9},{9,8},{10,11... | collective-permute-start | bytes 5308424 | tf_op jit(solution)/shard_map/ppermute | solution.py:452
  60.6 4.7 %collective-permute-start.6 = (f32[6,192,128]{2,1,0:T(8,128)S(1)}, f32[6,192,128]{2,1,0:T(8,128)S(1)}, u32[]{:S(2)}, u32[]{:S(2)}) collective-permute-start(f32[6,192,128]{2,1,0:T(8,128)S(1)} %copy-done.5), channel_id=1, source_target_pairs={{0,1},{1,0},{2,3},{3,2},{4,5},{5,4},{6,7},{7,6},{8,9},{9,8},{10,11... | collective-permute-start | bytes 1769480 | tf_op jit(solution)/shard_map/ppermute | solution.py:452
  61.0 26.0 %collective-permute-start.3 = (f32[6,192,128]{2,1,0:T(8,128)}, f32[6,192,128]{2,1,0:T(8,128)}, u32[]{:S(2)}, u32[]{:S(2)}) collective-permute-start(f32[6,192,128]{2,1,0:T(8,128)} %get-tuple-element.104), channel_id=1, source_target_pairs={{0,2},{1,3},{2,4},{3,5},{4,6},{5,7},{6,0},{7,1},{8,10},{9,11},{10,... | collective-permute-start | bytes 1769480 | tf_op jit(solution)/shard_map/ppermute | solution.py:447
  61.0 51.1 %collective-permute-start.4 = (f32[6,192,128]{2,1,0:T(8,128)}, f32[6,192,128]{2,1,0:T(8,128)}, u32[]{:S(2)}, u32[]{:S(2)}) collective-permute-start(f32[6,192,128]{2,1,0:T(8,128)} %get-tuple-element.105), channel_id=1, source_target_pairs={{0,4},{1,5},{2,6},{3,7},{4,0},{5,1},{6,2},{7,3},{8,12},{9,13},{10,... | collective-permute-start | bytes 1769480 | tf_op jit(solution)/shard_map/ppermute | solution.py:447
  62.5 52.1 %collective-permute-start.5 = (f32[6,192,128]{2,1,0:T(8,128)}, f32[6,192,128]{2,1,0:T(8,128)}, u32[]{:S(2)}, u32[]{:S(2)}) collective-permute-start(f32[6,192,128]{2,1,0:T(8,128)} %get-tuple-element.106), channel_id=1, source_target_pairs={{0,6},{1,7},{2,0},{3,1},{4,2},{5,3},{6,4},{7,5},{8,14},{9,15},{10,... | collective-permute-start | bytes 1769480 | tf_op jit(solution)/shard_map/ppermute | solution.py:447
  83.2 60.1 %all-to-all-start.1 = ((f32[4,3,192,384]{3,2,1,0:T(8,128)}), f32[4,3,192,384]{3,2,1,0:T(8,128)S(1)}, u32[]{:S(2)}, u32[]{:S(2)}) async-start(f32[4,3,192,384]{3,2,1,0:T(8,128)} %get-tuple-element.134), calls=%async_computation.1 | async-start | bytes 7077888 | tf_op jit(solution)/shard_map/all_to_all | solution.py:461
  116.2 4.7 %collective-permute-start.12 = (f32[18,192,128]{2,1,0:T(8,128)S(1)}, f32[18,192,128]{2,1,0:T(8,128)S(1)}, u32[]{:S(2)}, u32[]{:S(2)}) collective-permute-start(f32[18,192,128]{2,1,0:T(8,128)S(1)} %pad_maximum_fusion.1), channel_id=1, source_target_pairs={{0,1},{1,0},{2,3},{3,2},{4,5},{5,4},{6,7},{7,6},{8,9},{9,8},{10,11... | collective-permute-start | bytes 5308424 | tf_op jit(solution)/shard_map/ppermute | solution.py:452
  116.7 5.4 %collective-permute-start.11 = (f32[6,192,128]{2,1,0:T(8,128)S(1)}, f32[6,192,128]{2,1,0:T(8,128)S(1)}, u32[]{:S(2)}, u32[]{:S(2)}) collective-permute-start(f32[6,192,128]{2,1,0:T(8,128)S(1)} %copy-done.4), channel_id=1, source_target_pairs={{0,1},{1,0},{2,3},{3,2},{4,5},{5,4},{6,7},{7,6},{8,9},{9,8},{10,11... | collective-permute-start | bytes 1769480 | tf_op jit(solution)/shard_map/ppermute | solution.py:452
  116.8 28.7 %collective-permute-start.10 = (f32[6,192,128]{2,1,0:T(8,128)}, f32[6,192,128]{2,1,0:T(8,128)}, u32[]{:S(2)}, u32[]{:S(2)}) collective-permute-start(f32[6,192,128]{2,1,0:T(8,128)} %get-tuple-element.121), channel_id=1, source_target_pairs={{0,6},{1,7},{2,0},{3,1},{4,2},{5,3},{6,4},{7,5},{8,14},{9,15},{10,... | collective-permute-start | bytes 1769480 | tf_op jit(solution)/shard_map/ppermute | solution.py:447
  116.8 28.7 %collective-permute-start.8 = (f32[6,192,128]{2,1,0:T(8,128)}, f32[6,192,128]{2,1,0:T(8,128)}, u32[]{:S(2)}, u32[]{:S(2)}) collective-permute-start(f32[6,192,128]{2,1,0:T(8,128)} %get-tuple-element.119), channel_id=1, source_target_pairs={{0,2},{1,3},{2,4},{3,5},{4,6},{5,7},{6,0},{7,1},{8,10},{9,11},{10,... | collective-permute-start | bytes 1769480 | tf_op jit(solution)/shard_map/ppermute | solution.py:447
  118.3 51.0 %collective-permute-start.9 = (f32[6,192,128]{2,1,0:T(8,128)}, f32[6,192,128]{2,1,0:T(8,128)}, u32[]{:S(2)}, u32[]{:S(2)}) collective-permute-start(f32[6,192,128]{2,1,0:T(8,128)} %get-tuple-element.120), channel_id=1, source_target_pairs={{0,4},{1,5},{2,6},{3,7},{4,0},{5,1},{6,2},{7,3},{8,12},{9,13},{10,... | collective-permute-start | bytes 1769480 | tf_op jit(solution)/shard_map/ppermute | solution.py:447
  172.4 7.2 %copy-start.17 = (f32[3,192,128]{2,1,0:T(8,128)S(1)}, f32[3,192,128]{2,1,0:T(8,128)}, u32[]{:S(2)}) copy-start(f32[3,192,128]{2,1,0:T(8,128)} %get-tuple-element.147) | copy-start | bytes 884740
  172.4 8.3 %copy-start.15 = (s32[1,192,12]{1,0,2:T(1,128)S(1)}, s32[1,192,12]{1,0,2:T(1,128)}, u32[]{:S(2)}) copy-start(s32[1,192,12]{1,0,2:T(1,128)} %param.9) | copy-start | bytes 27652
  172.4 40.0 %all-to-all-start.2 = ((f32[4,192,384]{2,1,0:T(8,128)}), f32[4,192,384]{2,1,0:T(8,128)S(1)}, u32[]{:S(2)}, u32[]{:S(2)}) async-start(f32[4,192,384]{2,1,0:T(8,128)} %home_divergence.1), calls=%async_computation.2 | async-start | bytes 2359296 | tf_op jit(solution)/shard_map/all_to_all | solution.py:461
  176.1 21.8 %collective-permute-start.13 = (f32[3,192,128]{2,1,0:T(8,128)}, f32[3,192,128]{2,1,0:T(8,128)S(1)}, u32[]{:S(2)}, u32[]{:S(2)}) collective-permute-start(f32[3,192,128]{2,1,0:T(8,128)} %get-tuple-element.145), channel_id=1, source_target_pairs={{0,2},{1,3},{2,4},{3,5},{4,6},{5,7},{6,0},{7,1},{8,10},{9,11},{10,... | collective-permute-start | bytes 884744 | tf_op jit(solution)/shard_map/ppermute | solution.py:447
  176.1 24.7 %collective-permute-start.14 = (f32[3,192,128]{2,1,0:T(8,128)}, f32[3,192,128]{2,1,0:T(8,128)S(1)}, u32[]{:S(2)}, u32[]{:S(2)}) collective-permute-start(f32[3,192,128]{2,1,0:T(8,128)} %get-tuple-element.146), channel_id=1, source_target_pairs={{0,4},{1,5},{2,6},{3,7},{4,0},{5,1},{6,2},{7,3},{8,12},{9,13},{10,... | collective-permute-start | bytes 884744 | tf_op jit(solution)/shard_map/ppermute | solution.py:447
  179.6 32.8 %collective-permute-start.15 = (f32[3,192,128]{2,1,0:T(8,128)S(1)}, f32[3,192,128]{2,1,0:T(8,128)S(1)}, u32[]{:S(2)}, u32[]{:S(2)}) collective-permute-start(f32[3,192,128]{2,1,0:T(8,128)S(1)} %copy-done.17), channel_id=1, source_target_pairs={{0,6},{1,7},{2,0},{3,1},{4,2},{5,3},{6,4},{7,5},{8,14},{9,15},{10,... | collective-permute-start | bytes 884744 | tf_op jit(solution)/shard_map/ppermute | solution.py:447
  181.4 32.5 %copy-start.3 = (f32[4,192,384]{2,1,0:T(8,128)S(1)}, f32[4,192,384]{2,1,0:T(8,128)}, u32[]{:S(2)}) copy-start(f32[4,192,384]{2,1,0:T(8,128)} %get-tuple-element.173) | copy-start | bytes 3538948
  197.8 17.2 %copy-start.8 = (f32[3,192,128]{2,1,0:T(8,128)}, f32[3,192,128]{2,1,0:T(8,128)S(1)}, u32[]{:S(2)}) copy-start(f32[3,192,128]{2,1,0:T(8,128)S(1)} %collective-permute-done.13.rest_1_) | copy-start | bytes 884740
  200.9 14.2 %copy-start.9 = (f32[3,192,128]{2,1,0:T(8,128)}, f32[3,192,128]{2,1,0:T(8,128)S(1)}, u32[]{:S(2)}) copy-start(f32[3,192,128]{2,1,0:T(8,128)S(1)} %collective-permute-done.14.rest_2_) | copy-start | bytes 884740
  212.4 18.4 %collective-permute-start.16 = (f32[3,192,128]{2,1,0:T(8,128)}, f32[3,192,128]{2,1,0:T(8,128)S(1)}, u32[]{:S(2)}, u32[]{:S(2)}) collective-permute-start(f32[3,192,128]{2,1,0:T(8,128)} %get-tuple-element.159), channel_id=1, source_target_pairs={{0,2},{1,3},{2,4},{3,5},{4,6},{5,7},{6,0},{7,1},{8,10},{9,11},{10,... | collective-permute-start | bytes 884744 | tf_op jit(solution)/shard_map/ppermute | solution.py:447
  212.4 25.4 %collective-permute-start.17 = (f32[3,192,128]{2,1,0:T(8,128)}, f32[3,192,128]{2,1,0:T(8,128)S(1)}, u32[]{:S(2)}, u32[]{:S(2)}) collective-permute-start(f32[3,192,128]{2,1,0:T(8,128)} %get-tuple-element.160), channel_id=1, source_target_pairs={{0,4},{1,5},{2,6},{3,7},{4,0},{5,1},{6,2},{7,3},{8,12},{9,13},{10,... | collective-permute-start | bytes 884744 | tf_op jit(solution)/shard_map/ppermute | solution.py:447
  212.5 25.3 %collective-permute-start.18 = (f32[3,192,128]{2,1,0:T(8,128)}, f32[3,192,128]{2,1,0:T(8,128)}, u32[]{:S(2)}, u32[]{:S(2)}) collective-permute-start(f32[3,192,128]{2,1,0:T(8,128)} %get-tuple-element.161), channel_id=1, source_target_pairs={{0,6},{1,7},{2,0},{3,1},{4,2},{5,3},{6,4},{7,5},{8,14},{9,15},{10,... | collective-permute-start | bytes 884744 | tf_op jit(solution)/shard_map/ppermute | solution.py:447
  230.8 7.0 %copy-start.11 = (f32[3,192,128]{2,1,0:T(8,128)}, f32[3,192,128]{2,1,0:T(8,128)S(1)}, u32[]{:S(2)}) copy-start(f32[3,192,128]{2,1,0:T(8,128)S(1)} %collective-permute-done.16.rest_1_) | copy-start | bytes 884740
  (8 other events, 10.8 us)

commit v3 on v2

--- a/solution.py
+++ b/solution.py
@@ -62,8 +62,8 @@
     return pltpu.CompilerParams(vmem_limit_bytes=60 * 2**20)
 
 
-def cost(flops, moved):
-    return pl.CostEstimate(flops=int(flops) // 100, bytes_accessed=int(moved) // 100, transcendentals=0)
+def cost(flops, moved, share=0.01):
+    return pl.CostEstimate(flops=int(flops * share), bytes_accessed=int(moved * share), transcendentals=0)
 
 
 class Plan:
@@ -93,38 +93,30 @@
         c.wait()
 
 
-def pack_lines(plan, me, flow):
-    n, stages = plan.chips, plan.stages
+def pack_lines(plan, rounds, me, flow):
+    n = plan.chips
     fields, _, rows, depth = flow.shape
+    used = FIELD_ORDER[rounds[0] * n // plan.tiles : min((rounds[-1] * n + n - 1) // plan.tiles, fields - 1) + 1]
 
     def kernel(me_ref, flow_ref, *rest):
         outs, (held, in_sems, out_sems) = rest[:-3], rest[-3:]
-        loads = [pltpu.make_async_copy(flow_ref.at[f, 0], held.at[f], in_sems.at[f]) for f in FIELD_ORDER]
-        for c in loads:
-            c.start()
+        run_copies([pltpu.make_async_copy(flow_ref.at[f, 0], held.at[f], in_sems.at[f]) for f in used])
         copies = []
-        for i, rounds in enumerate(stages):
-            last = min((rounds[-1] * n + n - 1) // plan.tiles, fields - 1)
-            while len(loads) > fields - 1 - last:
-                loads.pop(0).wait()
-            for s in range(n):
-                chip = lax.rem(me_ref[0] // CORES + s, n)
-                for k, r in enumerate(rounds):
-                    field, z = plan.place(r, chip)
-                    c = pltpu.make_async_copy(held.at[field, :, pl.ds(z, LANES)], outs[i * n + s].at[k], out_sems.at[len(copies)])
-                    c.start()
-                    copies.append(c)
-        for c in copies:
-            c.wait()
-
-    shapes = [jax.ShapeDtypeStruct((len(rounds), rows, LANES), F32) for rounds in stages for _ in range(n)]
-    out = pl.pallas_call(
-        kernel, out_shape=shapes, in_specs=[SMEM, HBM], out_specs=[HBM] * len(shapes),
+        for s in range(n):
+            chip = lax.rem(me_ref[0] // CORES + s, n)
+            for k, r in enumerate(rounds):
+                field, z = plan.place(r, chip)
+                copies.append(pltpu.make_async_copy(
+                    held.at[field, :, pl.ds(z, LANES)], outs[s].at[k], out_sems.at[len(copies)]))
+        run_copies(copies)
+
+    shape = jax.ShapeDtypeStruct((len(rounds), rows, LANES), F32)
+    return pl.pallas_call(
+        kernel, out_shape=[shape] * n, in_specs=[SMEM, HBM], out_specs=[HBM] * n,
         scratch_shapes=[pltpu.VMEM((fields, rows, depth), F32), pltpu.SemaphoreType.DMA((fields,)),
-                        pltpu.SemaphoreType.DMA((n * plan.rounds,))],
+                        pltpu.SemaphoreType.DMA((n * len(rounds),))],
         compiler_params=params(), cost_estimate=cost(0, 2 * flow.size), name="pack_lines",
     )(me, flow)
-    return [out[i * n : (i + 1) * n] for i in range(len(stages))]
 
 
 def line_slopes(plan, rounds, groups, me, received, other, tables):
@@ -322,7 +314,7 @@
     )(me, slope_z, *buffers)
 
 
-def home_step(plan, component, me, flow, base, across, groups, order, solid, out):
+def home_step(plan, component, me, flow, base, groups, order, solid, out, share=0.01):
     rows, depth, tiles = plan.rows, plan.depth, plan.tiles
     wanted = (1, 3) if component == 1 else (component,)
     sources = [home_slopes(plan, FIELD_ORDER.index(f), groups) for f in wanted]
@@ -333,17 +325,16 @@
     chunks = entries[0].shape[0]
     marker_rows = plan.marker_rows
 
-    def kernel(me_ref, chunk_ref, tile_ref, flow_ref, base_ref, across_ref, row_ref, lane_ref, marker_ref,
+    def kernel(me_ref, chunk_ref, tile_ref, flow_ref, base_ref, row_ref, lane_ref, marker_ref,
                weight_ref, solid_ref, *rest):
         bufs = rest[:total]
         rest = rest[total:]
         if out is not None:
             rest = rest[1:]
-        out_ref, speed, value, cross, prov, terms, sems, *slopes = rest
+        out_ref, speed, value, prov, terms, found, sems, *slopes = rest
         copies = [
             pltpu.make_async_copy(flow_ref.at[1, 0], speed, sems.at[0]),
             pltpu.make_async_copy(base_ref.at[component], value, sems.at[1]),
-            pltpu.make_async_copy(across_ref.at[component], cross, sems.at[2]),
         ]
         used = 0
         for (held, _, count, _, copies_of), ref in zip(sources, slopes):
@@ -352,7 +343,7 @@
         run_copies(copies)
         for t in range(tiles):
             z = slice(t * LANES, (t + 1) * LANES)
-            term = cross[:, z] + speed[:, z] * slopes[0][sources[0][3] + t]
+            term = speed[:, z] * slopes[0][sources[0][3] + t]
             if component == 1:
                 term = term + slopes[1][sources[1][3] + t]
             result = value[:, z] - 0.1 * term
@@ -366,31 +357,45 @@
         marker_at = lax.broadcasted_iota(jnp.int32, (marker_rows, CHUNK), 0)
         one, zero = jnp.ones((), BF), jnp.zeros((), BF)
 
-        def entry(i):
+        def one_hot(hit):
+            return jnp.where(hit, 1.0, 0.0).astype(BF)
+
+        def pair(i):
             c, t = chunk_ref[i], tile_ref[i]
+            return c, jnp.minimum(t, tiles - 1), row_at == row_ref[c] - t * rows, lane_at == lane_ref[c]
+
+        found[...] = jnp.zeros_like(found)
+
+        def gather(i, carry):
+            c, t, rows_hit, lanes_hit = pair(i)
+            lanes = one_hot(lanes_hit)
+            both = dot(terms[t], jnp.concatenate([lanes, lanes], axis=0))
+            found[c] += jnp.sum(jnp.where(rows_hit, both, 0.0), axis=0, keepdims=True)
+            return carry
+
+        lax.fori_loop(0, pairs, gather, 0, unroll=UNROLL)
+
+        def add_up(c, total):
             m = marker_ref[c]
-            low_part = jnp.where(lane_at == m % LANES, 1.0, 0.0).astype(BF)
-            return c, jnp.minimum(t, tiles - 1), row_at == row_ref[c] - t * rows, lane_at == lane_ref[c], marker_at == m // LANES, low_part
-
-        def gather(i, total):
-            c, t, rows_hit, lanes_hit, marker_hit, low_part = entry(i)
-            lanes = jnp.where(lanes_hit, 1.0, 0.0).astype(BF)
-            both = dot(terms[t], jnp.concatenate([lanes, lanes], axis=0))
-            found = jnp.sum(jnp.where(rows_hit, both, 0.0), axis=0, keepdims=True) * weight_ref[c]
-            h, l = two_terms(jnp.where(marker_hit, found, 0.0))
-            return total + dot_t(jnp.concatenate([h, l], axis=0), low_part)
-
-        sampled = lax.fori_loop(0, pairs, gather, jnp.zeros((2 * marker_rows, LANES), F32), unroll=UNROLL)
+            share = jnp.where(marker_at == m // LANES, found[c] * weight_ref[c], 0.0)
+            return total + dot_t(jnp.concatenate(two_terms(share), axis=0), one_hot(lane_at == m % LANES))
+
+        sampled = lax.fori_loop(0, chunks, add_up, jnp.zeros((2 * marker_rows, LANES), F32), unroll=8)
         sampled = jnp.concatenate(two_terms(sampled[:marker_rows] + sampled[marker_rows:]), axis=0)
 
+        def spread(c, carry):
+            m = marker_ref[c]
+            both = dot(sampled, one_hot(lane_at == m % LANES))
+            both = jnp.where(marker_at == m // LANES, both[:marker_rows] + both[marker_rows:], 0.0)
+            found[c] = jnp.sum(both, axis=0, keepdims=True) * weight_ref[c]
+            return carry
+
+        lax.fori_loop(0, chunks, spread, 0, unroll=8)
+
         def scatter(i, carry):
-            c, t, rows_hit, lanes_hit, marker_hit, low_part = entry(i)
-            spread = dot(sampled, low_part)
-            spread = spread[:marker_rows] + spread[marker_rows:]
-            spread = jnp.sum(jnp.where(marker_hit, spread, 0.0), axis=0, keepdims=True) * weight_ref[c]
-            h, l = two_terms(spread)
-            value = [jnp.where(lanes_hit, x.astype(F32), 0.0).astype(BF) for x in (h, l)]
-            both = dot_t(jnp.where(rows_hit, 1.0, 0.0).astype(BF), jnp.concatenate(value, axis=0))
+            c, t, rows_hit, lanes_hit = pair(i)
+            value = [jnp.where(lanes_hit, x.astype(F32), 0.0).astype(BF) for x in two_terms(found[c])]
+            both = dot_t(one_hot(rows_hit), jnp.concatenate(value, axis=0))
             prov[t] -= both[:, :LANES] + both[:, LANES:]
             return carry
 
@@ -404,8 +409,8 @@
         last.start()
         last.wait()
 
-    operands = [me, chunk_of, tile_of, flow, base, across, *entries, solid, *buffers]
-    specs = [SMEM] * 3 + [HBM] * 3 + [VMEM] * (len(entries) + 1) + [HBM] * total
+    operands = [me, chunk_of, tile_of, flow, base, *entries, solid, *buffers]
+    specs = [SMEM] * 3 + [HBM] * 2 + [VMEM] * (len(entries) + 1) + [HBM] * total
     aliases = {}
     if out is not None:
         aliases = {len(operands): 0}
@@ -416,12 +421,13 @@
         kernel, out_shape=jax.ShapeDtypeStruct((3, 1, rows, depth), F32), in_specs=specs, out_specs=HBM,
         input_output_aliases=aliases,
         scratch_shapes=[
-            block, block, block, pltpu.VMEM((tiles, rows, LANES), F32), pltpu.VMEM((tiles, rows, 2 * LANES), BF),
-            pltpu.SemaphoreType.DMA((3 + sum(source[2] for source in sources),)),
+            block, block, pltpu.VMEM((tiles, rows, LANES), F32), pltpu.VMEM((tiles, rows, 2 * LANES), BF),
+            pltpu.VMEM((chunks, 1, CHUNK), F32),
+            pltpu.SemaphoreType.DMA((2 + sum(source[2] for source in sources),)),
             *[pltpu.VMEM((source[1], rows, LANES), F32) for source in sources],
         ],
         compiler_params=params(),
-        cost_estimate=cost(pairs * 16 * rows * CHUNK * LANES, 20 * rows * depth), name="home_step",
+        cost_estimate=cost(pairs * 16 * rows * CHUNK * LANES, 20 * rows * depth, share), name="home_step",
     )(*operands)
 
 
@@ -468,12 +474,13 @@
     cut = [second[:middle], second[middle:]] if len(second) > 1 else [second]
     together = lax.optimization_barrier
 
-    packed = pack_lines(plan, pen_at, flow)
-    lines = send_lines(packed[0])
+    packed = pack_lines(plan, first, pen_at, flow)
+    lines = send_lines(packed)
     lines_x = exchange(cut_depth(after(flow, packed)[:, 0]))
     order = marker_order(*after((marker_cells[0, 0], marker_weights[0, 0]), packed), rows, depth)
+    packed = pack_lines(plan, second, pen_at, after(flow, order))
     lines, order, packed = together((lines, order, packed))
-    lines_2 = send_lines(packed[1])
+    lines_2 = send_lines(packed)
     (slopes,) = slopes_of(first, [first], lines)
     terms_x, slopes_x = slab_terms(compact_matrix(grps), after(lines_x, slopes))
     across = exchange(terms_x)
@@ -481,22 +488,23 @@
     back = send_lines(slopes)
     slopes = slopes_of(second, cut, lines_2)
     base, slope_z = depth_terms(after(flow, slopes), tables_z)
-    across = jnp.moveaxis(after(across, base), 0, 2).reshape(3, rows, depth)
-    back, slopes, across, base, slope_z = together((back, slopes, across, base, slope_z))
+    base = base - 0.1 * jnp.moveaxis(after(across, base), 0, 2).reshape(3, rows, depth)
+    back, slopes, base, slope_z = together((back, slopes, base, slope_z))
     groups = [(first, back)]
-    step = functools.partial(home_step, plan, me=pen_at, flow=flow, base=base, across=across, order=order, solid=solid_blocks[0])
+    step = functools.partial(home_step, plan, me=pen_at, flow=flow, base=base, order=order, solid=solid_blocks[0])
     back = send_lines(slopes[0])
-    poisson = exchange(home_divergence(plan, grps, pen_at, slope_z, groups))
     out = step(1, groups=groups, out=None)
-    slopes, back, out, poisson = together((slopes, back, out, poisson))
+    slopes, back, out = together((slopes, back, out))
     groups = groups + [(cut[0], back)]
     if len(cut) > 1:
         back = send_lines(slopes[1])
     out = step(0, groups=groups, out=out)
+    divergence = home_divergence(plan, grps, pen_at, after(slope_z, out), groups)
+    poisson = exchange(divergence)
     if len(cut) > 1:
         back, out = together((back, out))
         groups = groups + [(cut[1], back)]
-    out = step(2, groups=groups, out=out)
+    out = step(2, groups=groups, out=out, share=10.0)
     return out, poisson + slopes_x
 
 

time: 257 us -> 238 us (0.926)
  Pallas kernels: 91.3 us -> 82.3 us
  waiting for transfers between devices: 96.6 us -> 89.4 us
  starting transfers between devices: 30.9 us -> 27.8 us
  other arithmetic: 12.2 us -> 15 us
    pallas_call x3, Pallas kernels: 48 us -> 36.6 us  [home_step(): pl.pallas_call(kernel, out_shape=jax.ShapeDtypeStruct((3, 1, rows, depth)...]
    ppermute x15, waiting for transfers between devices: 95.3 us -> 87.1 us  [send_lines(): lax.ppermute(blocks[s], 'pen', [(i, (i + CORES * s) % pens) for i in rang...]
    ppermute x15, starting transfers between devices: 17 us -> 13.9 us  [send_lines(): lax.ppermute(blocks[s], 'pen', [(i, (i + CORES * s) % pens) for i in rang...]
    pallas_call x1 -> x2, Pallas kernels: 4.23 us -> 6.61 us  [pack_lines(): pl.pallas_call(kernel, out_shape=[shape] * n, in_specs=[SMEM, HBM], out_s...]
  transfers between devices with their start and end apart: 22 -> 22, of which waited for: 9 -> 12; matrix products, arithmetic and copies ran while one was open for 12% -> 13% of each run, Pallas kernels for 27% -> 33%
where the time goes in v3:
time: 238 us; the launch traced here: 237 us
  waiting for transfers between devices  89.4 us (38%)
  Pallas kernels  82.3 us (35%)
  starting transfers between devices  27.8 us (12%)
  local copies, waits for them, and re-layouts  21.3 us (9%)
  other arithmetic  15 us (6%)
    ppermute x15, waiting for transfers between devices, send_lines(): lax.ppermute(blocks[s], 'pen', [(i, (i + CORES * s) % pens) for i in rang...  87.1 us
    pallas_call x3, Pallas kernels, home_step(): pl.pallas_call(kernel, out_shape=jax.ShapeDtypeStruct((3, 1, rows, depth)...  36.6 us
    pallas_call x2, Pallas kernels, line_slopes(): pl.pallas_call(kernel, out_shape=shapes, in_specs=[SMEM, VMEM, VMEM] + [H...  20.2 us
    ppermute x15, starting transfers between devices, send_lines(): lax.ppermute(blocks[s], 'pen', [(i, (i + CORES * s) % pens) for i in rang...  13.9 us
    all_to_all x3, starting transfers between devices, exchange(): return lax.all_to_all(value, 'grp', 0, 0, tiled=True)  12.6 us
    another operation x2, local copies, waits for them, and re-layouts, cut_depth(): return jnp.moveaxis(value.reshape(*value.shape[:-1], grps, width), -2, 0)  11.2 us
    pallas_call x1, Pallas kernels, depth_terms(): pl.pallas_call(kernel, grid=(rows // step,), out_shape=[jax.ShapeDtypeStr...  10.2 us
    sort x1, other arithmetic, marker_order(): key, weight = lax.sort((place * markers + marker, weight), num_keys=1)  6.89 us
  transfers between devices with their start and end apart: 22, of which 12 were waited for; matrix products, arithmetic and copies ran while one was open for 13% of the time, Pallas kernels for 33%

profile of v3, /device:TPU:9, one launch (start us, length us, event | category | flops | bytes accessed | tf_op | source)
XLA Modules:
  0.0 236.9 jit_solution(1566883943034728453)
XLA Ops:
  0.6 3.4 %pack_lines.2 = (f32[6,192,128]{2,1,0:T(8,128)}, f32[6,192,128]{2,1,0:T(8,128)}, f32[6,192,128]{2,1,0:T(8,128)}, f32[6,192,128]{2,1,0:T(8,128)}) custom-call(s32[1]{0:T(128)} %bitcast.me_ref, f32[4,1,192,1536]{3,2,1,0:T(8,128)} %flow_ref.9), custom_call_target="tpu_custom_call" | custom-call | bytes 23592 | tf_op jit(solution)/shard_map/pack_lines/pallas_call | solution.py:114
  7.8 6.2 %reshape_squeeze.3 = f32[4,192,4,384]{3,2,1,0:T(4,128)} reshape(f32[4,1,192,1536]{3,2,1,0:T(8,128)} %flow_ref.9) | data formatting | bytes 9437184 | tf_op jit(solution)/shard_map/reshape;squeeze | solution.py:464
  14.0 5.0 %copy.36 = f32[4,192,4,384]{3,1,0,2:T(8,128)} copy(f32[4,192,4,384]{3,2,1,0:T(4,128)} %reshape_squeeze.3) | data formatting | bytes 9437184 | tf_op jit(solution)/shard_map/reshape;squeeze | solution.py:464
  19.0 5.1 %all-to-all-start = ((f32[4,4,192,384]{3,2,1,0:T(8,128)}), f32[4,4,192,384]{3,2,1,0:T(8,128)}, u32[]{:S(2)}, u32[]{:S(2)}) async-start(f32[4,4,192,384]{3,2,1,0:T(8,128)} %bitcast.18), calls=%async_computation | async-start | bytes 9437184 | tf_op jit(solution)/shard_map/all_to_all | solution.py:467
  26.2 6.9 %sort.23 = (s32[8192]{0:T(1024)S(1)}, f32[8192]{0:T(1024)}, s32[8192]{0:T(1024)}) sort(s32[8192]{0:T(1024)S(1)} %fusion.5, f32[8192]{0:T(1024)S(1)} %reshape.61, s32[8192]{0:T(1024)S(1)} %iota.19), dimensions={0}, to_apply=%region_0.1 | sort | flops 106496 | bytes 196608 | tf_op jit(solution)/shard_map/sort | solution.py:257
  36.1 3.2 %pack_lines.3 = (f32[6,192,128]{2,1,0:T(8,128)}, f32[6,192,128]{2,1,0:T(8,128)}, f32[6,192,128]{2,1,0:T(8,128)}, f32[6,192,128]{2,1,0:T(8,128)}) custom-call(s32[1]{0:T(128)} %bitcast.me_ref, f32[4,1,192,1536]{3,2,1,0:T(8,128)} %flow_ref.9), custom_call_target="tpu_custom_call" | custom-call | bytes 23592 | tf_op jit(solution)/shard_map/pack_lines/pallas_call | solution.py:114
  39.4 16.2 %collective-permute-done.1.rest_2_ = f32[6,192,128]{2,1,0:T(8,128)S(1)} collective-permute-done((f32[6,192,128]{2,1,0:T(8,128)}, f32[6,192,128]{2,1,0:T(8,128)S(1)}, u32[]{:S(2)}, u32[]{:S(2)}) %collective-permute-start.1) | collective-permute-done | bytes 589856 | tf_op jit(solution)/shard_map/ppermute | solution.py:453
  55.6 2.8 %collective-permute-done.2.rest_3_ = f32[6,192,128]{2,1,0:T(8,128)S(1)} collective-permute-done((f32[6,192,128]{2,1,0:T(8,128)}, f32[6,192,128]{2,1,0:T(8,128)S(1)}, u32[]{:S(2)}, u32[]{:S(2)}) %collective-permute-start.2) | collective-permute-done | bytes 589856 | tf_op jit(solution)/shard_map/ppermute | solution.py:453
  60.1 1.5 collective-permute-start.4
  61.6 1.5 collective-permute-start.5
  65.2 10.1 %line_slopes.2 = (f32[6,192,128]{2,1,0:T(8,128)}, f32[6,192,128]{2,1,0:T(8,128)}, f32[6,192,128]{2,1,0:T(8,128)}, f32[6,192,128]{2,1,0:T(8,128)}) custom-call(s32[1]{0:T(128)} %bitcast.me_ref, bf16[2,768,768]{2,1,0:T(8,128)(2,1)} %constant.112.clone.high_ref, bf16[2,768,768]{2,1,0:T(8,128)(2,1)} %constant.113.clone.low_ref, ...), custom_call_target="tpu_custom_call" | custom-call | flops 27179088 | bytes 117964 | tf_op jit(solution)/shard_map/line_slopes/pallas_call | solution.py:174
  76.6 5.7 %slab_terms.1 = (f32[4,3,192,384]{3,2,1,0:T(8,128)}, f32[4,192,384]{2,1,0:T(8,128)}) custom-call(f32[4,4,192,384]{3,2,1,0:T(8,128)} %all-to-all-done.in_ref), custom_call_target="tpu_custom_call" | custom-call | flops 188743 | bytes 94371 | tf_op jit(solution)/shard_map/slab_terms/pallas_call | solution.py:239
  82.3 3.7 %all-to-all-start.1 = ((f32[4,3,192,384]{3,2,1,0:T(8,128)}), f32[4,3,192,384]{3,2,1,0:T(8,128)S(1)}, u32[]{:S(2)}, u32[]{:S(2)}) async-start(f32[4,3,192,384]{3,2,1,0:T(8,128)} %get-tuple-element.137), calls=%async_computation.1 | async-start | bytes 7077888 | tf_op jit(solution)/shard_map/all_to_all | solution.py:467
  86.1 25.1 %collective-permute-done.4.rest_2_ = f32[6,192,128]{2,1,0:T(8,128)} collective-permute-done((f32[6,192,128]{2,1,0:T(8,128)}, f32[6,192,128]{2,1,0:T(8,128)}, u32[]{:S(2)}, u32[]{:S(2)}) %collective-permute-start.4) | collective-permute-done | bytes 589856 | tf_op jit(solution)/shard_map/ppermute | solution.py:453
  111.2 2.5 %collective-permute-done.5.rest_3_ = f32[6,192,128]{2,1,0:T(8,128)} collective-permute-done((f32[6,192,128]{2,1,0:T(8,128)}, f32[6,192,128]{2,1,0:T(8,128)}, u32[]{:S(2)}, u32[]{:S(2)}) %collective-permute-start.5) | collective-permute-done | bytes 589856 | tf_op jit(solution)/shard_map/ppermute | solution.py:453
  113.7 1.6 pad_maximum_fusion.1
  116.8 1.5 collective-permute-start.10
  121.3 10.1 %line_slopes.3 = (f32[3,192,128]{2,1,0:T(8,128)}, f32[3,192,128]{2,1,0:T(8,128)}, f32[3,192,128]{2,1,0:T(8,128)}, f32[3,192,128]{2,1,0:T(8,128)}, f32[3,192,128]...) custom-call(s32[1]{0:T(128)} %bitcast.me_ref, ...), custom_call_target="tpu_custom_call" | custom-call | flops 27179088 | bytes 117964 | tf_op jit(solution)/shard_map/line_slopes/pallas_call | solution.py:174
  131.4 10.2 %depth_terms.1 = (f32[3,192,1536]{2,1,0:T(8,128)}, f32[192,1536]{1,0:T(8,128)}) custom-call(f32[4,1,192,1536]{3,2,1,0:T(8,128)} %flow_ref.9, bf16[2,768,768]{2,1,0:T(8,128)(2,1)} %constant.112.clone.high_ref, bf16[2,768,768]{2,1,0:T(8,128)(2,1)} %constant.113.clone.low_ref), custom_call_target="tpu_custom_call" | custom-call | flops 54358180 | bytes 141557 | tf_op jit(solution)/shard_map/depth_terms/pallas_call | solution.py:212
  142.4 1.5 copy-done
  143.9 2.4 %sub.64.base_ref = f32[3,192,1536]{2,1,0:T(8,128)} subtract(f32[3,192,1536]{2,1,0:T(8,128)S(1)} %copy-done, f32[3,192,1536]{2,1,0:T(8,128)S(1)} %bitcast.19) | non-fusion elementwise | flops 884736 | bytes 10616832 | tf_op jit(solution)/shard_map/sub | solution.py:491
  146.4 20.4 %collective-permute-done.9.rest_2_.rest_6_ = f32[6,192,128]{2,1,0:T(8,128)} collective-permute-done((f32[6,192,128]{2,1,0:T(8,128)}, f32[6,192,128]{2,1,0:T(8,128)}, u32[]{:S(2)}, u32[]{:S(2)}) %collective-permute-start.9) | collective-permute-done | bytes 589856 | tf_op jit(solution)/shard_map/ppermute | solution.py:453
  166.8 2.0 collective-permute-done.10.rest_3_.rest_7_
  172.1 12.6 %home_step.3.rest_4_ = f32[3,1,192,1536]{3,2,1,0:T(8,128)} custom-call(s32[1]{0:T(128)} %bitcast.me_ref, s32[44]{0:T(128)} %copy-done.15, s32[44]{0:T(128)} %compare_select_fusion.tile_ref, f32[4,1,192,1536]{3,2,1,0:T(8,128)} %flow_ref.9, f32[3,192,1536]{2,1,0:T(8,128)} %sub.64.base_ref, s32[32,1,256]{2,1,0:T(1,128)} %bitcast.29, s32[32,1,256]{2,1,0:T(1,128)} %bitcast.26, ...), custom_call_target="tpu_custom_call" | custom-call | flops 44291848 | bytes 58982 | tf_op jit(solution)/shard_map/home_step/pallas_call | solution.py:420
  184.7 9.3 %collective-permute-done.14.rest_2_ = f32[3,192,128]{2,1,0:T(8,128)S(1)} collective-permute-done((f32[3,192,128]{2,1,0:T(8,128)S(1)}, f32[3,192,128]{2,1,0:T(8,128)S(1)}, u32[]{:S(2)}, u32[]{:S(2)}) %collective-permute-start.14) | collective-permute-done | bytes 294944 | tf_op jit(solution)/shard_map/ppermute | solution.py:453
  194.0 2.4 %collective-permute-done.15.rest_3_ = f32[3,192,128]{2,1,0:T(8,128)S(1)} collective-permute-done((f32[3,192,128]{2,1,0:T(8,128)S(1)}, f32[3,192,128]{2,1,0:T(8,128)S(1)}, u32[]{:S(2)}, u32[]{:S(2)}) %collective-permute-start.15) | collective-permute-done | bytes 294944 | tf_op jit(solution)/shard_map/ppermute | solution.py:453
  198.6 12.0 %home_step.4.rest_4_ = f32[3,1,192,1536]{3,2,1,0:T(8,128)} custom-call(s32[1]{0:T(128)} %bitcast.me_ref, s32[44]{0:T(128)} %copy-done.15, s32[44]{0:T(128)} %compare_select_fusion.tile_ref, f32[4,1,192,1536]{3,2,1,0:T(8,128)} %flow_ref.9, f32[3,192,1536]{2,1,0:T(8,128)} %sub.64.base_ref, s32[32,1,256]{2,1,0:T(1,128)} %bitcast.30, ...), custom_call_target="tpu_custom_call", output_to_operand_aliasing={{}: (14, {})} | custom-call | flops 44291848 | bytes 58982 | tf_op jit(solution)/shard_map/home_step/pallas_call | solution.py:420
  210.7 2.9 %home_divergence.1 = f32[4,192,384]{2,1,0:T(8,128)} custom-call(s32[1]{0:T(128)} %bitcast.me_ref, f32[192,1536]{1,0:T(8,128)} %get-tuple-element.172.slope_ref, f32[6,192,128]{2,1,0:T(8,128)} %get-tuple-element.153.rest_0_.rest_4_, f32[6,192,128]{2,1,0:T(8,128)} %collective-permute-done.8.rest_1_.rest_5_, ...), custom_call_target="tpu_custom_call" | custom-call | bytes 35389 | tf_op jit(solution)/shard_map/home_divergence/pallas_call | solution.py:308
  213.6 3.8 %all-to-all-start.2 = ((f32[4,192,384]{2,1,0:T(8,128)}), f32[4,192,384]{2,1,0:T(8,128)S(1)}, u32[]{:S(2)}, u32[]{:S(2)}) async-start(f32[4,192,384]{2,1,0:T(8,128)} %home_divergence.1), calls=%async_computation.2 | async-start | bytes 2359296 | tf_op jit(solution)/shard_map/all_to_all | solution.py:467
  217.4 4.1 %collective-permute-done.17.rest_2_ = f32[3,192,128]{2,1,0:T(8,128)} collective-permute-done((f32[3,192,128]{2,1,0:T(8,128)S(1)}, f32[3,192,128]{2,1,0:T(8,128)}, u32[]{:S(2)}, u32[]{:S(2)}) %collective-permute-start.17) | collective-permute-done | bytes 294944 | tf_op jit(solution)/shard_map/ppermute | solution.py:453
  221.5 2.2 collective-permute-done.18.rest_3_
  223.7 12.0 %home_step.5 = f32[3,1,192,1536]{3,2,1,0:T(8,128)} custom-call(s32[1]{0:T(128)} %bitcast.me_ref, s32[44]{0:T(128)} %copy-done.15, s32[44]{0:T(128)} %compare_select_fusion.tile_ref, f32[4,1,192,1536]{3,2,1,0:T(8,128)} %flow_ref.9, f32[3,192,1536]{2,1,0:T(8,128)} %sub.64.base_ref, s32[32,1,256]{2,1,0:T(1,128)} %bitcast.31, ...), custom_call_target="tpu_custom_call", output_to_operand_aliasing={{}: (14, {})} | custom-call | flops 44291850240 | bytes 58982400 | tf_op jit(solution)/shard_map/home_step/pallas_call | solution.py:420
  (103 shorter events, 25.8 us)
Async XLA Ops:
  4.0 35.3 %collective-permute-start = (f32[6,192,128]{2,1,0:T(8,128)}, f32[6,192,128]{2,1,0:T(8,128)S(1)}, u32[]{:S(2)}, u32[]{:S(2)}) collective-permute-start(f32[6,192,128]{2,1,0:T(8,128)} %get-tuple-element.90), channel_id=1, source_target_pairs={{0,2},{1,3},{2,4},{3,5},{4,6},{5,7},{6,0},{7,1},{8,10},{9,11},{10,... | collective-permute-start | bytes 1769480 | tf_op jit(solution)/shard_map/ppermute | solution.py:453
  5.4 50.2 %collective-permute-start.1 = (f32[6,192,128]{2,1,0:T(8,128)}, f32[6,192,128]{2,1,0:T(8,128)S(1)}, u32[]{:S(2)}, u32[]{:S(2)}) collective-permute-start(f32[6,192,128]{2,1,0:T(8,128)} %get-tuple-element.91), channel_id=1, source_target_pairs={{0,4},{1,5},{2,6},{3,7},{4,0},{5,1},{6,2},{7,3},{8,12},{9,13},{10,... | collective-permute-start | bytes 1769480 | tf_op jit(solution)/shard_map/ppermute | solution.py:453
  6.4 52.0 %collective-permute-start.2 = (f32[6,192,128]{2,1,0:T(8,128)}, f32[6,192,128]{2,1,0:T(8,128)S(1)}, u32[]{:S(2)}, u32[]{:S(2)}) collective-permute-start(f32[6,192,128]{2,1,0:T(8,128)} %get-tuple-element.92), channel_id=1, source_target_pairs={{0,6},{1,7},{2,0},{3,1},{4,2},{5,3},{6,4},{7,5},{8,14},{9,15},{10,... | collective-permute-start | bytes 1769480 | tf_op jit(solution)/shard_map/ppermute | solution.py:453
  19.0 57.5 %all-to-all-start = ((f32[4,4,192,384]{3,2,1,0:T(8,128)}), f32[4,4,192,384]{3,2,1,0:T(8,128)}, u32[]{:S(2)}, u32[]{:S(2)}) async-start(f32[4,4,192,384]{3,2,1,0:T(8,128)} %bitcast.18), calls=%async_computation | async-start | bytes 9437184 | tf_op jit(solution)/shard_map/all_to_all | solution.py:467
  39.4 19.2 %copy-start.1 = (f32[6,192,128]{2,1,0:T(8,128)}, f32[6,192,128]{2,1,0:T(8,128)S(1)}, u32[]{:S(2)}) copy-start(f32[6,192,128]{2,1,0:T(8,128)S(1)} %collective-permute-done.rest_1_) | copy-start | bytes 1769476
  59.3 3.8 %collective-permute-start.7 = (f32[18,192,128]{2,1,0:T(8,128)S(1)}, f32[18,192,128]{2,1,0:T(8,128)S(1)}, u32[]{:S(2)}, u32[]{:S(2)}) collective-permute-start(f32[18,192,128]{2,1,0:T(8,128)S(1)} %pad_maximum_fusion), channel_id=1, source_target_pairs={{0,1},{1,0},{2,3},{3,2},{4,5},{5,4},{6,7},{7,6},{8,9},{9,8},{10,11... | collective-permute-start | bytes 5308424 | tf_op jit(solution)/shard_map/ppermute | solution.py:458
  59.7 4.6 %collective-permute-start.6 = (f32[6,192,128]{2,1,0:T(8,128)S(1)}, f32[6,192,128]{2,1,0:T(8,128)S(1)}, u32[]{:S(2)}, u32[]{:S(2)}) collective-permute-start(f32[6,192,128]{2,1,0:T(8,128)S(1)} %copy-done.5), channel_id=1, source_target_pairs={{0,1},{1,0},{2,3},{3,2},{4,5},{5,4},{6,7},{7,6},{8,9},{9,8},{10,11... | collective-permute-start | bytes 1769480 | tf_op jit(solution)/shard_map/ppermute | solution.py:458
  60.1 26.0 %collective-permute-start.3 = (f32[6,192,128]{2,1,0:T(8,128)}, f32[6,192,128]{2,1,0:T(8,128)}, u32[]{:S(2)}, u32[]{:S(2)}) collective-permute-start(f32[6,192,128]{2,1,0:T(8,128)} %get-tuple-element.105), channel_id=1, source_target_pairs={{0,2},{1,3},{2,4},{3,5},{4,6},{5,7},{6,0},{7,1},{8,10},{9,11},{10,... | collective-permute-start | bytes 1769480 | tf_op jit(solution)/shard_map/ppermute | solution.py:453
  60.1 51.1 %collective-permute-start.4 = (f32[6,192,128]{2,1,0:T(8,128)}, f32[6,192,128]{2,1,0:T(8,128)}, u32[]{:S(2)}, u32[]{:S(2)}) collective-permute-start(f32[6,192,128]{2,1,0:T(8,128)} %get-tuple-element.106), channel_id=1, source_target_pairs={{0,4},{1,5},{2,6},{3,7},{4,0},{5,1},{6,2},{7,3},{8,12},{9,13},{10,... | collective-permute-start | bytes 1769480 | tf_op jit(solution)/shard_map/ppermute | solution.py:453
  61.6 52.1 %collective-permute-start.5 = (f32[6,192,128]{2,1,0:T(8,128)}, f32[6,192,128]{2,1,0:T(8,128)}, u32[]{:S(2)}, u32[]{:S(2)}) collective-permute-start(f32[6,192,128]{2,1,0:T(8,128)} %get-tuple-element.107), channel_id=1, source_target_pairs={{0,6},{1,7},{2,0},{3,1},{4,2},{5,3},{6,4},{7,5},{8,14},{9,15},{10,... | collective-permute-start | bytes 1769480 | tf_op jit(solution)/shard_map/ppermute | solution.py:453
  82.3 59.3 %all-to-all-start.1 = ((f32[4,3,192,384]{3,2,1,0:T(8,128)}), f32[4,3,192,384]{3,2,1,0:T(8,128)S(1)}, u32[]{:S(2)}, u32[]{:S(2)}) async-start(f32[4,3,192,384]{3,2,1,0:T(8,128)} %get-tuple-element.137), calls=%async_computation.1 | async-start | bytes 7077888 | tf_op jit(solution)/shard_map/all_to_all | solution.py:467
  115.3 3.9 %collective-permute-start.12 = (f32[18,192,128]{2,1,0:T(8,128)S(1)}, f32[18,192,128]{2,1,0:T(8,128)S(1)}, u32[]{:S(2)}, u32[]{:S(2)}) collective-permute-start(f32[18,192,128]{2,1,0:T(8,128)S(1)} %pad_maximum_fusion.1), channel_id=1, source_target_pairs={{0,1},{1,0},{2,3},{3,2},{4,5},{5,4},{6,7},{7,6},{8,9},{9,8},{10,11... | collective-permute-start | bytes 5308424 | tf_op jit(solution)/shard_map/ppermute | solution.py:458
  115.9 4.6 %collective-permute-start.11 = (f32[6,192,128]{2,1,0:T(8,128)S(1)}, f32[6,192,128]{2,1,0:T(8,128)S(1)}, u32[]{:S(2)}, u32[]{:S(2)}) collective-permute-start(f32[6,192,128]{2,1,0:T(8,128)S(1)} %copy-done.6), channel_id=1, source_target_pairs={{0,1},{1,0},{2,3},{3,2},{4,5},{5,4},{6,7},{7,6},{8,9},{9,8},{10,11... | collective-permute-start | bytes 1769480 | tf_op jit(solution)/shard_map/ppermute | solution.py:458
  115.9 30.4 %collective-permute-start.8 = (f32[6,192,128]{2,1,0:T(8,128)}, f32[6,192,128]{2,1,0:T(8,128)}, u32[]{:S(2)}, u32[]{:S(2)}) collective-permute-start(f32[6,192,128]{2,1,0:T(8,128)} %get-tuple-element.120), channel_id=1, source_target_pairs={{0,2},{1,3},{2,4},{3,5},{4,6},{5,7},{6,0},{7,1},{8,10},{9,11},{10,... | collective-permute-start | bytes 1769480 | tf_op jit(solution)/shard_map/ppermute | solution.py:453
  115.9 50.8 %collective-permute-start.9 = (f32[6,192,128]{2,1,0:T(8,128)}, f32[6,192,128]{2,1,0:T(8,128)}, u32[]{:S(2)}, u32[]{:S(2)}) collective-permute-start(f32[6,192,128]{2,1,0:T(8,128)} %get-tuple-element.121), channel_id=1, source_target_pairs={{0,4},{1,5},{2,6},{3,7},{4,0},{5,1},{6,2},{7,3},{8,12},{9,13},{10,... | collective-permute-start | bytes 1769480 | tf_op jit(solution)/shard_map/ppermute | solution.py:453
  116.8 52.1 %collective-permute-start.10 = (f32[6,192,128]{2,1,0:T(8,128)}, f32[6,192,128]{2,1,0:T(8,128)}, u32[]{:S(2)}, u32[]{:S(2)}) collective-permute-start(f32[6,192,128]{2,1,0:T(8,128)} %get-tuple-element.122), channel_id=1, source_target_pairs={{0,6},{1,7},{2,0},{3,1},{4,2},{5,3},{6,4},{7,5},{8,14},{9,15},{10,... | collective-permute-start | bytes 1769480 | tf_op jit(solution)/shard_map/ppermute | solution.py:453
  143.9 24.9 %copy-start.21 = (f32[3,192,128]{2,1,0:T(8,128)S(1)}, f32[3,192,128]{2,1,0:T(8,128)}, u32[]{:S(2)}) copy-start(f32[3,192,128]{2,1,0:T(8,128)} %get-tuple-element.145) | copy-start | bytes 884740
  143.9 24.9 %copy-start.20 = (f32[3,192,128]{2,1,0:T(8,128)S(1)}, f32[3,192,128]{2,1,0:T(8,128)}, u32[]{:S(2)}) copy-start(f32[3,192,128]{2,1,0:T(8,128)} %get-tuple-element.146) | copy-start | bytes 884740
  143.9 26.0 %copy-start.19 = (f32[3,192,128]{2,1,0:T(8,128)S(1)}, f32[3,192,128]{2,1,0:T(8,128)}, u32[]{:S(2)}) copy-start(f32[3,192,128]{2,1,0:T(8,128)} %get-tuple-element.147) | copy-start | bytes 884740
  143.9 27.4 %copy-start.14 = (s32[1,192,12]{1,0,2:T(1,128)S(1)}, s32[1,192,12]{1,0,2:T(1,128)}, u32[]{:S(2)}) copy-start(s32[1,192,12]{1,0,2:T(1,128)} %param.9) | copy-start | bytes 27652
  168.8 15.9 %collective-permute-start.13 = (f32[3,192,128]{2,1,0:T(8,128)S(1)}, f32[3,192,128]{2,1,0:T(8,128)S(1)}, u32[]{:S(2)}, u32[]{:S(2)}) collective-permute-start(f32[3,192,128]{2,1,0:T(8,128)S(1)} %copy-done.21), channel_id=1, source_target_pairs={{0,2},{1,3},{2,4},{3,5},{4,6},{5,7},{6,0},{7,1},{8,10},{9,11},{10,... | collective-permute-start | bytes 884744 | tf_op jit(solution)/shard_map/ppermute | solution.py:453
  168.8 25.2 %collective-permute-start.14 = (f32[3,192,128]{2,1,0:T(8,128)S(1)}, f32[3,192,128]{2,1,0:T(8,128)S(1)}, u32[]{:S(2)}, u32[]{:S(2)}) collective-permute-start(f32[3,192,128]{2,1,0:T(8,128)S(1)} %copy-done.20), channel_id=1, source_target_pairs={{0,4},{1,5},{2,6},{3,7},{4,0},{5,1},{6,2},{7,3},{8,12},{9,13},{10,... | collective-permute-start | bytes 884744 | tf_op jit(solution)/shard_map/ppermute | solution.py:453
  170.0 26.4 %collective-permute-start.15 = (f32[3,192,128]{2,1,0:T(8,128)S(1)}, f32[3,192,128]{2,1,0:T(8,128)S(1)}, u32[]{:S(2)}, u32[]{:S(2)}) collective-permute-start(f32[3,192,128]{2,1,0:T(8,128)S(1)} %copy-done.19), channel_id=1, source_target_pairs={{0,6},{1,7},{2,0},{3,1},{4,2},{5,3},{6,4},{7,5},{8,14},{9,15},{10,... | collective-permute-start | bytes 884744 | tf_op jit(solution)/shard_map/ppermute | solution.py:453
  172.1 24.3 %copy-start.18 = (f32[3,192,128]{2,1,0:T(8,128)S(1)}, f32[3,192,128]{2,1,0:T(8,128)}, u32[]{:S(2)}) copy-start(f32[3,192,128]{2,1,0:T(8,128)} %get-tuple-element.158) | copy-start | bytes 884740
  172.1 24.3 %copy-start.17 = (f32[3,192,128]{2,1,0:T(8,128)S(1)}, f32[3,192,128]{2,1,0:T(8,128)}, u32[]{:S(2)}) copy-start(f32[3,192,128]{2,1,0:T(8,128)} %get-tuple-element.159) | copy-start | bytes 884740
  172.1 25.1 %copy-start.16 = (f32[3,192,128]{2,1,0:T(8,128)S(1)}, f32[3,192,128]{2,1,0:T(8,128)}, u32[]{:S(2)}) copy-start(f32[3,192,128]{2,1,0:T(8,128)} %get-tuple-element.160) | copy-start | bytes 884740
  184.7 13.9 %copy-start.9 = (f32[3,192,128]{2,1,0:T(8,128)}, f32[3,192,128]{2,1,0:T(8,128)S(1)}, u32[]{:S(2)}) copy-start(f32[3,192,128]{2,1,0:T(8,128)S(1)} %collective-permute-done.13.rest_1_) | copy-start | bytes 884740
  196.4 21.0 %collective-permute-start.16 = (f32[3,192,128]{2,1,0:T(8,128)S(1)}, f32[3,192,128]{2,1,0:T(8,128)S(1)}, u32[]{:S(2)}, u32[]{:S(2)}) collective-permute-start(f32[3,192,128]{2,1,0:T(8,128)S(1)} %copy-done.18), channel_id=1, source_target_pairs={{0,2},{1,3},{2,4},{3,5},{4,6},{5,7},{6,0},{7,1},{8,10},{9,11},{10,... | collective-permute-start | bytes 884744 | tf_op jit(solution)/shard_map/ppermute | solution.py:453
  196.4 25.2 %collective-permute-start.17 = (f32[3,192,128]{2,1,0:T(8,128)S(1)}, f32[3,192,128]{2,1,0:T(8,128)}, u32[]{:S(2)}, u32[]{:S(2)}) collective-permute-start(f32[3,192,128]{2,1,0:T(8,128)S(1)} %copy-done.17), channel_id=1, source_target_pairs={{0,4},{1,5},{2,6},{3,7},{4,0},{5,1},{6,2},{7,3},{8,12},{9,13},{10,... | collective-permute-start | bytes 884744 | tf_op jit(solution)/shard_map/ppermute | solution.py:453
  197.2 26.5 %collective-permute-start.18 = (f32[3,192,128]{2,1,0:T(8,128)S(1)}, f32[3,192,128]{2,1,0:T(8,128)}, u32[]{:S(2)}, u32[]{:S(2)}) collective-permute-start(f32[3,192,128]{2,1,0:T(8,128)S(1)} %copy-done.16), channel_id=1, source_target_pairs={{0,6},{1,7},{2,0},{3,1},{4,2},{5,3},{6,4},{7,5},{8,14},{9,15},{10,... | collective-permute-start | bytes 884744 | tf_op jit(solution)/shard_map/ppermute | solution.py:453
  213.6 22.2 %all-to-all-start.2 = ((f32[4,192,384]{2,1,0:T(8,128)}), f32[4,192,384]{2,1,0:T(8,128)S(1)}, u32[]{:S(2)}, u32[]{:S(2)}) async-start(f32[4,192,384]{2,1,0:T(8,128)} %home_divergence.1), calls=%async_computation.2 | async-start | bytes 2359296 | tf_op jit(solution)/shard_map/all_to_all | solution.py:467
  217.4 18.4 %copy-start.4 = (f32[4,192,384]{2,1,0:T(8,128)S(1)}, f32[4,192,384]{2,1,0:T(8,128)}, u32[]{:S(2)}) copy-start(f32[4,192,384]{2,1,0:T(8,128)} %get-tuple-element.173) | copy-start | bytes 3538948
  (13 other events, 35.9 us)

commit v4 on v3

--- a/solution.py
+++ b/solution.py
@@ -13,7 +13,7 @@
 LANES = 128
 CHUNK = 256
 CORES = 2
-UNROLL = 11
+UNROLL = 22
 FIELD_ORDER = (1, 3, 0, 2)
 ANY = pl.BlockSpec(memory_space=pl.ANY)
 HBM = pl.BlockSpec(memory_space=pltpu.HBM)
@@ -77,14 +77,6 @@
         if first < self.rounds:
             self.stages.append(list(range(first, self.rounds)))
 
-    def place(self, round_, chip):
-        pair = jnp.minimum(round_ * self.chips + chip, self.pairs - 1)
-        slot, tile = pair // self.tiles, pair % self.tiles
-        field = jnp.int32(FIELD_ORDER[0])
-        for i, f in enumerate(FIELD_ORDER[1:], 1):
-            field = jnp.where(slot == i, f, field)
-        return field, pl.multiple_of(tile * LANES, LANES)
-
 
 def run_copies(copies):
     for c in copies:
@@ -94,26 +86,31 @@
 
 
 def pack_lines(plan, rounds, me, flow):
-    n = plan.chips
-    fields, _, rows, depth = flow.shape
-    used = FIELD_ORDER[rounds[0] * n // plan.tiles : min((rounds[-1] * n + n - 1) // plan.tiles, fields - 1) + 1]
+    n, rows, tiles = plan.chips, plan.rows, plan.tiles
+    start, end = rounds[0] * n, min((rounds[-1] + 1) * n, plan.pairs)
 
     def kernel(me_ref, flow_ref, *rest):
         outs, (held, in_sems, out_sems) = rest[:-3], rest[-3:]
-        run_copies([pltpu.make_async_copy(flow_ref.at[f, 0], held.at[f], in_sems.at[f]) for f in used])
+        loads = [pltpu.make_async_copy(
+            flow_ref.at[FIELD_ORDER[q // tiles], 0, :, pl.ds(q % tiles * LANES, LANES)], held.at[q - start],
+            in_sems.at[q - start]) for q in range(start, end)]
+        for c in loads:
+            c.start()
         copies = []
-        for s in range(n):
-            chip = lax.rem(me_ref[0] // CORES + s, n)
-            for k, r in enumerate(rounds):
-                field, z = plan.place(r, chip)
-                copies.append(pltpu.make_async_copy(
-                    held.at[field, :, pl.ds(z, LANES)], outs[s].at[k], out_sems.at[len(copies)]))
-        run_copies(copies)
+        for k in range(len(rounds)):
+            for c in loads[k * n : (k + 1) * n]:
+                c.wait()
+            for s in range(n):
+                pair = jnp.minimum(k * n + lax.rem(me_ref[0] // CORES + s, n), end - start - 1)
+                copies.append(pltpu.make_async_copy(held.at[pair], outs[s].at[k], out_sems.at[len(copies)]))
+                copies[-1].start()
+        for c in copies:
+            c.wait()
 
     shape = jax.ShapeDtypeStruct((len(rounds), rows, LANES), F32)
     return pl.pallas_call(
         kernel, out_shape=[shape] * n, in_specs=[SMEM, HBM], out_specs=[HBM] * n,
-        scratch_shapes=[pltpu.VMEM((fields, rows, depth), F32), pltpu.SemaphoreType.DMA((fields,)),
+        scratch_shapes=[pltpu.VMEM((end - start, rows, LANES), F32), pltpu.SemaphoreType.DMA((end - start,)),
                         pltpu.SemaphoreType.DMA((n * len(rounds),))],
         compiler_params=params(), cost_estimate=cost(0, 2 * flow.size), name="pack_lines",
     )(me, flow)
@@ -283,20 +280,22 @@
             buffers += blocks
 
     def copies(me, refs, slopes, sems, first):
-        return [pltpu.make_async_copy(
-            refs[b].at[k], slopes.at[(r - low) * n + lax.rem(me // CORES + n - s, n)], sems.at[first + i])
+        return [(r, pltpu.make_async_copy(
+            refs[b].at[k], slopes.at[(r - low) * n + lax.rem(me // CORES + n - s, n)], sems.at[first + i]))
             for i, (b, k, r, s) in enumerate(wanted)]
 
-    return buffers, (high - low + 1) * n, len(wanted), slot * tiles - low * n, copies
+    skip = slot * tiles - low * n
+    spans = [(r, max(0, (r - low) * n - skip), min(tiles, (r - low + 1) * n - skip)) for r in range(low, high + 1)]
+    return buffers, (high - low + 1) * n, len(wanted), skip, copies, spans
 
 
 def home_divergence(plan, parts, me, slope_z, groups):
     rows, depth, tiles = plan.rows, plan.depth, plan.tiles
-    buffers, span, count, skip, copies_of = home_slopes(plan, FIELD_ORDER.index(1), groups)
+    buffers, span, count, skip, copies_of, _ = home_slopes(plan, FIELD_ORDER.index(1), groups)
 
     def kernel(me_ref, slope_ref, *rest):
         refs, (out_ref, slopes, third, sems) = rest[: len(buffers)], rest[len(buffers) :]
-        copies = copies_of(me_ref[0], refs, slopes, sems, 1)
+        copies = [c for _, c in copies_of(me_ref[0], refs, slopes, sems, 1)]
         run_copies([pltpu.make_async_copy(slope_ref, third, sems.at[0])] + copies)
         for t in range(tiles):
             z = slice(t * LANES, (t + 1) * LANES)
@@ -324,53 +323,67 @@
     pairs = chunk_of.shape[0]
     chunks = entries[0].shape[0]
     marker_rows = plan.marker_rows
-
-    def kernel(me_ref, chunk_ref, tile_ref, flow_ref, base_ref, row_ref, lane_ref, marker_ref,
-               weight_ref, solid_ref, *rest):
-        bufs = rest[:total]
-        rest = rest[total:]
+    assert rows <= 256
+
+    spans = sources[0][5]
+
+    def kernel(me_ref, chunk_ref, tile_ref, flow_ref, base_ref, *rest):
+        early, bufs, rest = rest[:5], rest[5 : 5 + total], rest[5 + total :]
         if out is not None:
             rest = rest[1:]
-        out_ref, speed, value, prov, terms, found, sems, *slopes = rest
-        copies = [
-            pltpu.make_async_copy(flow_ref.at[1, 0], speed, sems.at[0]),
-            pltpu.make_async_copy(base_ref.at[component], value, sems.at[1]),
-        ]
-        used = 0
-        for (held, _, count, _, copies_of), ref in zip(sources, slopes):
-            copies += copies_of(me_ref[0], bufs[used : used + len(held)], ref, sems, len(copies))
-            used += len(held)
-        run_copies(copies)
-        for t in range(tiles):
-            z = slice(t * LANES, (t + 1) * LANES)
-            term = speed[:, z] * slopes[0][sources[0][3] + t]
-            if component == 1:
-                term = term + slopes[1][sources[1][3] + t]
-            result = value[:, z] - 0.1 * term
-            prov[t] = result
-            h, l = two_terms(result)
-            terms[t, :, :LANES] = h
-            terms[t, :, LANES:] = l
+        out_ref, speed, value, prov, terms, found, row_ref, lane_ref, marker_ref, weight_ref, solid_ref, sems, *slopes = rest
+        first = {span[0]: [] for span in spans}
+        for r, start, end in spans:
+            z = pl.ds(start * LANES, (end - start) * LANES)
+            for src, dst in ((flow_ref.at[1, 0], speed), (base_ref.at[component], value)):
+                at = sum(len(cs) for cs in first.values())
+                first[r].append(pltpu.make_async_copy(src.at[:, z], dst.at[:, z], sems.at[at]))
+        at, used = 2 * len(spans), 0
+        for source, ref in zip(sources, slopes):
+            for r, c in source[4](me_ref[0], bufs[used : used + len(source[0])], ref, sems, at):
+                first[r if source is sources[0] else spans[0][0]].append(c)
+            at += source[2]
+            used += len(source[0])
+        later = [pltpu.make_async_copy(src, dst, sems.at[at + i]) for i, (src, dst) in enumerate(zip(
+            early, (row_ref, lane_ref, marker_ref, weight_ref, solid_ref)))]
+        for c in [c for cs in first.values() for c in cs] + later:
+            c.start()
+        for r, start, end in spans:
+            for c in first[r]:
+                c.wait()
+            for t in range(start, end):
+                z = slice(t * LANES, (t + 1) * LANES)
+                term = speed[:, z] * slopes[0][sources[0][3] + t]
+                if component == 1:
+                    term = term + slopes[1][sources[1][3] + t]
+                result = value[:, z] - 0.1 * term
+                prov[t] = result
+                h, l = two_terms(result)
+                terms[t, :, :LANES] = h
+                terms[t, :, LANES:] = l
+        for c in later:
+            c.wait()
 
         row_at = lax.broadcasted_iota(jnp.int32, (rows, CHUNK), 0)
-        lane_at = lax.broadcasted_iota(jnp.int32, (LANES, CHUNK), 0)
         marker_at = lax.broadcasted_iota(jnp.int32, (marker_rows, CHUNK), 0)
+        row_key = row_at.astype(BF)
+        lane_key = lax.broadcasted_iota(jnp.int32, (LANES, CHUNK), 0).astype(BF)
         one, zero = jnp.ones((), BF), jnp.zeros((), BF)
 
-        def one_hot(hit):
-            return jnp.where(hit, 1.0, 0.0).astype(BF)
+        def key(value):
+            return value.astype(F32).astype(BF)
 
         def pair(i):
             c, t = chunk_ref[i], tile_ref[i]
-            return c, jnp.minimum(t, tiles - 1), row_at == row_ref[c] - t * rows, lane_at == lane_ref[c]
+            return c, jnp.minimum(t, tiles - 1), row_ref[c] - t * rows, lane_key == key(lane_ref[c])
 
         found[...] = jnp.zeros_like(found)
 
         def gather(i, carry):
-            c, t, rows_hit, lanes_hit = pair(i)
-            lanes = one_hot(lanes_hit)
+            c, t, row, lanes_hit = pair(i)
+            lanes = jnp.where(lanes_hit, one, zero)
             both = dot(terms[t], jnp.concatenate([lanes, lanes], axis=0))
-            found[c] += jnp.sum(jnp.where(rows_hit, both, 0.0), axis=0, keepdims=True)
+            found[c] += jnp.sum(jnp.where(row_at == row, both, 0.0), axis=0, keepdims=True)
             return carry
 
         lax.fori_loop(0, pairs, gather, 0, unroll=UNROLL)
@@ -378,14 +391,15 @@
         def add_up(c, total):
             m = marker_ref[c]
             share = jnp.where(marker_at == m // LANES, found[c] * weight_ref[c], 0.0)
-            return total + dot_t(jnp.concatenate(two_terms(share), axis=0), one_hot(lane_at == m % LANES))
+            low_part = jnp.where(lane_key == key(m % LANES), one, zero)
+            return total + dot_t(jnp.concatenate(two_terms(share), axis=0), low_part)
 
         sampled = lax.fori_loop(0, chunks, add_up, jnp.zeros((2 * marker_rows, LANES), F32), unroll=8)
         sampled = jnp.concatenate(two_terms(sampled[:marker_rows] + sampled[marker_rows:]), axis=0)
 
         def spread(c, carry):
             m = marker_ref[c]
-            both = dot(sampled, one_hot(lane_at == m % LANES))
+            both = dot(sampled, jnp.where(lane_key == key(m % LANES), one, zero))
             both = jnp.where(marker_at == m // LANES, both[:marker_rows] + both[marker_rows:], 0.0)
             found[c] = jnp.sum(both, axis=0, keepdims=True) * weight_ref[c]
             return carry
@@ -393,24 +407,27 @@
         lax.fori_loop(0, chunks, spread, 0, unroll=8)
 
         def scatter(i, carry):
-            c, t, rows_hit, lanes_hit = pair(i)
-            value = [jnp.where(lanes_hit, x.astype(F32), 0.0).astype(BF) for x in two_terms(found[c])]
-            both = dot_t(one_hot(rows_hit), jnp.concatenate(value, axis=0))
+            c, t, row, lanes_hit = pair(i)
+            value = [jnp.where(lanes_hit, x, zero) for x in two_terms(found[c])]
+            both = dot_t(jnp.where(row_key == key(row), one, zero), jnp.concatenate(value, axis=0))
             prov[t] -= both[:, :LANES] + both[:, LANES:]
             return carry
 
         lax.fori_loop(0, pairs, scatter, 0, unroll=UNROLL)
         fluid = 1.0 - solid_ref[...].astype(F32)
-        for t in range(tiles):
-            z = slice(t * LANES, (t + 1) * LANES)
-            b = t * LANES // (depth // solid.shape[1])
-            value[:, z] = fluid[:, b : b + 1] * prov[t]
-        last = pltpu.make_async_copy(value, out_ref.at[component, 0], sems.at[0])
-        last.start()
-        last.wait()
+        last = []
+        for i, (_, start, end) in enumerate(spans):
+            for t in range(start, end):
+                b = t * LANES // (depth // solid.shape[1])
+                value[:, t * LANES : (t + 1) * LANES] = fluid[:, b : b + 1] * prov[t]
+            z = pl.ds(start * LANES, (end - start) * LANES)
+            last.append(pltpu.make_async_copy(value.at[:, z], out_ref.at[component, 0, :, z], sems.at[i]))
+            last[-1].start()
+        for c in last:
+            c.wait()
 
     operands = [me, chunk_of, tile_of, flow, base, *entries, solid, *buffers]
-    specs = [SMEM] * 3 + [HBM] * 2 + [VMEM] * (len(entries) + 1) + [HBM] * total
+    specs = [SMEM] * 3 + [HBM] * (2 + len(entries) + 1 + total)
     aliases = {}
     if out is not None:
         aliases = {len(operands): 0}
@@ -423,7 +440,8 @@
         scratch_shapes=[
             block, block, pltpu.VMEM((tiles, rows, LANES), F32), pltpu.VMEM((tiles, rows, 2 * LANES), BF),
             pltpu.VMEM((chunks, 1, CHUNK), F32),
-            pltpu.SemaphoreType.DMA((2 + sum(source[2] for source in sources),)),
+            *[pltpu.VMEM(x.shape, x.dtype) for x in (*entries, solid)],
+            pltpu.SemaphoreType.DMA((2 * len(spans) + sum(source[2] for source in sources) + 5,)),
             *[pltpu.VMEM((source[1], rows, LANES), F32) for source in sources],
         ],
         compiler_params=params(),

time: 238 us -> 236 us (level)
  Pallas kernels: 82.3 us -> 75.8 us
  waiting for transfers between devices: 89.4 us -> 93.8 us
    pallas_call x3, Pallas kernels: 36.6 us -> 30.7 us  [home_step(): pl.pallas_call(kernel, out_shape=jax.ShapeDtypeStruct((3, 1, rows, depth)...]
    ppermute x15, waiting for transfers between devices: 87.1 us -> 91.6 us  [send_lines(): lax.ppermute(blocks[s], 'pen', [(i, (i + CORES * s) % pens) for i in rang...]
  transfers between devices with their start and end apart: 22 -> 22, of which waited for: 12 -> 12; matrix products, arithmetic and copies ran while one was open for 13% -> 13% of each run, Pallas kernels for 33% -> 31%
where the time goes in v4:
time: 236 us; the launch traced here: 235 us
  waiting for transfers between devices  93.8 us (40%)
  Pallas kernels  75.8 us (32%)
  starting transfers between devices  27.6 us (12%)
  local copies, waits for them, and re-layouts  21.3 us (9%)
  other arithmetic  15 us (6%)
    ppermute x15, waiting for transfers between devices, send_lines(): lax.ppermute(blocks[s], 'pen', [(i, (i + CORES * s) % pens) for i in rang...  91.6 us
    pallas_call x3, Pallas kernels, home_step(): pl.pallas_call(kernel, out_shape=jax.ShapeDtypeStruct((3, 1, rows, depth)...  30.7 us
    pallas_call x2, Pallas kernels, line_slopes(): pl.pallas_call(kernel, out_shape=shapes, in_specs=[SMEM, VMEM, VMEM] + [H...  20.2 us
    ppermute x15, starting transfers between devices, send_lines(): lax.ppermute(blocks[s], 'pen', [(i, (i + CORES * s) % pens) for i in rang...  13.9 us
    all_to_all x3, starting transfers between devices, exchange(): return lax.all_to_all(value, 'grp', 0, 0, tiled=True)  12.3 us
    another operation x2, local copies, waits for them, and re-layouts, cut_depth(): return jnp.moveaxis(value.reshape(*value.shape[:-1], grps, width), -2, 0)  11.2 us
    pallas_call x1, Pallas kernels, depth_terms(): pl.pallas_call(kernel, grid=(rows // step,), out_shape=[jax.ShapeDtypeStr...  10.2 us
    sort x1, other arithmetic, marker_order(): key, weight = lax.sort((place * markers + marker, weight), num_keys=1)  6.89 us
  transfers between devices with their start and end apart: 22, of which 12 were waited for; matrix products, arithmetic and copies ran while one was open for 13% of the time, Pallas kernels for 31%

profile of v4, /device:TPU:9, one launch (start us, length us, event | category | flops | bytes accessed | tf_op | source)
XLA Modules:
  0.0 234.6 jit_solution(10792743822682979595)
XLA Ops:
  0.6 3.0 %pack_lines.2 = (f32[6,192,128]{2,1,0:T(8,128)}, f32[6,192,128]{2,1,0:T(8,128)}, f32[6,192,128]{2,1,0:T(8,128)}, f32[6,192,128]{2,1,0:T(8,128)}) custom-call(s32[1]{0:T(128)} %bitcast.me_ref, f32[4,1,192,1536]{3,2,1,0:T(8,128)} %flow_ref.9), custom_call_target="tpu_custom_call" | custom-call | bytes 23592 | tf_op jit(solution)/shard_map/pack_lines/pallas_call | solution.py:111
  7.5 6.2 %reshape_squeeze.3 = f32[4,192,4,384]{3,2,1,0:T(4,128)} reshape(f32[4,1,192,1536]{3,2,1,0:T(8,128)} %flow_ref.9) | data formatting | bytes 9437184 | tf_op jit(solution)/shard_map/reshape;squeeze | solution.py:482
  13.7 5.0 %copy.36 = f32[4,192,4,384]{3,1,0,2:T(8,128)} copy(f32[4,192,4,384]{3,2,1,0:T(4,128)} %reshape_squeeze.3) | data formatting | bytes 9437184 | tf_op jit(solution)/shard_map/reshape;squeeze | solution.py:482
  18.7 5.1 %all-to-all-start = ((f32[4,4,192,384]{3,2,1,0:T(8,128)}), f32[4,4,192,384]{3,2,1,0:T(8,128)}, u32[]{:S(2)}, u32[]{:S(2)}) async-start(f32[4,4,192,384]{3,2,1,0:T(8,128)} %bitcast.18), calls=%async_computation | async-start | bytes 9437184 | tf_op jit(solution)/shard_map/all_to_all | solution.py:485
  25.9 6.9 %sort.23 = (s32[8192]{0:T(1024)S(1)}, f32[8192]{0:T(1024)}, s32[8192]{0:T(1024)}) sort(s32[8192]{0:T(1024)S(1)} %fusion.5, f32[8192]{0:T(1024)S(1)} %reshape.61, s32[8192]{0:T(1024)S(1)} %iota.19), dimensions={0}, to_apply=%region_0.1 | sort | flops 106496 | bytes 196608 | tf_op jit(solution)/shard_map/sort | solution.py:254
  35.8 2.9 %pack_lines.3 = (f32[6,192,128]{2,1,0:T(8,128)}, f32[6,192,128]{2,1,0:T(8,128)}, f32[6,192,128]{2,1,0:T(8,128)}, f32[6,192,128]{2,1,0:T(8,128)}) custom-call(s32[1]{0:T(128)} %bitcast.me_ref, f32[4,1,192,1536]{3,2,1,0:T(8,128)} %flow_ref.9), custom_call_target="tpu_custom_call" | custom-call | bytes 23592 | tf_op jit(solution)/shard_map/pack_lines/pallas_call | solution.py:111
  38.7 16.6 %collective-permute-done.1.rest_2_ = f32[6,192,128]{2,1,0:T(8,128)S(1)} collective-permute-done((f32[6,192,128]{2,1,0:T(8,128)}, f32[6,192,128]{2,1,0:T(8,128)S(1)}, u32[]{:S(2)}, u32[]{:S(2)}) %collective-permute-start.1) | collective-permute-done | bytes 589856 | tf_op jit(solution)/shard_map/ppermute | solution.py:471
  55.3 2.8 %collective-permute-done.2.rest_3_ = f32[6,192,128]{2,1,0:T(8,128)S(1)} collective-permute-done((f32[6,192,128]{2,1,0:T(8,128)}, f32[6,192,128]{2,1,0:T(8,128)S(1)}, u32[]{:S(2)}, u32[]{:S(2)}) %collective-permute-start.2) | collective-permute-done | bytes 589856 | tf_op jit(solution)/shard_map/ppermute | solution.py:471
  59.8 1.5 collective-permute-start.4
  61.3 1.5 collective-permute-start.5
  64.8 10.1 %line_slopes.2 = (f32[6,192,128]{2,1,0:T(8,128)}, f32[6,192,128]{2,1,0:T(8,128)}, f32[6,192,128]{2,1,0:T(8,128)}, f32[6,192,128]{2,1,0:T(8,128)}) custom-call(s32[1]{0:T(128)} %bitcast.me_ref, bf16[2,768,768]{2,1,0:T(8,128)(2,1)} %constant.112.clone.high_ref, bf16[2,768,768]{2,1,0:T(8,128)(2,1)} %constant.113.clone.low_ref, ...), custom_call_target="tpu_custom_call" | custom-call | flops 27179088 | bytes 117964 | tf_op jit(solution)/shard_map/line_slopes/pallas_call | solution.py:171
  76.3 5.7 %slab_terms.1 = (f32[4,3,192,384]{3,2,1,0:T(8,128)}, f32[4,192,384]{2,1,0:T(8,128)}) custom-call(f32[4,4,192,384]{3,2,1,0:T(8,128)} %all-to-all-done.in_ref), custom_call_target="tpu_custom_call" | custom-call | flops 188743 | bytes 94371 | tf_op jit(solution)/shard_map/slab_terms/pallas_call | solution.py:236
  82.0 3.7 %all-to-all-start.1 = ((f32[4,3,192,384]{3,2,1,0:T(8,128)}), f32[4,3,192,384]{3,2,1,0:T(8,128)S(1)}, u32[]{:S(2)}, u32[]{:S(2)}) async-start(f32[4,3,192,384]{3,2,1,0:T(8,128)} %get-tuple-element.137), calls=%async_computation.1 | async-start | bytes 7077888 | tf_op jit(solution)/shard_map/all_to_all | solution.py:485
  85.7 25.1 %collective-permute-done.4.rest_2_ = f32[6,192,128]{2,1,0:T(8,128)} collective-permute-done((f32[6,192,128]{2,1,0:T(8,128)}, f32[6,192,128]{2,1,0:T(8,128)}, u32[]{:S(2)}, u32[]{:S(2)}) %collective-permute-start.4) | collective-permute-done | bytes 589856 | tf_op jit(solution)/shard_map/ppermute | solution.py:471
  110.9 2.5 %collective-permute-done.5.rest_3_ = f32[6,192,128]{2,1,0:T(8,128)} collective-permute-done((f32[6,192,128]{2,1,0:T(8,128)}, f32[6,192,128]{2,1,0:T(8,128)}, u32[]{:S(2)}, u32[]{:S(2)}) %collective-permute-start.5) | collective-permute-done | bytes 589856 | tf_op jit(solution)/shard_map/ppermute | solution.py:471
  113.4 1.6 pad_maximum_fusion.1
  116.4 1.5 collective-permute-start.10
  120.9 10.1 %line_slopes.3 = (f32[3,192,128]{2,1,0:T(8,128)}, f32[3,192,128]{2,1,0:T(8,128)}, f32[3,192,128]{2,1,0:T(8,128)}, f32[3,192,128]{2,1,0:T(8,128)}, f32[3,192,128]...) custom-call(s32[1]{0:T(128)} %bitcast.me_ref, ...), custom_call_target="tpu_custom_call" | custom-call | flops 27179088 | bytes 117964 | tf_op jit(solution)/shard_map/line_slopes/pallas_call | solution.py:171
  131.0 10.2 %depth_terms.1 = (f32[3,192,1536]{2,1,0:T(8,128)}, f32[192,1536]{1,0:T(8,128)}) custom-call(f32[4,1,192,1536]{3,2,1,0:T(8,128)} %flow_ref.9, bf16[2,768,768]{2,1,0:T(8,128)(2,1)} %constant.112.clone.high_ref, bf16[2,768,768]{2,1,0:T(8,128)(2,1)} %constant.113.clone.low_ref), custom_call_target="tpu_custom_call" | custom-call | flops 54358180 | bytes 141557 | tf_op jit(solution)/shard_map/depth_terms/pallas_call | solution.py:209
  142.1 1.5 copy-done
  143.6 2.4 %sub.64.base_ref = f32[3,192,1536]{2,1,0:T(8,128)} subtract(f32[3,192,1536]{2,1,0:T(8,128)S(1)} %copy-done, f32[3,192,1536]{2,1,0:T(8,128)S(1)} %bitcast.19) | non-fusion elementwise | flops 884736 | bytes 10616832 | tf_op jit(solution)/shard_map/sub | solution.py:509
  146.1 20.4 %collective-permute-done.9.rest_7_.rest_11_.rest_2_ = f32[6,192,128]{2,1,0:T(8,128)} collective-permute-done((f32[6,192,128]{2,1,0:T(8,128)}, f32[6,192,128]{2,1,0:T(8,128)}, u32[]{:S(2)}, u32[]{:S(2)}) %collective-permute-start.9) | collective-permute-done | bytes 589856 | tf_op jit(solution)/shard_map/ppermute | solution.py:471
  166.5 2.0 collective-permute-done.10.rest_8_.rest_12_.rest_3_
  171.8 10.7 %home_step.3.rest_9_ = f32[3,1,192,1536]{3,2,1,0:T(8,128)} custom-call(s32[1]{0:T(128)} %bitcast.me_ref, s32[44]{0:T(128)} %copy-done.15, s32[44]{0:T(128)} %compare_select_fusion.tile_ref, f32[4,1,192,1536]{3,2,1,0:T(8,128)} %flow_ref.9, f32[3,192,1536]{2,1,0:T(8,128)} %sub.64.base_ref, s32[32,1,256]{2,1,0:T(1,128)} %bitcast.29, s32[32,1,256]{2,1,0:T(1,128)} %bitcast.26, ...), custom_call_target="tpu_custom_call" | custom-call | flops 44291848 | bytes 58982 | tf_op jit(solution)/shard_map/home_step/pallas_call | solution.py:437
  182.5 11.2 %collective-permute-done.14.rest_7_ = f32[3,192,128]{2,1,0:T(8,128)S(1)} collective-permute-done((f32[3,192,128]{2,1,0:T(8,128)S(1)}, f32[3,192,128]{2,1,0:T(8,128)S(1)}, u32[]{:S(2)}, u32[]{:S(2)}) %collective-permute-start.14) | collective-permute-done | bytes 294944 | tf_op jit(solution)/shard_map/ppermute | solution.py:471
  193.7 2.4 %collective-permute-done.15.rest_8_ = f32[3,192,128]{2,1,0:T(8,128)S(1)} collective-permute-done((f32[3,192,128]{2,1,0:T(8,128)S(1)}, f32[3,192,128]{2,1,0:T(8,128)S(1)}, u32[]{:S(2)}, u32[]{:S(2)}) %collective-permute-start.15) | collective-permute-done | bytes 294944 | tf_op jit(solution)/shard_map/ppermute | solution.py:471
  198.3 10.0 %home_step.4.rest_9_ = f32[3,1,192,1536]{3,2,1,0:T(8,128)} custom-call(s32[1]{0:T(128)} %bitcast.me_ref, s32[44]{0:T(128)} %copy-done.15, s32[44]{0:T(128)} %compare_select_fusion.tile_ref, f32[4,1,192,1536]{3,2,1,0:T(8,128)} %flow_ref.9, f32[3,192,1536]{2,1,0:T(8,128)} %sub.64.base_ref, s32[32,1,256]{2,1,0:T(1,128)} %bitcast.30, ...), custom_call_target="tpu_custom_call", output_to_operand_aliasing={{}: (14, {})} | custom-call | flops 44291848 | bytes 58982 | tf_op jit(solution)/shard_map/home_step/pallas_call | solution.py:437
  208.4 2.9 %home_divergence.1 = f32[4,192,384]{2,1,0:T(8,128)} custom-call(s32[1]{0:T(128)} %bitcast.me_ref, f32[192,1536]{1,0:T(8,128)} %get-tuple-element.172.slope_ref, f32[6,192,128]{2,1,0:T(8,128)} %get-tuple-element.153.rest_5_.rest_9_.rest_0_, f32[6,192,128]{2,1,0:T(8,128)} %collective-permute-done.8.rest_6_.rest_10_.rest_1_, ...), custom_call_target="tpu_custom_call" | custom-call | bytes 35389 | tf_op jit(solution)/shard_map/home_divergence/pallas_call | solution.py:307
  211.3 3.5 %all-to-all-start.2 = ((f32[4,192,384]{2,1,0:T(8,128)}), f32[4,192,384]{2,1,0:T(8,128)S(1)}, u32[]{:S(2)}, u32[]{:S(2)}) async-start(f32[4,192,384]{2,1,0:T(8,128)} %home_divergence.1), calls=%async_computation.2 | async-start | bytes 2359296 | tf_op jit(solution)/shard_map/all_to_all | solution.py:485
  214.9 6.3 %collective-permute-done.17.rest_7_ = f32[3,192,128]{2,1,0:T(8,128)} collective-permute-done((f32[3,192,128]{2,1,0:T(8,128)S(1)}, f32[3,192,128]{2,1,0:T(8,128)}, u32[]{:S(2)}, u32[]{:S(2)}) %collective-permute-start.17) | collective-permute-done | bytes 294944 | tf_op jit(solution)/shard_map/ppermute | solution.py:471
  221.2 2.2 collective-permute-done.18.rest_8_
  223.4 10.0 %home_step.5 = f32[3,1,192,1536]{3,2,1,0:T(8,128)} custom-call(s32[1]{0:T(128)} %bitcast.me_ref, s32[44]{0:T(128)} %copy-done.15, s32[44]{0:T(128)} %compare_select_fusion.tile_ref, f32[4,1,192,1536]{3,2,1,0:T(8,128)} %flow_ref.9, f32[3,192,1536]{2,1,0:T(8,128)} %sub.64.base_ref, s32[32,1,256]{2,1,0:T(1,128)} %bitcast.31, ...), custom_call_target="tpu_custom_call", output_to_operand_aliasing={{}: (14, {})} | custom-call | flops 44291850240 | bytes 58982400 | tf_op jit(solution)/shard_map/home_step/pallas_call | solution.py:437
  (103 shorter events, 25.8 us)
Async XLA Ops:
  3.7 35.0 %collective-permute-start = (f32[6,192,128]{2,1,0:T(8,128)}, f32[6,192,128]{2,1,0:T(8,128)S(1)}, u32[]{:S(2)}, u32[]{:S(2)}) collective-permute-start(f32[6,192,128]{2,1,0:T(8,128)} %get-tuple-element.90), channel_id=1, source_target_pairs={{0,2},{1,3},{2,4},{3,5},{4,6},{5,7},{6,0},{7,1},{8,10},{9,11},{10,... | collective-permute-start | bytes 1769480 | tf_op jit(solution)/shard_map/ppermute | solution.py:471
  5.0 50.2 %collective-permute-start.1 = (f32[6,192,128]{2,1,0:T(8,128)}, f32[6,192,128]{2,1,0:T(8,128)S(1)}, u32[]{:S(2)}, u32[]{:S(2)}) collective-permute-start(f32[6,192,128]{2,1,0:T(8,128)} %get-tuple-element.91), channel_id=1, source_target_pairs={{0,4},{1,5},{2,6},{3,7},{4,0},{5,1},{6,2},{7,3},{8,12},{9,13},{10,... | collective-permute-start | bytes 1769480 | tf_op jit(solution)/shard_map/ppermute | solution.py:471
  6.1 52.0 %collective-permute-start.2 = (f32[6,192,128]{2,1,0:T(8,128)}, f32[6,192,128]{2,1,0:T(8,128)S(1)}, u32[]{:S(2)}, u32[]{:S(2)}) collective-permute-start(f32[6,192,128]{2,1,0:T(8,128)} %get-tuple-element.92), channel_id=1, source_target_pairs={{0,6},{1,7},{2,0},{3,1},{4,2},{5,3},{6,4},{7,5},{8,14},{9,15},{10,... | collective-permute-start | bytes 1769480 | tf_op jit(solution)/shard_map/ppermute | solution.py:471
  18.7 57.5 %all-to-all-start = ((f32[4,4,192,384]{3,2,1,0:T(8,128)}), f32[4,4,192,384]{3,2,1,0:T(8,128)}, u32[]{:S(2)}, u32[]{:S(2)}) async-start(f32[4,4,192,384]{3,2,1,0:T(8,128)} %bitcast.18), calls=%async_computation | async-start | bytes 9437184 | tf_op jit(solution)/shard_map/all_to_all | solution.py:485
  38.7 19.6 %copy-start.1 = (f32[6,192,128]{2,1,0:T(8,128)}, f32[6,192,128]{2,1,0:T(8,128)S(1)}, u32[]{:S(2)}) copy-start(f32[6,192,128]{2,1,0:T(8,128)S(1)} %collective-permute-done.rest_1_) | copy-start | bytes 1769476
  58.9 3.8 %collective-permute-start.7 = (f32[18,192,128]{2,1,0:T(8,128)S(1)}, f32[18,192,128]{2,1,0:T(8,128)S(1)}, u32[]{:S(2)}, u32[]{:S(2)}) collective-permute-start(f32[18,192,128]{2,1,0:T(8,128)S(1)} %pad_maximum_fusion), channel_id=1, source_target_pairs={{0,1},{1,0},{2,3},{3,2},{4,5},{5,4},{6,7},{7,6},{8,9},{9,8},{10,11... | collective-permute-start | bytes 5308424 | tf_op jit(solution)/shard_map/ppermute | solution.py:476
  59.4 4.6 %collective-permute-start.6 = (f32[6,192,128]{2,1,0:T(8,128)S(1)}, f32[6,192,128]{2,1,0:T(8,128)S(1)}, u32[]{:S(2)}, u32[]{:S(2)}) collective-permute-start(f32[6,192,128]{2,1,0:T(8,128)S(1)} %copy-done.5), channel_id=1, source_target_pairs={{0,1},{1,0},{2,3},{3,2},{4,5},{5,4},{6,7},{7,6},{8,9},{9,8},{10,11... | collective-permute-start | bytes 1769480 | tf_op jit(solution)/shard_map/ppermute | solution.py:476
  59.8 26.0 %collective-permute-start.3 = (f32[6,192,128]{2,1,0:T(8,128)}, f32[6,192,128]{2,1,0:T(8,128)}, u32[]{:S(2)}, u32[]{:S(2)}) collective-permute-start(f32[6,192,128]{2,1,0:T(8,128)} %get-tuple-element.105), channel_id=1, source_target_pairs={{0,2},{1,3},{2,4},{3,5},{4,6},{5,7},{6,0},{7,1},{8,10},{9,11},{10,... | collective-permute-start | bytes 1769480 | tf_op jit(solution)/shard_map/ppermute | solution.py:471
  59.8 51.1 %collective-permute-start.4 = (f32[6,192,128]{2,1,0:T(8,128)}, f32[6,192,128]{2,1,0:T(8,128)}, u32[]{:S(2)}, u32[]{:S(2)}) collective-permute-start(f32[6,192,128]{2,1,0:T(8,128)} %get-tuple-element.106), channel_id=1, source_target_pairs={{0,4},{1,5},{2,6},{3,7},{4,0},{5,1},{6,2},{7,3},{8,12},{9,13},{10,... | collective-permute-start | bytes 1769480 | tf_op jit(solution)/shard_map/ppermute | solution.py:471
  61.3 52.1 %collective-permute-start.5 = (f32[6,192,128]{2,1,0:T(8,128)}, f32[6,192,128]{2,1,0:T(8,128)}, u32[]{:S(2)}, u32[]{:S(2)}) collective-permute-start(f32[6,192,128]{2,1,0:T(8,128)} %get-tuple-element.107), channel_id=1, source_target_pairs={{0,6},{1,7},{2,0},{3,1},{4,2},{5,3},{6,4},{7,5},{8,14},{9,15},{10,... | collective-permute-start | bytes 1769480 | tf_op jit(solution)/shard_map/ppermute | solution.py:471
  82.0 59.3 %all-to-all-start.1 = ((f32[4,3,192,384]{3,2,1,0:T(8,128)}), f32[4,3,192,384]{3,2,1,0:T(8,128)S(1)}, u32[]{:S(2)}, u32[]{:S(2)}) async-start(f32[4,3,192,384]{3,2,1,0:T(8,128)} %get-tuple-element.137), calls=%async_computation.1 | async-start | bytes 7077888 | tf_op jit(solution)/shard_map/all_to_all | solution.py:485
  115.0 3.9 %collective-permute-start.12 = (f32[18,192,128]{2,1,0:T(8,128)S(1)}, f32[18,192,128]{2,1,0:T(8,128)S(1)}, u32[]{:S(2)}, u32[]{:S(2)}) collective-permute-start(f32[18,192,128]{2,1,0:T(8,128)S(1)} %pad_maximum_fusion.1), channel_id=1, source_target_pairs={{0,1},{1,0},{2,3},{3,2},{4,5},{5,4},{6,7},{7,6},{8,9},{9,8},{10,11... | collective-permute-start | bytes 5308424 | tf_op jit(solution)/shard_map/ppermute | solution.py:476
  115.5 4.6 %collective-permute-start.11 = (f32[6,192,128]{2,1,0:T(8,128)S(1)}, f32[6,192,128]{2,1,0:T(8,128)S(1)}, u32[]{:S(2)}, u32[]{:S(2)}) collective-permute-start(f32[6,192,128]{2,1,0:T(8,128)S(1)} %copy-done.6), channel_id=1, source_target_pairs={{0,1},{1,0},{2,3},{3,2},{4,5},{5,4},{6,7},{7,6},{8,9},{9,8},{10,11... | collective-permute-start | bytes 1769480 | tf_op jit(solution)/shard_map/ppermute | solution.py:476
  115.6 30.4 %collective-permute-start.8 = (f32[6,192,128]{2,1,0:T(8,128)}, f32[6,192,128]{2,1,0:T(8,128)}, u32[]{:S(2)}, u32[]{:S(2)}) collective-permute-start(f32[6,192,128]{2,1,0:T(8,128)} %get-tuple-element.120), channel_id=1, source_target_pairs={{0,2},{1,3},{2,4},{3,5},{4,6},{5,7},{6,0},{7,1},{8,10},{9,11},{10,... | collective-permute-start | bytes 1769480 | tf_op jit(solution)/shard_map/ppermute | solution.py:471
  115.6 50.8 %collective-permute-start.9 = (f32[6,192,128]{2,1,0:T(8,128)}, f32[6,192,128]{2,1,0:T(8,128)}, u32[]{:S(2)}, u32[]{:S(2)}) collective-permute-start(f32[6,192,128]{2,1,0:T(8,128)} %get-tuple-element.121), channel_id=1, source_target_pairs={{0,4},{1,5},{2,6},{3,7},{4,0},{5,1},{6,2},{7,3},{8,12},{9,13},{10,... | collective-permute-start | bytes 1769480 | tf_op jit(solution)/shard_map/ppermute | solution.py:471
  116.4 52.1 %collective-permute-start.10 = (f32[6,192,128]{2,1,0:T(8,128)}, f32[6,192,128]{2,1,0:T(8,128)}, u32[]{:S(2)}, u32[]{:S(2)}) collective-permute-start(f32[6,192,128]{2,1,0:T(8,128)} %get-tuple-element.122), channel_id=1, source_target_pairs={{0,6},{1,7},{2,0},{3,1},{4,2},{5,3},{6,4},{7,5},{8,14},{9,15},{10,... | collective-permute-start | bytes 1769480 | tf_op jit(solution)/shard_map/ppermute | solution.py:471
  143.6 24.9 %copy-start.21 = (f32[3,192,128]{2,1,0:T(8,128)S(1)}, f32[3,192,128]{2,1,0:T(8,128)}, u32[]{:S(2)}) copy-start(f32[3,192,128]{2,1,0:T(8,128)} %get-tuple-element.145) | copy-start | bytes 884740
  143.6 24.9 %copy-start.20 = (f32[3,192,128]{2,1,0:T(8,128)S(1)}, f32[3,192,128]{2,1,0:T(8,128)}, u32[]{:S(2)}) copy-start(f32[3,192,128]{2,1,0:T(8,128)} %get-tuple-element.146) | copy-start | bytes 884740
  143.6 26.0 %copy-start.19 = (f32[3,192,128]{2,1,0:T(8,128)S(1)}, f32[3,192,128]{2,1,0:T(8,128)}, u32[]{:S(2)}) copy-start(f32[3,192,128]{2,1,0:T(8,128)} %get-tuple-element.147) | copy-start | bytes 884740
  143.6 27.4 %copy-start.14 = (s32[1,192,12]{1,0,2:T(1,128)S(1)}, s32[1,192,12]{1,0,2:T(1,128)}, u32[]{:S(2)}) copy-start(s32[1,192,12]{1,0,2:T(1,128)} %param.9) | copy-start | bytes 27652
  168.5 14.0 %collective-permute-start.13 = (f32[3,192,128]{2,1,0:T(8,128)S(1)}, f32[3,192,128]{2,1,0:T(8,128)S(1)}, u32[]{:S(2)}, u32[]{:S(2)}) collective-permute-start(f32[3,192,128]{2,1,0:T(8,128)S(1)} %copy-done.21), channel_id=1, source_target_pairs={{0,2},{1,3},{2,4},{3,5},{4,6},{5,7},{6,0},{7,1},{8,10},{9,11},{10,... | collective-permute-start | bytes 884744 | tf_op jit(solution)/shard_map/ppermute | solution.py:471
  168.5 25.2 %collective-permute-start.14 = (f32[3,192,128]{2,1,0:T(8,128)S(1)}, f32[3,192,128]{2,1,0:T(8,128)S(1)}, u32[]{:S(2)}, u32[]{:S(2)}) collective-permute-start(f32[3,192,128]{2,1,0:T(8,128)S(1)} %copy-done.20), channel_id=1, source_target_pairs={{0,4},{1,5},{2,6},{3,7},{4,0},{5,1},{6,2},{7,3},{8,12},{9,13},{10,... | collective-permute-start | bytes 884744 | tf_op jit(solution)/shard_map/ppermute | solution.py:471
  169.6 26.4 %collective-permute-start.15 = (f32[3,192,128]{2,1,0:T(8,128)S(1)}, f32[3,192,128]{2,1,0:T(8,128)S(1)}, u32[]{:S(2)}, u32[]{:S(2)}) collective-permute-start(f32[3,192,128]{2,1,0:T(8,128)S(1)} %copy-done.19), channel_id=1, source_target_pairs={{0,6},{1,7},{2,0},{3,1},{4,2},{5,3},{6,4},{7,5},{8,14},{9,15},{10,... | collective-permute-start | bytes 884744 | tf_op jit(solution)/shard_map/ppermute | solution.py:471
  171.8 24.3 %copy-start.18 = (f32[3,192,128]{2,1,0:T(8,128)S(1)}, f32[3,192,128]{2,1,0:T(8,128)}, u32[]{:S(2)}) copy-start(f32[3,192,128]{2,1,0:T(8,128)} %get-tuple-element.158) | copy-start | bytes 884740
  171.8 24.3 %copy-start.17 = (f32[3,192,128]{2,1,0:T(8,128)S(1)}, f32[3,192,128]{2,1,0:T(8,128)}, u32[]{:S(2)}) copy-start(f32[3,192,128]{2,1,0:T(8,128)} %get-tuple-element.159) | copy-start | bytes 884740
  171.8 25.1 %copy-start.16 = (f32[3,192,128]{2,1,0:T(8,128)S(1)}, f32[3,192,128]{2,1,0:T(8,128)}, u32[]{:S(2)}) copy-start(f32[3,192,128]{2,1,0:T(8,128)} %get-tuple-element.160) | copy-start | bytes 884740
  182.5 15.8 %copy-start.9 = (f32[3,192,128]{2,1,0:T(8,128)}, f32[3,192,128]{2,1,0:T(8,128)S(1)}, u32[]{:S(2)}) copy-start(f32[3,192,128]{2,1,0:T(8,128)S(1)} %collective-permute-done.13.rest_6_) | copy-start | bytes 884740
  196.0 18.8 %collective-permute-start.16 = (f32[3,192,128]{2,1,0:T(8,128)S(1)}, f32[3,192,128]{2,1,0:T(8,128)S(1)}, u32[]{:S(2)}, u32[]{:S(2)}) collective-permute-start(f32[3,192,128]{2,1,0:T(8,128)S(1)} %copy-done.18), channel_id=1, source_target_pairs={{0,2},{1,3},{2,4},{3,5},{4,6},{5,7},{6,0},{7,1},{8,10},{9,11},{10,... | collective-permute-start | bytes 884744 | tf_op jit(solution)/shard_map/ppermute | solution.py:471
  196.1 25.2 %collective-permute-start.17 = (f32[3,192,128]{2,1,0:T(8,128)S(1)}, f32[3,192,128]{2,1,0:T(8,128)}, u32[]{:S(2)}, u32[]{:S(2)}) collective-permute-start(f32[3,192,128]{2,1,0:T(8,128)S(1)} %copy-done.17), channel_id=1, source_target_pairs={{0,4},{1,5},{2,6},{3,7},{4,0},{5,1},{6,2},{7,3},{8,12},{9,13},{10,... | collective-permute-start | bytes 884744 | tf_op jit(solution)/shard_map/ppermute | solution.py:471
  196.9 26.5 %collective-permute-start.18 = (f32[3,192,128]{2,1,0:T(8,128)S(1)}, f32[3,192,128]{2,1,0:T(8,128)}, u32[]{:S(2)}, u32[]{:S(2)}) collective-permute-start(f32[3,192,128]{2,1,0:T(8,128)S(1)} %copy-done.16), channel_id=1, source_target_pairs={{0,6},{1,7},{2,0},{3,1},{4,2},{5,3},{6,4},{7,5},{8,14},{9,15},{10,... | collective-permute-start | bytes 884744 | tf_op jit(solution)/shard_map/ppermute | solution.py:471
  211.3 22.2 %all-to-all-start.2 = ((f32[4,192,384]{2,1,0:T(8,128)}), f32[4,192,384]{2,1,0:T(8,128)S(1)}, u32[]{:S(2)}, u32[]{:S(2)}) async-start(f32[4,192,384]{2,1,0:T(8,128)} %home_divergence.1), calls=%async_computation.2 | async-start | bytes 2359296 | tf_op jit(solution)/shard_map/all_to_all | solution.py:485
  214.9 18.6 %copy-start.4 = (f32[4,192,384]{2,1,0:T(8,128)S(1)}, f32[4,192,384]{2,1,0:T(8,128)}, u32[]{:S(2)}) copy-start(f32[4,192,384]{2,1,0:T(8,128)} %get-tuple-element.173) | copy-start | bytes 3538948
  (13 other events, 37.7 us)

commit v5 on v4

--- a/solution.py
+++ b/solution.py
@@ -76,6 +76,13 @@
         self.stages = [list(range(first))]
         if first < self.rounds:
             self.stages.append(list(range(first, self.rounds)))
+        self.paired = self.chips & (self.chips - 1) == 0
+
+    def to(self, chip, s):
+        return chip ^ s if self.paired else (chip + s) % self.chips
+
+    def source(self, chip, s):
+        return chip ^ s if self.paired else (chip + self.chips - s) % self.chips
 
 
 def run_copies(copies):
@@ -101,7 +108,7 @@
             for c in loads[k * n : (k + 1) * n]:
                 c.wait()
             for s in range(n):
-                pair = jnp.minimum(k * n + lax.rem(me_ref[0] // CORES + s, n), end - start - 1)
+                pair = jnp.minimum(k * n + plan.to(me_ref[0] // CORES, s), end - start - 1)
                 copies.append(pltpu.make_async_copy(held.at[pair], outs[s].at[k], out_sems.at[len(copies)]))
                 copies[-1].start()
         for c in copies:
@@ -116,7 +123,7 @@
     )(me, flow)
 
 
-def line_slopes(plan, rounds, groups, me, received, other, tables):
+def line_slopes(plan, rounds, groups, me, received, other, tables, share=0.01):
     n, rows = plan.chips, plan.rows
     length, half, count = plan.pens * rows, plan.pens * rows // 2, len(rounds)
     wide = count * LANES
@@ -130,7 +137,7 @@
         copies = []
         for refs, c in ((ins, core), (others, 1 - core)):
             for s in range(n):
-                pen = lax.rem(chip + n - s, n) * CORES + c
+                pen = plan.source(chip, s) * CORES + c
                 at = pl.ds(pl.multiple_of(pen * rows, 8), rows)
                 copies.append(pltpu.make_async_copy(refs[s], lines.at[:, at, :], in_sems.at[len(copies)]))
         run_copies(copies)
@@ -163,7 +170,7 @@
         for g, group in enumerate(groups):
             at_k = pl.ds(rounds.index(group[0]), len(group))
             for s in range(n):
-                home = lax.rem(chip + s, n)
+                home = plan.to(chip, s)
                 copies.append(pltpu.make_async_copy(result.at[home, at_k], outs[g * n + s], out_sems.at[len(copies)]))
         run_copies(copies)
 
@@ -177,7 +184,7 @@
             pltpu.SemaphoreType.DMA((2 * n,)), pltpu.SemaphoreType.DMA((len(shapes),)),
         ],
         compiler_params=params(),
-        cost_estimate=cost(6 * half * half * wide, 6 * count * length * LANES + 8 * half * half),
+        cost_estimate=cost(6 * half * half * wide, 6 * count * length * LANES + 8 * half * half, share),
         name="line_slopes",
     )(me, *tables, *received, *other)
     return [out[g * n : (g + 1) * n] for g in range(len(groups))]
@@ -281,7 +288,7 @@
 
     def copies(me, refs, slopes, sems, first):
         return [(r, pltpu.make_async_copy(
-            refs[b].at[k], slopes.at[(r - low) * n + lax.rem(me // CORES + n - s, n)], sems.at[first + i]))
+            refs[b].at[k], slopes.at[(r - low) * n + plan.source(me // CORES, s)], sems.at[first + i]))
             for i, (b, k, r, s) in enumerate(wanted)]
 
     skip = slot * tiles - low * n
@@ -463,18 +470,18 @@
         return lax.optimization_barrier((value, others))[0]
 
     chips = plan.chips
-    shifts = sorted(range(1, chips), key=lambda s: abs(2 * s - chips))
+    shifts = [2, 1, 3] if chips == 4 else list(range(1, chips))
 
     def send_lines(blocks):
         got = {0: blocks[0]}
         for s in shifts:
-            got[s] = lax.ppermute(blocks[s], "pen", [(i, (i + CORES * s) % pens) for i in range(pens)])
+            got[s] = lax.ppermute(blocks[s], "pen", [(i, plan.to(i // CORES, s) * CORES + i % CORES) for i in range(pens)])
         return [got[s] for s in range(chips)]
 
+    def other(value):
+        return lax.ppermute(value, "pen", [(i, i ^ 1) for i in range(pens)])
+
     def swap(blocks):
-        def other(value):
-            return lax.ppermute(value, "pen", [(i, i ^ 1) for i in range(pens)])
-
         joined = other(jnp.concatenate(blocks[1:], axis=0))
         return [other(blocks[0])] + jnp.split(joined, chips - 1, axis=0)
 
@@ -484,13 +491,18 @@
     def exchange(value):
         return lax.all_to_all(value, "grp", 0, 0, tiled=True)
 
-    def slopes_of(rounds, cut, lines):
-        return line_slopes(plan, rounds, cut, pen_at, lines, swap(lines), tables)
+    def slopes_of(rounds, cut, lines, swapped, share=0.01):
+        return line_slopes(plan, rounds, cut, pen_at, lines, swapped, tables, share)
 
     first, second = plan.stages
     middle = -(-len(second) // 2)
     cut = [second[:middle], second[middle:]] if len(second) > 1 else [second]
-    together = lax.optimization_barrier
+    def together(values):
+        turn = lambda v, back: [v[0]] + [v[1 + (shifts.index(s) if back else shifts[s - 1] - 1)] for s in range(1, chips)]
+        is_lines = lambda v: isinstance(v, list) and len(v) == chips and all(hasattr(x, "shape") for x in v)
+        turned = [turn(v, False) if is_lines(v) else v for v in values]
+        out = lax.optimization_barrier(tuple(turned))
+        return [turn(o, True) if is_lines(v) else o for v, o in zip(values, out)]
 
     packed = pack_lines(plan, first, pen_at, flow)
     lines = send_lines(packed)
@@ -499,12 +511,13 @@
     packed = pack_lines(plan, second, pen_at, after(flow, order))
     lines, order, packed = together((lines, order, packed))
     lines_2 = send_lines(packed)
-    (slopes,) = slopes_of(first, [first], lines)
+    (slopes,) = slopes_of(first, [first], lines, swap(lines))
+    own = other(after(packed[0], slopes))
     terms_x, slopes_x = slab_terms(compact_matrix(grps), after(lines_x, slopes))
     across = exchange(terms_x)
-    lines_2, slopes, slopes_x = together((lines_2, slopes, slopes_x))
+    lines_2, slopes, slopes_x, own = together((lines_2, slopes, slopes_x, own))
     back = send_lines(slopes)
-    slopes = slopes_of(second, cut, lines_2)
+    slopes = slopes_of(second, cut, lines_2, [own] + [other(x) for x in lines_2[1:]], 6.5)
     base, slope_z = depth_terms(after(flow, slopes), tables_z)
     base = base - 0.1 * jnp.moveaxis(after(across, base), 0, 2).reshape(3, rows, depth)
     back, slopes, base, slope_z = together((back, slopes, base, slope_z))

time: 236 us -> 233 us (0.987)
  local copies, waits for them, and re-layouts: 21.3 us -> 18.5 us
  transfers between devices with their start and end apart: 22 -> 24, of which waited for: 12 -> 10; matrix products, arithmetic and copies ran while one was open for 13% -> 12% of each run, Pallas kernels for 31% -> 31%
where the time goes in v5:
time: 233 us; the launch traced here: 232 us
  waiting for transfers between devices  93.3 us (40%)
  Pallas kernels  75.9 us (33%)
  starting transfers between devices  29.9 us (13%)
  local copies, waits for them, and re-layouts  18.5 us (8%)
  other arithmetic  13.5 us (6%)
    ppermute x15, waiting for transfers between devices, send_lines(): lax.ppermute(blocks[s], 'pen', [(i, plan.to(i // CORES, s) * CORES + i %...  91.1 us
    pallas_call x3, Pallas kernels, home_step(): pl.pallas_call(kernel, out_shape=jax.ShapeDtypeStruct((3, 1, rows, depth)...  31 us
    pallas_call x2, Pallas kernels, line_slopes(): pl.pallas_call(kernel, out_shape=shapes, in_specs=[SMEM, VMEM, VMEM] + [H...  20.1 us
    ppermute x15, starting transfers between devices, send_lines(): lax.ppermute(blocks[s], 'pen', [(i, plan.to(i // CORES, s) * CORES + i %...  14.5 us
    all_to_all x3, starting transfers between devices, exchange(): return lax.all_to_all(value, 'grp', 0, 0, tiled=True)  12.5 us
    another operation x2, local copies, waits for them, and re-layouts, cut_depth(): return jnp.moveaxis(value.reshape(*value.shape[:-1], grps, width), -2, 0)  11.2 us
    pallas_call x1, Pallas kernels, depth_terms(): pl.pallas_call(kernel, grid=(rows // step,), out_shape=[jax.ShapeDtypeStr...  10.2 us
    sort x1, other arithmetic, marker_order(): key, weight = lax.sort((place * markers + marker, weight), num_keys=1)  6.91 us
  transfers between devices with their start and end apart: 24, of which 10 were waited for; matrix products, arithmetic and copies ran while one was open for 12% of the time, Pallas kernels for 31%

profile of v5, /device:TPU:9, one launch (start us, length us, event | category | flops | bytes accessed | tf_op | source)
XLA Modules:
  0.0 232.1 jit_solution(8703489403936882638)
XLA Ops:
  0.6 3.0 %pack_lines.2 = (f32[6,192,128]{2,1,0:T(8,128)}, f32[6,192,128]{2,1,0:T(8,128)}, f32[6,192,128]{2,1,0:T(8,128)}, f32[6,192,128]{2,1,0:T(8,128)}) custom-call(s32[1]{0:T(128)} %bitcast.me_ref, f32[4,1,192,1536]{3,2,1,0:T(8,128)} %flow_ref.9), custom_call_target="tpu_custom_call" | custom-call | bytes 23592 | tf_op jit(solution)/shard_map/pack_lines/pallas_call | solution.py:118
  3.6 2.4 %collective-permute-start = (f32[6,192,128]{2,1,0:T(8,128)}, f32[6,192,128]{2,1,0:T(8,128)S(1)}, u32[]{:S(2)}, u32[]{:S(2)}) collective-permute-start(f32[6,192,128]{2,1,0:T(8,128)} %get-tuple-element.92), channel_id=1, source_target_pairs={{0,4},{1,5},{2,6},{3,7},{4,0},{5,1},{6,2},{7,3},{8,12},{9,13},{10,... | collective-permute-start | bytes 1769480 | tf_op jit(solution)/shard_map/ppermute | solution.py:478
  6.3 6.2 %reshape_squeeze.3 = f32[4,192,4,384]{3,2,1,0:T(4,128)} reshape(f32[4,1,192,1536]{3,2,1,0:T(8,128)} %flow_ref.9) | data formatting | bytes 9437184 | tf_op jit(solution)/shard_map/reshape;squeeze | solution.py:489
  12.5 5.0 %copy.36 = f32[4,192,4,384]{3,1,0,2:T(8,128)} copy(f32[4,192,4,384]{3,2,1,0:T(4,128)} %reshape_squeeze.3) | data formatting | bytes 9437184 | tf_op jit(solution)/shard_map/reshape;squeeze | solution.py:489
  17.6 5.1 %all-to-all-start = ((f32[4,4,192,384]{3,2,1,0:T(8,128)}), f32[4,4,192,384]{3,2,1,0:T(8,128)}, u32[]{:S(2)}, u32[]{:S(2)}) async-start(f32[4,4,192,384]{3,2,1,0:T(8,128)} %bitcast.18), calls=%async_computation | async-start | bytes 9437184 | tf_op jit(solution)/shard_map/all_to_all | solution.py:492
  24.7 6.9 %sort.23 = (s32[8192]{0:T(1024)S(1)}, f32[8192]{0:T(1024)}, s32[8192]{0:T(1024)}) sort(s32[8192]{0:T(1024)S(1)} %fusion.5, f32[8192]{0:T(1024)S(1)} %reshape.61, s32[8192]{0:T(1024)S(1)} %iota.19), dimensions={0}, to_apply=%region_0.1 | sort | flops 106496 | bytes 196608 | tf_op jit(solution)/shard_map/sort | solution.py:261
  33.4 1.2 compare_select_fusion.tile_ref
  34.6 3.0 %pack_lines.3 = (f32[6,192,128]{2,1,0:T(8,128)}, f32[6,192,128]{2,1,0:T(8,128)}, f32[6,192,128]{2,1,0:T(8,128)}, f32[6,192,128]{2,1,0:T(8,128)}) custom-call(s32[1]{0:T(128)} %bitcast.me_ref, f32[4,1,192,1536]{3,2,1,0:T(8,128)} %flow_ref.9), custom_call_target="tpu_custom_call" | custom-call | bytes 23592 | tf_op jit(solution)/shard_map/pack_lines/pallas_call | solution.py:118
  37.7 19.5 %collective-permute-done.2.rest_3_ = f32[6,192,128]{2,1,0:T(8,128)S(1)} collective-permute-done((f32[6,192,128]{2,1,0:T(8,128)}, f32[6,192,128]{2,1,0:T(8,128)S(1)}, u32[]{:S(2)}, u32[]{:S(2)}) %collective-permute-start.2) | collective-permute-done | bytes 589856 | tf_op jit(solution)/shard_map/ppermute | solution.py:478
  57.9 3.3 %collective-permute-start.4 = (f32[6,192,128]{2,1,0:T(8,128)}, f32[6,192,128]{2,1,0:T(8,128)}, u32[]{:S(2)}, u32[]{:S(2)}) collective-permute-start(f32[6,192,128]{2,1,0:T(8,128)} %get-tuple-element.108), channel_id=1, source_target_pairs={{0,2},{1,3},{2,0},{3,1},{4,6},{5,7},{6,4},{7,5},{8,10},{9,11},{10,... | collective-permute-start | bytes 1769480 | tf_op jit(solution)/shard_map/ppermute | solution.py:478
  61.3 1.3 fusion.18
  63.4 10.0 %line_slopes.2 = (f32[6,192,128]{2,1,0:T(8,128)}, f32[6,192,128]{2,1,0:T(8,128)}, f32[6,192,128]{2,1,0:T(8,128)}, f32[6,192,128]{2,1,0:T(8,128)}) custom-call(s32[1]{0:T(128)} %bitcast.me_ref, bf16[2,768,768]{2,1,0:T(8,128)(2,1)} %constant.112.clone.high_ref, bf16[2,768,768]{2,1,0:T(8,128)(2,1)} %constant.113.clone.low_ref, ...), custom_call_target="tpu_custom_call" | custom-call | flops 27179088 | bytes 117964 | tf_op jit(solution)/shard_map/line_slopes/pallas_call | solution.py:178
  75.1 5.7 %slab_terms.1 = (f32[4,3,192,384]{3,2,1,0:T(8,128)}, f32[4,192,384]{2,1,0:T(8,128)}) custom-call(f32[4,4,192,384]{3,2,1,0:T(8,128)} %all-to-all-done.in_ref), custom_call_target="tpu_custom_call" | custom-call | flops 188743 | bytes 94371 | tf_op jit(solution)/shard_map/slab_terms/pallas_call | solution.py:243
  80.9 3.9 %all-to-all-start.1 = ((f32[4,3,192,384]{3,2,1,0:T(8,128)}), f32[4,3,192,384]{3,2,1,0:T(8,128)S(1)}, u32[]{:S(2)}, u32[]{:S(2)}) async-start(f32[4,3,192,384]{3,2,1,0:T(8,128)} %get-tuple-element.141), calls=%async_computation.1 | async-start | bytes 7077888 | tf_op jit(solution)/shard_map/all_to_all | solution.py:492
  84.8 2.5 %collective-permute-done.4.rest_1_ = f32[6,192,128]{2,1,0:T(8,128)} collective-permute-done((f32[6,192,128]{2,1,0:T(8,128)}, f32[6,192,128]{2,1,0:T(8,128)}, u32[]{:S(2)}, u32[]{:S(2)}) %collective-permute-start.4) | collective-permute-done | bytes 589856 | tf_op jit(solution)/shard_map/ppermute | solution.py:478
  87.3 24.6 %collective-permute-done.5.rest_3_ = f32[6,192,128]{2,1,0:T(8,128)} collective-permute-done((f32[6,192,128]{2,1,0:T(8,128)}, f32[6,192,128]{2,1,0:T(8,128)}, u32[]{:S(2)}, u32[]{:S(2)}) %collective-permute-start.5) | collective-permute-done | bytes 589856 | tf_op jit(solution)/shard_map/ppermute | solution.py:478
  114.6 1.2 collective-permute-start.11
  116.3 10.1 %line_slopes.3 = (f32[3,192,128]{2,1,0:T(8,128)}, f32[3,192,128]{2,1,0:T(8,128)}, f32[3,192,128]{2,1,0:T(8,128)}, f32[3,192,128]{2,1,0:T(8,128)}, f32[3,192,128]...) custom-call(s32[1]{0:T(128)} %bitcast.me_ref, ...), custom_call_target="tpu_custom_call" | custom-call | flops 17666408448 | bytes 76677120 | tf_op jit(solution)/shard_map/line_slopes/pallas_call | solution.py:178
  126.4 10.2 %depth_terms.1 = (f32[3,192,1536]{2,1,0:T(8,128)}, f32[192,1536]{1,0:T(8,128)}) custom-call(f32[4,1,192,1536]{3,2,1,0:T(8,128)} %flow_ref.9, bf16[2,768,768]{2,1,0:T(8,128)(2,1)} %constant.112.clone.high_ref, bf16[2,768,768]{2,1,0:T(8,128)(2,1)} %constant.113.clone.low_ref), custom_call_target="tpu_custom_call" | custom-call | flops 54358180 | bytes 141557 | tf_op jit(solution)/shard_map/depth_terms/pallas_call | solution.py:216
  137.4 1.5 copy-done
  139.0 2.4 %sub.64.base_ref = f32[3,192,1536]{2,1,0:T(8,128)} subtract(f32[3,192,1536]{2,1,0:T(8,128)S(1)} %copy-done, f32[3,192,1536]{2,1,0:T(8,128)S(1)} %bitcast.19) | non-fusion elementwise | flops 884736 | bytes 10616832 | tf_op jit(solution)/shard_map/sub | solution.py:522
  141.4 23.0 %collective-permute-done.11.rest_8_.rest_12_.rest_3_ = f32[6,192,128]{2,1,0:T(8,128)} collective-permute-done((f32[6,192,128]{2,1,0:T(8,128)}, f32[6,192,128]{2,1,0:T(8,128)}, u32[]{:S(2)}, u32[]{:S(2)}) %collective-permute-start.11) | collective-permute-done | bytes 589856 | tf_op jit(solution)/shard_map/ppermute | solution.py:478
  164.4 3.4 %collective-permute-start.15 = (f32[3,192,128]{2,1,0:T(8,128)S(1)}, f32[3,192,128]{2,1,0:T(8,128)S(1)}, u32[]{:S(2)}, u32[]{:S(2)}) collective-permute-start(f32[3,192,128]{2,1,0:T(8,128)S(1)} %copy-done.18), channel_id=1, source_target_pairs={{0,4},{1,5},{2,6},{3,7},{4,0},{5,1},{6,2},{7,3},{8,12},{9,13},{10,... | collective-permute-start | bytes 884744 | tf_op jit(solution)/shard_map/ppermute | solution.py:478
  168.6 10.7 %home_step.3.rest_9_ = f32[3,1,192,1536]{3,2,1,0:T(8,128)} custom-call(s32[1]{0:T(128)} %bitcast.me_ref, s32[44]{0:T(128)} %copy-done.13, s32[44]{0:T(128)} %compare_select_fusion.tile_ref, f32[4,1,192,1536]{3,2,1,0:T(8,128)} %flow_ref.9, f32[3,192,1536]{2,1,0:T(8,128)} %sub.64.base_ref, s32[32,1,256]{2,1,0:T(1,128)} %bitcast.29, s32[32,1,256]{2,1,0:T(1,128)} %bitcast.26, ...), custom_call_target="tpu_custom_call" | custom-call | flops 44291848 | bytes 58982 | tf_op jit(solution)/shard_map/home_step/pallas_call | solution.py:444
  179.2 6.8 %collective-permute-done.15.rest_7_ = f32[3,192,128]{2,1,0:T(8,128)S(1)} collective-permute-done((f32[3,192,128]{2,1,0:T(8,128)S(1)}, f32[3,192,128]{2,1,0:T(8,128)S(1)}, u32[]{:S(2)}, u32[]{:S(2)}) %collective-permute-start.15) | collective-permute-done | bytes 294944 | tf_op jit(solution)/shard_map/ppermute | solution.py:478
  186.0 6.3 %collective-permute-done.17.rest_8_ = f32[3,192,128]{2,1,0:T(8,128)S(1)} collective-permute-done((f32[3,192,128]{2,1,0:T(8,128)S(1)}, f32[3,192,128]{2,1,0:T(8,128)S(1)}, u32[]{:S(2)}, u32[]{:S(2)}) %collective-permute-start.17) | collective-permute-done | bytes 294944 | tf_op jit(solution)/shard_map/ppermute | solution.py:478
  192.3 3.4 %collective-permute-start.19 = (f32[3,192,128]{2,1,0:T(8,128)S(1)}, f32[3,192,128]{2,1,0:T(8,128)}, u32[]{:S(2)}, u32[]{:S(2)}) collective-permute-start(f32[3,192,128]{2,1,0:T(8,128)S(1)} %copy-done.15), channel_id=1, source_target_pairs={{0,2},{1,3},{2,0},{3,1},{4,6},{5,7},{6,4},{7,5},{8,10},{9,11},{10,... | collective-permute-start | bytes 884744 | tf_op jit(solution)/shard_map/ppermute | solution.py:478
  195.7 10.3 %home_step.4.rest_9_ = f32[3,1,192,1536]{3,2,1,0:T(8,128)} custom-call(s32[1]{0:T(128)} %bitcast.me_ref, s32[44]{0:T(128)} %copy-done.13, s32[44]{0:T(128)} %compare_select_fusion.tile_ref, f32[4,1,192,1536]{3,2,1,0:T(8,128)} %flow_ref.9, f32[3,192,1536]{2,1,0:T(8,128)} %sub.64.base_ref, s32[32,1,256]{2,1,0:T(1,128)} %bitcast.30, ...), custom_call_target="tpu_custom_call", output_to_operand_aliasing={{}: (14, {})} | custom-call | flops 44291848 | bytes 58982 | tf_op jit(solution)/shard_map/home_step/pallas_call | solution.py:444
  206.0 2.9 %home_divergence.1 = f32[4,192,384]{2,1,0:T(8,128)} custom-call(s32[1]{0:T(128)} %bitcast.me_ref, f32[192,1536]{1,0:T(8,128)} %get-tuple-element.176.slope_ref, f32[6,192,128]{2,1,0:T(8,128)} %get-tuple-element.157.rest_5_.rest_9_.rest_0_, f32[6,192,128]{2,1,0:T(8,128)} %collective-permute-done.10.rest_6_.rest_10_.rest_1_, ...), custom_call_target="tpu_custom_call" | custom-call | bytes 35389 | tf_op jit(solution)/shard_map/home_divergence/pallas_call | solution.py:314
  209.0 3.5 %all-to-all-start.2 = ((f32[4,192,384]{2,1,0:T(8,128)}), f32[4,192,384]{2,1,0:T(8,128)S(1)}, u32[]{:S(2)}, u32[]{:S(2)}) async-start(f32[4,192,384]{2,1,0:T(8,128)} %home_divergence.1), calls=%async_computation.2 | async-start | bytes 2359296 | tf_op jit(solution)/shard_map/all_to_all | solution.py:492
  212.5 8.4 %collective-permute-done.20.rest_8_ = f32[3,192,128]{2,1,0:T(8,128)} collective-permute-done((f32[3,192,128]{2,1,0:T(8,128)S(1)}, f32[3,192,128]{2,1,0:T(8,128)}, u32[]{:S(2)}, u32[]{:S(2)}) %collective-permute-start.20) | collective-permute-done | bytes 294944 | tf_op jit(solution)/shard_map/ppermute | solution.py:478
  220.9 10.0 %home_step.5 = f32[3,1,192,1536]{3,2,1,0:T(8,128)} custom-call(s32[1]{0:T(128)} %bitcast.me_ref, s32[44]{0:T(128)} %copy-done.13, s32[44]{0:T(128)} %compare_select_fusion.tile_ref, f32[4,1,192,1536]{3,2,1,0:T(8,128)} %flow_ref.9, f32[3,192,1536]{2,1,0:T(8,128)} %sub.64.base_ref, s32[32,1,256]{2,1,0:T(1,128)} %bitcast.31, ...), custom_call_target="tpu_custom_call", output_to_operand_aliasing={{}: (14, {})} | custom-call | flops 44291850240 | bytes 58982400 | tf_op jit(solution)/shard_map/home_step/pallas_call | solution.py:444
  (101 shorter events, 13.4 us)
Async XLA Ops:
  3.6 34.0 %collective-permute-start = (f32[6,192,128]{2,1,0:T(8,128)}, f32[6,192,128]{2,1,0:T(8,128)S(1)}, u32[]{:S(2)}, u32[]{:S(2)}) collective-permute-start(f32[6,192,128]{2,1,0:T(8,128)} %get-tuple-element.92), channel_id=1, source_target_pairs={{0,4},{1,5},{2,6},{3,7},{4,0},{5,1},{6,2},{7,3},{8,12},{9,13},{10,... | collective-permute-start | bytes 1769480 | tf_op jit(solution)/shard_map/ppermute | solution.py:478
  6.0 31.6 %collective-permute-start.1 = (f32[6,192,128]{2,1,0:T(8,128)}, f32[6,192,128]{2,1,0:T(8,128)S(1)}, u32[]{:S(2)}, u32[]{:S(2)}) collective-permute-start(f32[6,192,128]{2,1,0:T(8,128)} %get-tuple-element.93), channel_id=1, source_target_pairs={{0,2},{1,3},{2,0},{3,1},{4,6},{5,7},{6,4},{7,5},{8,10},{9,11},{10,... | collective-permute-start | bytes 1769480 | tf_op jit(solution)/shard_map/ppermute | solution.py:478
  6.2 51.0 %collective-permute-start.2 = (f32[6,192,128]{2,1,0:T(8,128)}, f32[6,192,128]{2,1,0:T(8,128)S(1)}, u32[]{:S(2)}, u32[]{:S(2)}) collective-permute-start(f32[6,192,128]{2,1,0:T(8,128)} %get-tuple-element.94), channel_id=1, source_target_pairs={{0,6},{1,7},{2,4},{3,5},{4,2},{5,3},{6,0},{7,1},{8,14},{9,15},{10,... | collective-permute-start | bytes 1769480 | tf_op jit(solution)/shard_map/ppermute | solution.py:478
  17.6 57.6 %all-to-all-start = ((f32[4,4,192,384]{3,2,1,0:T(8,128)}), f32[4,4,192,384]{3,2,1,0:T(8,128)}, u32[]{:S(2)}, u32[]{:S(2)}) async-start(f32[4,4,192,384]{3,2,1,0:T(8,128)} %bitcast.18), calls=%async_computation | async-start | bytes 9437184 | tf_op jit(solution)/shard_map/all_to_all | solution.py:492
  32.8 24.5 %copy-start.13 = (s32[44]{0:T(128)}, s32[44]{0:T(128)S(1)}, u32[]{:S(2)}) copy-start(s32[44]{0:T(128)S(1)} %broadcast_minimum_fusion.chunk_ref) | copy-start | bytes 532
  37.6 24.9 %copy-start.1 = (f32[6,192,128]{2,1,0:T(8,128)}, f32[6,192,128]{2,1,0:T(8,128)S(1)}, u32[]{:S(2)}) copy-start(f32[6,192,128]{2,1,0:T(8,128)S(1)} %collective-permute-done.rest_2_) | copy-start | bytes 1769476
  37.6 24.9 %copy-start.2 = (f32[6,192,128]{2,1,0:T(8,128)}, f32[6,192,128]{2,1,0:T(8,128)S(1)}, u32[]{:S(2)}) copy-start(f32[6,192,128]{2,1,0:T(8,128)S(1)} %collective-permute-done.1.rest_1_) | copy-start | bytes 1769476
  57.3 4.0 %collective-permute-start.7 = (f32[18,192,128]{2,1,0:T(8,128)S(1)}, f32[18,192,128]{2,1,0:T(8,128)S(1)}, u32[]{:S(2)}, u32[]{:S(2)}) collective-permute-start(f32[18,192,128]{2,1,0:T(8,128)S(1)} %pad_maximum_fusion), channel_id=1, source_target_pairs={{0,1},{1,0},{2,3},{3,2},{4,5},{5,4},{6,7},{7,6},{8,9},{9,8},{10,11... | collective-permute-start | bytes 5308424 | tf_op jit(solution)/shard_map/ppermute | solution.py:482
  57.9 4.7 %collective-permute-start.6 = (f32[6,192,128]{2,1,0:T(8,128)S(1)}, f32[6,192,128]{2,1,0:T(8,128)S(1)}, u32[]{:S(2)}, u32[]{:S(2)}) collective-permute-start(f32[6,192,128]{2,1,0:T(8,128)S(1)} %copy-done.5), channel_id=1, source_target_pairs={{0,1},{1,0},{2,3},{3,2},{4,5},{5,4},{6,7},{7,6},{8,9},{9,8},{10,11... | collective-permute-start | bytes 1769480 | tf_op jit(solution)/shard_map/ppermute | solution.py:482
  57.9 26.8 %collective-permute-start.3 = (f32[6,192,128]{2,1,0:T(8,128)}, f32[6,192,128]{2,1,0:T(8,128)}, u32[]{:S(2)}, u32[]{:S(2)}) collective-permute-start(f32[6,192,128]{2,1,0:T(8,128)} %get-tuple-element.107), channel_id=1, source_target_pairs={{0,4},{1,5},{2,6},{3,7},{4,0},{5,1},{6,2},{7,3},{8,12},{9,13},{10,... | collective-permute-start | bytes 1769480 | tf_op jit(solution)/shard_map/ppermute | solution.py:478
  57.9 29.4 %collective-permute-start.4 = (f32[6,192,128]{2,1,0:T(8,128)}, f32[6,192,128]{2,1,0:T(8,128)}, u32[]{:S(2)}, u32[]{:S(2)}) collective-permute-start(f32[6,192,128]{2,1,0:T(8,128)} %get-tuple-element.108), channel_id=1, source_target_pairs={{0,2},{1,3},{2,0},{3,1},{4,6},{5,7},{6,4},{7,5},{8,10},{9,11},{10,... | collective-permute-start | bytes 1769480 | tf_op jit(solution)/shard_map/ppermute | solution.py:478
  61.3 50.7 %collective-permute-start.5 = (f32[6,192,128]{2,1,0:T(8,128)}, f32[6,192,128]{2,1,0:T(8,128)}, u32[]{:S(2)}, u32[]{:S(2)}) collective-permute-start(f32[6,192,128]{2,1,0:T(8,128)} %get-tuple-element.109), channel_id=1, source_target_pairs={{0,6},{1,7},{2,4},{3,5},{4,2},{5,3},{6,0},{7,1},{8,14},{9,15},{10,... | collective-permute-start | bytes 1769480 | tf_op jit(solution)/shard_map/ppermute | solution.py:478
  73.4 38.5 %collective-permute-start.8 = (f32[6,192,128]{2,1,0:T(8,128)}, f32[6,192,128]{2,1,0:T(8,128)}, u32[]{:S(2)}, u32[]{:S(2)}) collective-permute-start(f32[6,192,128]{2,1,0:T(8,128)} %get-tuple-element.126.rest_0_), channel_id=1, source_target_pairs={{0,1},{1,0},{2,3},{3,2},{4,5},{5,4},{6,7},{7,6},{8,9},{9,8},{10,11... | collective-permute-start | bytes 1769480 | tf_op jit(solution)/shard_map/ppermute | solution.py:482
  80.9 55.8 %all-to-all-start.1 = ((f32[4,3,192,384]{3,2,1,0:T(8,128)}), f32[4,3,192,384]{3,2,1,0:T(8,128)S(1)}, u32[]{:S(2)}, u32[]{:S(2)}) async-start(f32[4,3,192,384]{3,2,1,0:T(8,128)} %get-tuple-element.141), calls=%async_computation.1 | async-start | bytes 7077888 | tf_op jit(solution)/shard_map/all_to_all | solution.py:492
  111.9 2.7 %collective-permute-start.12 = (f32[6,192,128]{2,1,0:T(8,128)}, f32[6,192,128]{2,1,0:T(8,128)}, u32[]{:S(2)}, u32[]{:S(2)}) collective-permute-start(f32[6,192,128]{2,1,0:T(8,128)} %collective-permute-done.4.rest_1_), channel_id=1, source_target_pairs={{0,1},{1,0},{2,3},{3,2},{4,5},{5,4},{6,7},{7,6},{8,9},{9,8},{10,11... | collective-permute-start | bytes 1769480 | tf_op jit(solution)/shard_map/ppermute | solution.py:482
  112.6 3.2 %collective-permute-start.13 = (f32[6,192,128]{2,1,0:T(8,128)}, f32[6,192,128]{2,1,0:T(8,128)}, u32[]{:S(2)}, u32[]{:S(2)}) collective-permute-start(f32[6,192,128]{2,1,0:T(8,128)} %collective-permute-done.3.rest_2_), channel_id=1, source_target_pairs={{0,1},{1,0},{2,3},{3,2},{4,5},{5,4},{6,7},{7,6},{8,9},{9,8},{10,11... | collective-permute-start | bytes 1769480 | tf_op jit(solution)/shard_map/ppermute | solution.py:482
  112.6 3.7 %collective-permute-start.14 = (f32[6,192,128]{2,1,0:T(8,128)}, f32[6,192,128]{2,1,0:T(8,128)}, u32[]{:S(2)}, u32[]{:S(2)}) collective-permute-start(f32[6,192,128]{2,1,0:T(8,128)} %collective-permute-done.5.rest_3_), channel_id=1, source_target_pairs={{0,1},{1,0},{2,3},{3,2},{4,5},{5,4},{6,7},{7,6},{8,9},{9,8},{10,11... | collective-permute-start | bytes 1769480 | tf_op jit(solution)/shard_map/ppermute | solution.py:482
  113.2 28.2 %collective-permute-start.9 = (f32[6,192,128]{2,1,0:T(8,128)}, f32[6,192,128]{2,1,0:T(8,128)}, u32[]{:S(2)}, u32[]{:S(2)}) collective-permute-start(f32[6,192,128]{2,1,0:T(8,128)} %get-tuple-element.123), channel_id=1, source_target_pairs={{0,4},{1,5},{2,6},{3,7},{4,0},{5,1},{6,2},{7,3},{8,12},{9,13},{10,... | collective-permute-start | bytes 1769480 | tf_op jit(solution)/shard_map/ppermute | solution.py:478
  113.2 28.2 %collective-permute-start.10 = (f32[6,192,128]{2,1,0:T(8,128)}, f32[6,192,128]{2,1,0:T(8,128)}, u32[]{:S(2)}, u32[]{:S(2)}) collective-permute-start(f32[6,192,128]{2,1,0:T(8,128)} %get-tuple-element.124), channel_id=1, source_target_pairs={{0,2},{1,3},{2,0},{3,1},{4,6},{5,7},{6,4},{7,5},{8,10},{9,11},{10,... | collective-permute-start | bytes 1769480 | tf_op jit(solution)/shard_map/ppermute | solution.py:478
  114.6 49.8 %collective-permute-start.11 = (f32[6,192,128]{2,1,0:T(8,128)}, f32[6,192,128]{2,1,0:T(8,128)}, u32[]{:S(2)}, u32[]{:S(2)}) collective-permute-start(f32[6,192,128]{2,1,0:T(8,128)} %get-tuple-element.125), channel_id=1, source_target_pairs={{0,6},{1,7},{2,4},{3,5},{4,2},{5,3},{6,0},{7,1},{8,14},{9,15},{10,... | collective-permute-start | bytes 1769480 | tf_op jit(solution)/shard_map/ppermute | solution.py:478
  138.9 25.5 %copy-start.19 = (f32[3,192,128]{2,1,0:T(8,128)S(1)}, f32[3,192,128]{2,1,0:T(8,128)}, u32[]{:S(2)}) copy-start(f32[3,192,128]{2,1,0:T(8,128)} %get-tuple-element.149) | copy-start | bytes 884740
  138.9 25.5 %copy-start.18 = (f32[3,192,128]{2,1,0:T(8,128)S(1)}, f32[3,192,128]{2,1,0:T(8,128)}, u32[]{:S(2)}) copy-start(f32[3,192,128]{2,1,0:T(8,128)} %get-tuple-element.150) | copy-start | bytes 884740
  138.9 28.8 %copy-start.17 = (f32[3,192,128]{2,1,0:T(8,128)S(1)}, f32[3,192,128]{2,1,0:T(8,128)}, u32[]{:S(2)}) copy-start(f32[3,192,128]{2,1,0:T(8,128)} %get-tuple-element.151) | copy-start | bytes 884740
  138.9 28.9 %copy-start.12 = (s32[1,192,12]{1,0,2:T(1,128)S(1)}, s32[1,192,12]{1,0,2:T(1,128)}, u32[]{:S(2)}) copy-start(s32[1,192,12]{1,0,2:T(1,128)} %param.9) | copy-start | bytes 27652
  164.4 14.8 %collective-permute-start.16 = (f32[3,192,128]{2,1,0:T(8,128)S(1)}, f32[3,192,128]{2,1,0:T(8,128)S(1)}, u32[]{:S(2)}, u32[]{:S(2)}) collective-permute-start(f32[3,192,128]{2,1,0:T(8,128)S(1)} %copy-done.19), channel_id=1, source_target_pairs={{0,2},{1,3},{2,0},{3,1},{4,6},{5,7},{6,4},{7,5},{8,10},{9,11},{10,... | collective-permute-start | bytes 884744 | tf_op jit(solution)/shard_map/ppermute | solution.py:478
  164.4 21.6 %collective-permute-start.15 = (f32[3,192,128]{2,1,0:T(8,128)S(1)}, f32[3,192,128]{2,1,0:T(8,128)S(1)}, u32[]{:S(2)}, u32[]{:S(2)}) collective-permute-start(f32[3,192,128]{2,1,0:T(8,128)S(1)} %copy-done.18), channel_id=1, source_target_pairs={{0,4},{1,5},{2,6},{3,7},{4,0},{5,1},{6,2},{7,3},{8,12},{9,13},{10,... | collective-permute-start | bytes 884744 | tf_op jit(solution)/shard_map/ppermute | solution.py:478
  167.8 24.5 %collective-permute-start.17 = (f32[3,192,128]{2,1,0:T(8,128)S(1)}, f32[3,192,128]{2,1,0:T(8,128)S(1)}, u32[]{:S(2)}, u32[]{:S(2)}) collective-permute-start(f32[3,192,128]{2,1,0:T(8,128)S(1)} %copy-done.17), channel_id=1, source_target_pairs={{0,6},{1,7},{2,4},{3,5},{4,2},{5,3},{6,0},{7,1},{8,14},{9,15},{10,... | collective-permute-start | bytes 884744 | tf_op jit(solution)/shard_map/ppermute | solution.py:478
  168.6 27.1 %copy-start.14 = (f32[3,192,128]{2,1,0:T(8,128)S(1)}, f32[3,192,128]{2,1,0:T(8,128)}, u32[]{:S(2)}) copy-start(f32[3,192,128]{2,1,0:T(8,128)} %get-tuple-element.164) | copy-start | bytes 884740
  192.3 20.2 %collective-permute-start.18 = (f32[3,192,128]{2,1,0:T(8,128)S(1)}, f32[3,192,128]{2,1,0:T(8,128)S(1)}, u32[]{:S(2)}, u32[]{:S(2)}) collective-permute-start(f32[3,192,128]{2,1,0:T(8,128)S(1)} %copy-done.16), channel_id=1, source_target_pairs={{0,4},{1,5},{2,6},{3,7},{4,0},{5,1},{6,2},{7,3},{8,12},{9,13},{10,... | collective-permute-start | bytes 884744 | tf_op jit(solution)/shard_map/ppermute | solution.py:478
  192.3 20.2 %collective-permute-start.19 = (f32[3,192,128]{2,1,0:T(8,128)S(1)}, f32[3,192,128]{2,1,0:T(8,128)}, u32[]{:S(2)}, u32[]{:S(2)}) collective-permute-start(f32[3,192,128]{2,1,0:T(8,128)S(1)} %copy-done.15), channel_id=1, source_target_pairs={{0,2},{1,3},{2,0},{3,1},{4,6},{5,7},{6,4},{7,5},{8,10},{9,11},{10,... | collective-permute-start | bytes 884744 | tf_op jit(solution)/shard_map/ppermute | solution.py:478
  195.7 25.2 %collective-permute-start.20 = (f32[3,192,128]{2,1,0:T(8,128)S(1)}, f32[3,192,128]{2,1,0:T(8,128)}, u32[]{:S(2)}, u32[]{:S(2)}) collective-permute-start(f32[3,192,128]{2,1,0:T(8,128)S(1)} %copy-done.14), channel_id=1, source_target_pairs={{0,6},{1,7},{2,4},{3,5},{4,2},{5,3},{6,0},{7,1},{8,14},{9,15},{10,... | collective-permute-start | bytes 884744 | tf_op jit(solution)/shard_map/ppermute | solution.py:478
  209.0 22.0 %all-to-all-start.2 = ((f32[4,192,384]{2,1,0:T(8,128)}), f32[4,192,384]{2,1,0:T(8,128)S(1)}, u32[]{:S(2)}, u32[]{:S(2)}) async-start(f32[4,192,384]{2,1,0:T(8,128)} %home_divergence.1), calls=%async_computation.2 | async-start | bytes 2359296 | tf_op jit(solution)/shard_map/all_to_all | solution.py:492
  (13 other events, 147.2 us)

commit v6 on v5

--- a/solution.py
+++ b/solution.py
@@ -401,7 +401,7 @@
             low_part = jnp.where(lane_key == key(m % LANES), one, zero)
             return total + dot_t(jnp.concatenate(two_terms(share), axis=0), low_part)
 
-        sampled = lax.fori_loop(0, chunks, add_up, jnp.zeros((2 * marker_rows, LANES), F32), unroll=8)
+        sampled = lax.fori_loop(0, chunks, add_up, jnp.zeros((2 * marker_rows, LANES), F32), unroll=16)
         sampled = jnp.concatenate(two_terms(sampled[:marker_rows] + sampled[marker_rows:]), axis=0)
 
         def spread(c, carry):
@@ -411,7 +411,7 @@
             found[c] = jnp.sum(both, axis=0, keepdims=True) * weight_ref[c]
             return carry
 
-        lax.fori_loop(0, chunks, spread, 0, unroll=8)
+        lax.fori_loop(0, chunks, spread, 0, unroll=16)
 
         def scatter(i, carry):
             c, t, row, lanes_hit = pair(i)
@@ -525,7 +525,7 @@
     step = functools.partial(home_step, plan, me=pen_at, flow=flow, base=base, order=order, solid=solid_blocks[0])
     back = send_lines(slopes[0])
     out = step(1, groups=groups, out=None)
-    slopes, back, out = together((slopes, back, out))
+    back, slopes, out = together((back, slopes, out))
     groups = groups + [(cut[0], back)]
     if len(cut) > 1:
         back = send_lines(slopes[1])

time: 233 us -> 231 us (level)
  no operation moved by 1% of the time
where the time goes in v6:
time: 231 us; the launch traced here: 229 us
  waiting for transfers between devices  92.7 us (40%)
  Pallas kernels  74.3 us (32%)
  starting transfers between devices  29.2 us (13%)
  local copies, waits for them, and re-layouts  18.5 us (8%)
  other arithmetic  13.5 us (6%)
    ppermute x15, waiting for transfers between devices, send_lines(): lax.ppermute(blocks[s], 'pen', [(i, plan.to(i // CORES, s) * CORES + i %...  90.5 us
    pallas_call x3, Pallas kernels, home_step(): pl.pallas_call(kernel, out_shape=jax.ShapeDtypeStruct((3, 1, rows, depth)...  29.3 us
    pallas_call x2, Pallas kernels, line_slopes(): pl.pallas_call(kernel, out_shape=shapes, in_specs=[SMEM, VMEM, VMEM] + [H...  20.1 us
    ppermute x15, starting transfers between devices, send_lines(): lax.ppermute(blocks[s], 'pen', [(i, plan.to(i // CORES, s) * CORES + i %...  13.7 us
    all_to_all x3, starting transfers between devices, exchange(): return lax.all_to_all(value, 'grp', 0, 0, tiled=True)  12.5 us
    another operation x2, local copies, waits for them, and re-layouts, cut_depth(): return jnp.moveaxis(value.reshape(*value.shape[:-1], grps, width), -2, 0)  11.2 us
    pallas_call x1, Pallas kernels, depth_terms(): pl.pallas_call(kernel, grid=(rows // step,), out_shape=[jax.ShapeDtypeStr...  10.2 us
    sort x1, other arithmetic, marker_order(): key, weight = lax.sort((place * markers + marker, weight), num_keys=1)  6.91 us
  transfers between devices with their start and end apart: 24, of which 10 were waited for; matrix products, arithmetic and copies ran while one was open for 12% of the time, Pallas kernels for 31%

profile of v6, /device:TPU:9, one launch (start us, length us, event | category | flops | bytes accessed | tf_op | source)
XLA Modules:
  0.0 229.2 jit_solution(424185833798246148)
XLA Ops:
  0.6 3.0 %pack_lines.2 = (f32[6,192,128]{2,1,0:T(8,128)}, f32[6,192,128]{2,1,0:T(8,128)}, f32[6,192,128]{2,1,0:T(8,128)}, f32[6,192,128]{2,1,0:T(8,128)}) custom-call(s32[1]{0:T(128)} %bitcast.me_ref, f32[4,1,192,1536]{3,2,1,0:T(8,128)} %flow_ref.9), custom_call_target="tpu_custom_call" | custom-call | bytes 23592 | tf_op jit(solution)/shard_map/pack_lines/pallas_call | solution.py:118
  3.6 2.4 %collective-permute-start = (f32[6,192,128]{2,1,0:T(8,128)}, f32[6,192,128]{2,1,0:T(8,128)S(1)}, u32[]{:S(2)}, u32[]{:S(2)}) collective-permute-start(f32[6,192,128]{2,1,0:T(8,128)} %get-tuple-element.92), channel_id=1, source_target_pairs={{0,4},{1,5},{2,6},{3,7},{4,0},{5,1},{6,2},{7,3},{8,12},{9,13},{10,... | collective-permute-start | bytes 1769480 | tf_op jit(solution)/shard_map/ppermute | solution.py:478
  6.3 6.2 %reshape_squeeze.3 = f32[4,192,4,384]{3,2,1,0:T(4,128)} reshape(f32[4,1,192,1536]{3,2,1,0:T(8,128)} %flow_ref.9) | data formatting | bytes 9437184 | tf_op jit(solution)/shard_map/reshape;squeeze | solution.py:489
  12.5 5.0 %copy.36 = f32[4,192,4,384]{3,1,0,2:T(8,128)} copy(f32[4,192,4,384]{3,2,1,0:T(4,128)} %reshape_squeeze.3) | data formatting | bytes 9437184 | tf_op jit(solution)/shard_map/reshape;squeeze | solution.py:489
  17.6 5.1 %all-to-all-start = ((f32[4,4,192,384]{3,2,1,0:T(8,128)}), f32[4,4,192,384]{3,2,1,0:T(8,128)}, u32[]{:S(2)}, u32[]{:S(2)}) async-start(f32[4,4,192,384]{3,2,1,0:T(8,128)} %bitcast.18), calls=%async_computation | async-start | bytes 9437184 | tf_op jit(solution)/shard_map/all_to_all | solution.py:492
  24.7 6.9 %sort.23 = (s32[8192]{0:T(1024)S(1)}, f32[8192]{0:T(1024)}, s32[8192]{0:T(1024)}) sort(s32[8192]{0:T(1024)S(1)} %fusion.5, f32[8192]{0:T(1024)S(1)} %reshape.61, s32[8192]{0:T(1024)S(1)} %iota.19), dimensions={0}, to_apply=%region_0.1 | sort | flops 106496 | bytes 196608 | tf_op jit(solution)/shard_map/sort | solution.py:261
  33.4 1.2 compare_select_fusion.tile_ref
  34.6 3.0 %pack_lines.3 = (f32[6,192,128]{2,1,0:T(8,128)}, f32[6,192,128]{2,1,0:T(8,128)}, f32[6,192,128]{2,1,0:T(8,128)}, f32[6,192,128]{2,1,0:T(8,128)}) custom-call(s32[1]{0:T(128)} %bitcast.me_ref, f32[4,1,192,1536]{3,2,1,0:T(8,128)} %flow_ref.9), custom_call_target="tpu_custom_call" | custom-call | bytes 23592 | tf_op jit(solution)/shard_map/pack_lines/pallas_call | solution.py:118
  37.7 19.5 %collective-permute-done.2.rest_3_ = f32[6,192,128]{2,1,0:T(8,128)S(1)} collective-permute-done((f32[6,192,128]{2,1,0:T(8,128)}, f32[6,192,128]{2,1,0:T(8,128)S(1)}, u32[]{:S(2)}, u32[]{:S(2)}) %collective-permute-start.2) | collective-permute-done | bytes 589856 | tf_op jit(solution)/shard_map/ppermute | solution.py:478
  57.9 3.3 %collective-permute-start.4 = (f32[6,192,128]{2,1,0:T(8,128)}, f32[6,192,128]{2,1,0:T(8,128)}, u32[]{:S(2)}, u32[]{:S(2)}) collective-permute-start(f32[6,192,128]{2,1,0:T(8,128)} %get-tuple-element.108), channel_id=1, source_target_pairs={{0,2},{1,3},{2,0},{3,1},{4,6},{5,7},{6,4},{7,5},{8,10},{9,11},{10,... | collective-permute-start | bytes 1769480 | tf_op jit(solution)/shard_map/ppermute | solution.py:478
  61.3 1.3 fusion.18
  63.4 10.0 %line_slopes.2 = (f32[6,192,128]{2,1,0:T(8,128)}, f32[6,192,128]{2,1,0:T(8,128)}, f32[6,192,128]{2,1,0:T(8,128)}, f32[6,192,128]{2,1,0:T(8,128)}) custom-call(s32[1]{0:T(128)} %bitcast.me_ref, bf16[2,768,768]{2,1,0:T(8,128)(2,1)} %constant.112.clone.high_ref, bf16[2,768,768]{2,1,0:T(8,128)(2,1)} %constant.113.clone.low_ref, ...), custom_call_target="tpu_custom_call" | custom-call | flops 27179088 | bytes 117964 | tf_op jit(solution)/shard_map/line_slopes/pallas_call | solution.py:178
  75.1 5.7 %slab_terms.1 = (f32[4,3,192,384]{3,2,1,0:T(8,128)}, f32[4,192,384]{2,1,0:T(8,128)}) custom-call(f32[4,4,192,384]{3,2,1,0:T(8,128)} %all-to-all-done.in_ref), custom_call_target="tpu_custom_call" | custom-call | flops 188743 | bytes 94371 | tf_op jit(solution)/shard_map/slab_terms/pallas_call | solution.py:243
  80.9 3.9 %all-to-all-start.1 = ((f32[4,3,192,384]{3,2,1,0:T(8,128)}), f32[4,3,192,384]{3,2,1,0:T(8,128)S(1)}, u32[]{:S(2)}, u32[]{:S(2)}) async-start(f32[4,3,192,384]{3,2,1,0:T(8,128)} %get-tuple-element.141), calls=%async_computation.1 | async-start | bytes 7077888 | tf_op jit(solution)/shard_map/all_to_all | solution.py:492
  84.8 2.5 %collective-permute-done.4.rest_1_ = f32[6,192,128]{2,1,0:T(8,128)} collective-permute-done((f32[6,192,128]{2,1,0:T(8,128)}, f32[6,192,128]{2,1,0:T(8,128)}, u32[]{:S(2)}, u32[]{:S(2)}) %collective-permute-start.4) | collective-permute-done | bytes 589856 | tf_op jit(solution)/shard_map/ppermute | solution.py:478
  87.3 24.6 %collective-permute-done.5.rest_3_ = f32[6,192,128]{2,1,0:T(8,128)} collective-permute-done((f32[6,192,128]{2,1,0:T(8,128)}, f32[6,192,128]{2,1,0:T(8,128)}, u32[]{:S(2)}, u32[]{:S(2)}) %collective-permute-start.5) | collective-permute-done | bytes 589856 | tf_op jit(solution)/shard_map/ppermute | solution.py:478
  114.6 1.2 collective-permute-start.11
  116.3 10.1 %line_slopes.3 = (f32[3,192,128]{2,1,0:T(8,128)}, f32[3,192,128]{2,1,0:T(8,128)}, f32[3,192,128]{2,1,0:T(8,128)}, f32[3,192,128]{2,1,0:T(8,128)}, f32[3,192,128]...) custom-call(s32[1]{0:T(128)} %bitcast.me_ref, ...), custom_call_target="tpu_custom_call" | custom-call | flops 17666408448 | bytes 76677120 | tf_op jit(solution)/shard_map/line_slopes/pallas_call | solution.py:178
  126.4 10.2 %depth_terms.1 = (f32[3,192,1536]{2,1,0:T(8,128)}, f32[192,1536]{1,0:T(8,128)}) custom-call(f32[4,1,192,1536]{3,2,1,0:T(8,128)} %flow_ref.9, bf16[2,768,768]{2,1,0:T(8,128)(2,1)} %constant.112.clone.high_ref, bf16[2,768,768]{2,1,0:T(8,128)(2,1)} %constant.113.clone.low_ref), custom_call_target="tpu_custom_call" | custom-call | flops 54358180 | bytes 141557 | tf_op jit(solution)/shard_map/depth_terms/pallas_call | solution.py:216
  137.4 1.5 copy-done
  139.0 2.4 %sub.64.base_ref = f32[3,192,1536]{2,1,0:T(8,128)} subtract(f32[3,192,1536]{2,1,0:T(8,128)S(1)} %copy-done, f32[3,192,1536]{2,1,0:T(8,128)S(1)} %bitcast.19) | non-fusion elementwise | flops 884736 | bytes 10616832 | tf_op jit(solution)/shard_map/sub | solution.py:522
  141.4 23.0 %collective-permute-done.11.rest_8_.rest_12_.rest_3_ = f32[6,192,128]{2,1,0:T(8,128)} collective-permute-done((f32[6,192,128]{2,1,0:T(8,128)}, f32[6,192,128]{2,1,0:T(8,128)}, u32[]{:S(2)}, u32[]{:S(2)}) %collective-permute-start.11) | collective-permute-done | bytes 589856 | tf_op jit(solution)/shard_map/ppermute | solution.py:478
  164.4 3.4 %collective-permute-start.16 = (f32[3,192,128]{2,1,0:T(8,128)S(1)}, f32[3,192,128]{2,1,0:T(8,128)S(1)}, u32[]{:S(2)}, u32[]{:S(2)}) collective-permute-start(f32[3,192,128]{2,1,0:T(8,128)S(1)} %copy-done.18), channel_id=1, source_target_pairs={{0,2},{1,3},{2,0},{3,1},{4,6},{5,7},{6,4},{7,5},{8,10},{9,11},{10,... | collective-permute-start | bytes 884744 | tf_op jit(solution)/shard_map/ppermute | solution.py:478
  168.6 10.1 %home_step.3.rest_9_ = f32[3,1,192,1536]{3,2,1,0:T(8,128)} custom-call(s32[1]{0:T(128)} %bitcast.me_ref, s32[44]{0:T(128)} %copy-done.13, s32[44]{0:T(128)} %compare_select_fusion.tile_ref, f32[4,1,192,1536]{3,2,1,0:T(8,128)} %flow_ref.9, f32[3,192,1536]{2,1,0:T(8,128)} %sub.64.base_ref, s32[32,1,256]{2,1,0:T(1,128)} %bitcast.29, s32[32,1,256]{2,1,0:T(1,128)} %bitcast.26, ...), custom_call_target="tpu_custom_call" | custom-call | flops 44291848 | bytes 58982 | tf_op jit(solution)/shard_map/home_step/pallas_call | solution.py:444
  178.7 2.0 collective-permute-done.16.rest_6_
  180.7 12.2 %collective-permute-done.17.rest_8_ = f32[3,192,128]{2,1,0:T(8,128)S(1)} collective-permute-done((f32[3,192,128]{2,1,0:T(8,128)S(1)}, f32[3,192,128]{2,1,0:T(8,128)S(1)}, u32[]{:S(2)}, u32[]{:S(2)}) %collective-permute-start.17) | collective-permute-done | bytes 294944 | tf_op jit(solution)/shard_map/ppermute | solution.py:478
  193.4 2.2 collective-permute-start.20
  195.6 9.7 %home_step.4.rest_9_ = f32[3,1,192,1536]{3,2,1,0:T(8,128)} custom-call(s32[1]{0:T(128)} %bitcast.me_ref, s32[44]{0:T(128)} %copy-done.13, s32[44]{0:T(128)} %compare_select_fusion.tile_ref, f32[4,1,192,1536]{3,2,1,0:T(8,128)} %flow_ref.9, f32[3,192,1536]{2,1,0:T(8,128)} %sub.64.base_ref, s32[32,1,256]{2,1,0:T(1,128)} %bitcast.30, ...), custom_call_target="tpu_custom_call", output_to_operand_aliasing={{}: (14, {})} | custom-call | flops 44291848 | bytes 58982 | tf_op jit(solution)/shard_map/home_step/pallas_call | solution.py:444
  205.3 2.9 %home_divergence.1 = f32[4,192,384]{2,1,0:T(8,128)} custom-call(s32[1]{0:T(128)} %bitcast.me_ref, f32[192,1536]{1,0:T(8,128)} %get-tuple-element.176.slope_ref, f32[6,192,128]{2,1,0:T(8,128)} %get-tuple-element.157.rest_5_.rest_9_.rest_0_, f32[6,192,128]{2,1,0:T(8,128)} %collective-permute-done.10.rest_6_.rest_10_.rest_1_, ...), custom_call_target="tpu_custom_call" | custom-call | bytes 35389 | tf_op jit(solution)/shard_map/home_divergence/pallas_call | solution.py:314
  208.2 3.5 %all-to-all-start.2 = ((f32[4,192,384]{2,1,0:T(8,128)}), f32[4,192,384]{2,1,0:T(8,128)S(1)}, u32[]{:S(2)}, u32[]{:S(2)}) async-start(f32[4,192,384]{2,1,0:T(8,128)} %home_divergence.1), calls=%async_computation.2 | async-start | bytes 2359296 | tf_op jit(solution)/shard_map/all_to_all | solution.py:492
  211.8 6.7 %collective-permute-done.20.rest_8_ = f32[3,192,128]{2,1,0:T(8,128)} collective-permute-done((f32[3,192,128]{2,1,0:T(8,128)S(1)}, f32[3,192,128]{2,1,0:T(8,128)}, u32[]{:S(2)}, u32[]{:S(2)}) %collective-permute-start.20) | collective-permute-done | bytes 294944 | tf_op jit(solution)/shard_map/ppermute | solution.py:478
  218.5 9.5 %home_step.5 = f32[3,1,192,1536]{3,2,1,0:T(8,128)} custom-call(s32[1]{0:T(128)} %bitcast.me_ref, s32[44]{0:T(128)} %copy-done.13, s32[44]{0:T(128)} %compare_select_fusion.tile_ref, f32[4,1,192,1536]{3,2,1,0:T(8,128)} %flow_ref.9, f32[3,192,1536]{2,1,0:T(8,128)} %sub.64.base_ref, s32[32,1,256]{2,1,0:T(1,128)} %bitcast.31, ...), custom_call_target="tpu_custom_call", output_to_operand_aliasing={{}: (14, {})} | custom-call | flops 44291850240 | bytes 58982400 | tf_op jit(solution)/shard_map/home_step/pallas_call | solution.py:444
  (101 shorter events, 13.8 us)
Async XLA Ops:
  3.6 34.0 %collective-permute-start = (f32[6,192,128]{2,1,0:T(8,128)}, f32[6,192,128]{2,1,0:T(8,128)S(1)}, u32[]{:S(2)}, u32[]{:S(2)}) collective-permute-start(f32[6,192,128]{2,1,0:T(8,128)} %get-tuple-element.92), channel_id=1, source_target_pairs={{0,4},{1,5},{2,6},{3,7},{4,0},{5,1},{6,2},{7,3},{8,12},{9,13},{10,... | collective-permute-start | bytes 1769480 | tf_op jit(solution)/shard_map/ppermute | solution.py:478
  6.0 31.6 %collective-permute-start.1 = (f32[6,192,128]{2,1,0:T(8,128)}, f32[6,192,128]{2,1,0:T(8,128)S(1)}, u32[]{:S(2)}, u32[]{:S(2)}) collective-permute-start(f32[6,192,128]{2,1,0:T(8,128)} %get-tuple-element.93), channel_id=1, source_target_pairs={{0,2},{1,3},{2,0},{3,1},{4,6},{5,7},{6,4},{7,5},{8,10},{9,11},{10,... | collective-permute-start | bytes 1769480 | tf_op jit(solution)/shard_map/ppermute | solution.py:478
  6.2 51.0 %collective-permute-start.2 = (f32[6,192,128]{2,1,0:T(8,128)}, f32[6,192,128]{2,1,0:T(8,128)S(1)}, u32[]{:S(2)}, u32[]{:S(2)}) collective-permute-start(f32[6,192,128]{2,1,0:T(8,128)} %get-tuple-element.94), channel_id=1, source_target_pairs={{0,6},{1,7},{2,4},{3,5},{4,2},{5,3},{6,0},{7,1},{8,14},{9,15},{10,... | collective-permute-start | bytes 1769480 | tf_op jit(solution)/shard_map/ppermute | solution.py:478
  17.6 57.6 %all-to-all-start = ((f32[4,4,192,384]{3,2,1,0:T(8,128)}), f32[4,4,192,384]{3,2,1,0:T(8,128)}, u32[]{:S(2)}, u32[]{:S(2)}) async-start(f32[4,4,192,384]{3,2,1,0:T(8,128)} %bitcast.18), calls=%async_computation | async-start | bytes 9437184 | tf_op jit(solution)/shard_map/all_to_all | solution.py:492
  32.8 24.5 %copy-start.13 = (s32[44]{0:T(128)}, s32[44]{0:T(128)S(1)}, u32[]{:S(2)}) copy-start(s32[44]{0:T(128)S(1)} %broadcast_minimum_fusion.chunk_ref) | copy-start | bytes 532
  37.6 24.9 %copy-start.1 = (f32[6,192,128]{2,1,0:T(8,128)}, f32[6,192,128]{2,1,0:T(8,128)S(1)}, u32[]{:S(2)}) copy-start(f32[6,192,128]{2,1,0:T(8,128)S(1)} %collective-permute-done.rest_2_) | copy-start | bytes 1769476
  37.6 24.9 %copy-start.2 = (f32[6,192,128]{2,1,0:T(8,128)}, f32[6,192,128]{2,1,0:T(8,128)S(1)}, u32[]{:S(2)}) copy-start(f32[6,192,128]{2,1,0:T(8,128)S(1)} %collective-permute-done.1.rest_1_) | copy-start | bytes 1769476
  57.3 4.0 %collective-permute-start.7 = (f32[18,192,128]{2,1,0:T(8,128)S(1)}, f32[18,192,128]{2,1,0:T(8,128)S(1)}, u32[]{:S(2)}, u32[]{:S(2)}) collective-permute-start(f32[18,192,128]{2,1,0:T(8,128)S(1)} %pad_maximum_fusion), channel_id=1, source_target_pairs={{0,1},{1,0},{2,3},{3,2},{4,5},{5,4},{6,7},{7,6},{8,9},{9,8},{10,11... | collective-permute-start | bytes 5308424 | tf_op jit(solution)/shard_map/ppermute | solution.py:482
  57.9 4.7 %collective-permute-start.6 = (f32[6,192,128]{2,1,0:T(8,128)S(1)}, f32[6,192,128]{2,1,0:T(8,128)S(1)}, u32[]{:S(2)}, u32[]{:S(2)}) collective-permute-start(f32[6,192,128]{2,1,0:T(8,128)S(1)} %copy-done.5), channel_id=1, source_target_pairs={{0,1},{1,0},{2,3},{3,2},{4,5},{5,4},{6,7},{7,6},{8,9},{9,8},{10,11... | collective-permute-start | bytes 1769480 | tf_op jit(solution)/shard_map/ppermute | solution.py:482
  57.9 26.8 %collective-permute-start.3 = (f32[6,192,128]{2,1,0:T(8,128)}, f32[6,192,128]{2,1,0:T(8,128)}, u32[]{:S(2)}, u32[]{:S(2)}) collective-permute-start(f32[6,192,128]{2,1,0:T(8,128)} %get-tuple-element.107), channel_id=1, source_target_pairs={{0,4},{1,5},{2,6},{3,7},{4,0},{5,1},{6,2},{7,3},{8,12},{9,13},{10,... | collective-permute-start | bytes 1769480 | tf_op jit(solution)/shard_map/ppermute | solution.py:478
  57.9 29.4 %collective-permute-start.4 = (f32[6,192,128]{2,1,0:T(8,128)}, f32[6,192,128]{2,1,0:T(8,128)}, u32[]{:S(2)}, u32[]{:S(2)}) collective-permute-start(f32[6,192,128]{2,1,0:T(8,128)} %get-tuple-element.108), channel_id=1, source_target_pairs={{0,2},{1,3},{2,0},{3,1},{4,6},{5,7},{6,4},{7,5},{8,10},{9,11},{10,... | collective-permute-start | bytes 1769480 | tf_op jit(solution)/shard_map/ppermute | solution.py:478
  61.3 50.7 %collective-permute-start.5 = (f32[6,192,128]{2,1,0:T(8,128)}, f32[6,192,128]{2,1,0:T(8,128)}, u32[]{:S(2)}, u32[]{:S(2)}) collective-permute-start(f32[6,192,128]{2,1,0:T(8,128)} %get-tuple-element.109), channel_id=1, source_target_pairs={{0,6},{1,7},{2,4},{3,5},{4,2},{5,3},{6,0},{7,1},{8,14},{9,15},{10,... | collective-permute-start | bytes 1769480 | tf_op jit(solution)/shard_map/ppermute | solution.py:478
  73.4 38.5 %collective-permute-start.8 = (f32[6,192,128]{2,1,0:T(8,128)}, f32[6,192,128]{2,1,0:T(8,128)}, u32[]{:S(2)}, u32[]{:S(2)}) collective-permute-start(f32[6,192,128]{2,1,0:T(8,128)} %get-tuple-element.126.rest_0_), channel_id=1, source_target_pairs={{0,1},{1,0},{2,3},{3,2},{4,5},{5,4},{6,7},{7,6},{8,9},{9,8},{10,11... | collective-permute-start | bytes 1769480 | tf_op jit(solution)/shard_map/ppermute | solution.py:482
  80.9 55.8 %all-to-all-start.1 = ((f32[4,3,192,384]{3,2,1,0:T(8,128)}), f32[4,3,192,384]{3,2,1,0:T(8,128)S(1)}, u32[]{:S(2)}, u32[]{:S(2)}) async-start(f32[4,3,192,384]{3,2,1,0:T(8,128)} %get-tuple-element.141), calls=%async_computation.1 | async-start | bytes 7077888 | tf_op jit(solution)/shard_map/all_to_all | solution.py:492
  111.9 2.7 %collective-permute-start.12 = (f32[6,192,128]{2,1,0:T(8,128)}, f32[6,192,128]{2,1,0:T(8,128)}, u32[]{:S(2)}, u32[]{:S(2)}) collective-permute-start(f32[6,192,128]{2,1,0:T(8,128)} %collective-permute-done.4.rest_1_), channel_id=1, source_target_pairs={{0,1},{1,0},{2,3},{3,2},{4,5},{5,4},{6,7},{7,6},{8,9},{9,8},{10,11... | collective-permute-start | bytes 1769480 | tf_op jit(solution)/shard_map/ppermute | solution.py:482
  112.6 3.2 %collective-permute-start.13 = (f32[6,192,128]{2,1,0:T(8,128)}, f32[6,192,128]{2,1,0:T(8,128)}, u32[]{:S(2)}, u32[]{:S(2)}) collective-permute-start(f32[6,192,128]{2,1,0:T(8,128)} %collective-permute-done.3.rest_2_), channel_id=1, source_target_pairs={{0,1},{1,0},{2,3},{3,2},{4,5},{5,4},{6,7},{7,6},{8,9},{9,8},{10,11... | collective-permute-start | bytes 1769480 | tf_op jit(solution)/shard_map/ppermute | solution.py:482
  112.6 3.7 %collective-permute-start.14 = (f32[6,192,128]{2,1,0:T(8,128)}, f32[6,192,128]{2,1,0:T(8,128)}, u32[]{:S(2)}, u32[]{:S(2)}) collective-permute-start(f32[6,192,128]{2,1,0:T(8,128)} %collective-permute-done.5.rest_3_), channel_id=1, source_target_pairs={{0,1},{1,0},{2,3},{3,2},{4,5},{5,4},{6,7},{7,6},{8,9},{9,8},{10,11... | collective-permute-start | bytes 1769480 | tf_op jit(solution)/shard_map/ppermute | solution.py:482
  113.2 28.2 %collective-permute-start.9 = (f32[6,192,128]{2,1,0:T(8,128)}, f32[6,192,128]{2,1,0:T(8,128)}, u32[]{:S(2)}, u32[]{:S(2)}) collective-permute-start(f32[6,192,128]{2,1,0:T(8,128)} %get-tuple-element.123), channel_id=1, source_target_pairs={{0,4},{1,5},{2,6},{3,7},{4,0},{5,1},{6,2},{7,3},{8,12},{9,13},{10,... | collective-permute-start | bytes 1769480 | tf_op jit(solution)/shard_map/ppermute | solution.py:478
  113.2 28.2 %collective-permute-start.10 = (f32[6,192,128]{2,1,0:T(8,128)}, f32[6,192,128]{2,1,0:T(8,128)}, u32[]{:S(2)}, u32[]{:S(2)}) collective-permute-start(f32[6,192,128]{2,1,0:T(8,128)} %get-tuple-element.124), channel_id=1, source_target_pairs={{0,2},{1,3},{2,0},{3,1},{4,6},{5,7},{6,4},{7,5},{8,10},{9,11},{10,... | collective-permute-start | bytes 1769480 | tf_op jit(solution)/shard_map/ppermute | solution.py:478
  114.6 49.8 %collective-permute-start.11 = (f32[6,192,128]{2,1,0:T(8,128)}, f32[6,192,128]{2,1,0:T(8,128)}, u32[]{:S(2)}, u32[]{:S(2)}) collective-permute-start(f32[6,192,128]{2,1,0:T(8,128)} %get-tuple-element.125), channel_id=1, source_target_pairs={{0,6},{1,7},{2,4},{3,5},{4,2},{5,3},{6,0},{7,1},{8,14},{9,15},{10,... | collective-permute-start | bytes 1769480 | tf_op jit(solution)/shard_map/ppermute | solution.py:478
  138.9 25.5 %copy-start.19 = (f32[3,192,128]{2,1,0:T(8,128)S(1)}, f32[3,192,128]{2,1,0:T(8,128)}, u32[]{:S(2)}) copy-start(f32[3,192,128]{2,1,0:T(8,128)} %get-tuple-element.150) | copy-start | bytes 884740
  138.9 25.5 %copy-start.18 = (f32[3,192,128]{2,1,0:T(8,128)S(1)}, f32[3,192,128]{2,1,0:T(8,128)}, u32[]{:S(2)}) copy-start(f32[3,192,128]{2,1,0:T(8,128)} %get-tuple-element.151) | copy-start | bytes 884740
  138.9 28.8 %copy-start.17 = (f32[3,192,128]{2,1,0:T(8,128)S(1)}, f32[3,192,128]{2,1,0:T(8,128)}, u32[]{:S(2)}) copy-start(f32[3,192,128]{2,1,0:T(8,128)} %get-tuple-element.152) | copy-start | bytes 884740
  138.9 28.9 %copy-start.12 = (s32[1,192,12]{1,0,2:T(1,128)S(1)}, s32[1,192,12]{1,0,2:T(1,128)}, u32[]{:S(2)}) copy-start(s32[1,192,12]{1,0,2:T(1,128)} %param.9) | copy-start | bytes 27652
  164.4 14.3 %collective-permute-start.15 = (f32[3,192,128]{2,1,0:T(8,128)S(1)}, f32[3,192,128]{2,1,0:T(8,128)S(1)}, u32[]{:S(2)}, u32[]{:S(2)}) collective-permute-start(f32[3,192,128]{2,1,0:T(8,128)S(1)} %copy-done.19), channel_id=1, source_target_pairs={{0,4},{1,5},{2,6},{3,7},{4,0},{5,1},{6,2},{7,3},{8,12},{9,13},{10,... | collective-permute-start | bytes 884744 | tf_op jit(solution)/shard_map/ppermute | solution.py:478
  164.4 16.3 %collective-permute-start.16 = (f32[3,192,128]{2,1,0:T(8,128)S(1)}, f32[3,192,128]{2,1,0:T(8,128)S(1)}, u32[]{:S(2)}, u32[]{:S(2)}) collective-permute-start(f32[3,192,128]{2,1,0:T(8,128)S(1)} %copy-done.18), channel_id=1, source_target_pairs={{0,2},{1,3},{2,0},{3,1},{4,6},{5,7},{6,4},{7,5},{8,10},{9,11},{10,... | collective-permute-start | bytes 884744 | tf_op jit(solution)/shard_map/ppermute | solution.py:478
  167.8 25.1 %collective-permute-start.17 = (f32[3,192,128]{2,1,0:T(8,128)S(1)}, f32[3,192,128]{2,1,0:T(8,128)S(1)}, u32[]{:S(2)}, u32[]{:S(2)}) collective-permute-start(f32[3,192,128]{2,1,0:T(8,128)S(1)} %copy-done.17), channel_id=1, source_target_pairs={{0,6},{1,7},{2,4},{3,5},{4,2},{5,3},{6,0},{7,1},{8,14},{9,15},{10,... | collective-permute-start | bytes 884744 | tf_op jit(solution)/shard_map/ppermute | solution.py:478
  168.6 24.8 %copy-start.14 = (f32[3,192,128]{2,1,0:T(8,128)S(1)}, f32[3,192,128]{2,1,0:T(8,128)}, u32[]{:S(2)}) copy-start(f32[3,192,128]{2,1,0:T(8,128)} %get-tuple-element.164) | copy-start | bytes 884740
  192.9 18.9 %collective-permute-start.18 = (f32[3,192,128]{2,1,0:T(8,128)S(1)}, f32[3,192,128]{2,1,0:T(8,128)S(1)}, u32[]{:S(2)}, u32[]{:S(2)}) collective-permute-start(f32[3,192,128]{2,1,0:T(8,128)S(1)} %copy-done.16), channel_id=1, source_target_pairs={{0,4},{1,5},{2,6},{3,7},{4,0},{5,1},{6,2},{7,3},{8,12},{9,13},{10,... | collective-permute-start | bytes 884744 | tf_op jit(solution)/shard_map/ppermute | solution.py:478
  192.9 18.9 %collective-permute-start.19 = (f32[3,192,128]{2,1,0:T(8,128)S(1)}, f32[3,192,128]{2,1,0:T(8,128)}, u32[]{:S(2)}, u32[]{:S(2)}) collective-permute-start(f32[3,192,128]{2,1,0:T(8,128)S(1)} %copy-done.15), channel_id=1, source_target_pairs={{0,2},{1,3},{2,0},{3,1},{4,6},{5,7},{6,4},{7,5},{8,10},{9,11},{10,... | collective-permute-start | bytes 884744 | tf_op jit(solution)/shard_map/ppermute | solution.py:478
  193.4 25.1 %collective-permute-start.20 = (f32[3,192,128]{2,1,0:T(8,128)S(1)}, f32[3,192,128]{2,1,0:T(8,128)}, u32[]{:S(2)}, u32[]{:S(2)}) collective-permute-start(f32[3,192,128]{2,1,0:T(8,128)S(1)} %copy-done.14), channel_id=1, source_target_pairs={{0,6},{1,7},{2,4},{3,5},{4,2},{5,3},{6,0},{7,1},{8,14},{9,15},{10,... | collective-permute-start | bytes 884744 | tf_op jit(solution)/shard_map/ppermute | solution.py:478
  208.2 19.8 %all-to-all-start.2 = ((f32[4,192,384]{2,1,0:T(8,128)}), f32[4,192,384]{2,1,0:T(8,128)S(1)}, u32[]{:S(2)}, u32[]{:S(2)}) async-start(f32[4,192,384]{2,1,0:T(8,128)} %home_divergence.1), calls=%async_computation.2 | async-start | bytes 2359296 | tf_op jit(solution)/shard_map/all_to_all | solution.py:492
  (13 other events, 149.2 us)

commit v7 on v6

--- a/solution.py
+++ b/solution.py
@@ -13,7 +13,7 @@
 LANES = 128
 CHUNK = 256
 CORES = 2
-UNROLL = 22
+UNROLL = 44
 FIELD_ORDER = (1, 3, 0, 2)
 ANY = pl.BlockSpec(memory_space=pl.ANY)
 HBM = pl.BlockSpec(memory_space=pltpu.HBM)
@@ -92,33 +92,50 @@
         c.wait()
 
 
-def pack_lines(plan, rounds, me, flow):
+def pack_lines(plan, rounds, me, flow, messages):
     n, rows, tiles = plan.chips, plan.rows, plan.tiles
     start, end = rounds[0] * n, min((rounds[-1] + 1) * n, plan.pairs)
 
     def kernel(me_ref, flow_ref, *rest):
         outs, (held, in_sems, out_sems) = rest[:-3], rest[-3:]
-        loads = [pltpu.make_async_copy(
-            flow_ref.at[FIELD_ORDER[q // tiles], 0, :, pl.ds(q % tiles * LANES, LANES)], held.at[q - start],
-            in_sems.at[q - start]) for q in range(start, end)]
-        for c in loads:
-            c.start()
+        chip = me_ref[0] // CORES
         copies = []
-        for k in range(len(rounds)):
-            for c in loads[k * n : (k + 1) * n]:
-                c.wait()
-            for s in range(n):
-                pair = jnp.minimum(k * n + plan.to(me_ref[0] // CORES, s), end - start - 1)
-                copies.append(pltpu.make_async_copy(held.at[pair], outs[s].at[k], out_sems.at[len(copies)]))
-                copies[-1].start()
+        if len(messages) == 1:
+            loads = []
+            for k, r in enumerate(rounds):
+                pair = jnp.minimum(r * n + plan.to(chip, messages[0]), plan.pairs - 1)
+                slot, z = pair // tiles, pl.multiple_of(pair % tiles * LANES, LANES)
+                field = jnp.int32(FIELD_ORDER[0])
+                for i, f in enumerate(FIELD_ORDER[1:], 1):
+                    field = jnp.where(slot == i, f, field)
+                loads.append(pltpu.make_async_copy(flow_ref.at[field, 0, :, pl.ds(z, LANES)], held.at[k], in_sems.at[k]))
+                copies.append(pltpu.make_async_copy(held.at[k], outs[0].at[k], out_sems.at[k]))
+            for c in loads:
+                c.start()
+            for load, store in zip(loads, copies):
+                load.wait()
+                store.start()
+        else:
+            loads = [pltpu.make_async_copy(
+                flow_ref.at[FIELD_ORDER[q // tiles], 0, :, pl.ds(q % tiles * LANES, LANES)], held.at[q - start],
+                in_sems.at[q - start]) for q in range(start, end)]
+            for c in loads:
+                c.start()
+            for k in range(len(rounds)):
+                for c in loads[k * n : (k + 1) * n]:
+                    c.wait()
+                for i, s in enumerate(messages):
+                    pair = jnp.minimum(k * n + plan.to(chip, s), end - start - 1)
+                    copies.append(pltpu.make_async_copy(held.at[pair], outs[i].at[k], out_sems.at[len(copies)]))
+                    copies[-1].start()
         for c in copies:
             c.wait()
 
     shape = jax.ShapeDtypeStruct((len(rounds), rows, LANES), F32)
     return pl.pallas_call(
-        kernel, out_shape=[shape] * n, in_specs=[SMEM, HBM], out_specs=[HBM] * n,
+        kernel, out_shape=[shape] * len(messages), in_specs=[SMEM, HBM], out_specs=[HBM] * len(messages),
         scratch_shapes=[pltpu.VMEM((end - start, rows, LANES), F32), pltpu.SemaphoreType.DMA((end - start,)),
-                        pltpu.SemaphoreType.DMA((n * len(rounds),))],
+                        pltpu.SemaphoreType.DMA((len(messages) * len(rounds),))],
         compiler_params=params(), cost_estimate=cost(0, 2 * flow.size), name="pack_lines",
     )(me, flow)
 
@@ -504,11 +521,15 @@
         out = lax.optimization_barrier(tuple(turned))
         return [turn(o, True) if is_lines(v) else o for v, o in zip(values, out)]
 
-    packed = pack_lines(plan, first, pen_at, flow)
+    heavy, everything = shifts[0], list(range(chips))
+    light = [s for s in everything if s != heavy]
+    (packed_heavy,) = pack_lines(plan, first, pen_at, flow, [heavy])
+    packed = list(pack_lines(plan, first, pen_at, after(flow, packed_heavy), light))
+    packed.insert(heavy, packed_heavy)
     lines = send_lines(packed)
     lines_x = exchange(cut_depth(after(flow, packed)[:, 0]))
     order = marker_order(*after((marker_cells[0, 0], marker_weights[0, 0]), packed), rows, depth)
-    packed = pack_lines(plan, second, pen_at, after(flow, order))
+    packed = pack_lines(plan, second, pen_at, after(flow, order), everything)
     lines, order, packed = together((lines, order, packed))
     lines_2 = send_lines(packed)
     (slopes,) = slopes_of(first, [first], lines, swap(lines))

time: 231 us -> 230 us (level)
    ppermute x15, waiting for transfers between devices: 90.5 us -> 85.8 us  [send_lines(): lax.ppermute(blocks[s], 'pen', [(i, plan.to(i // CORES, s) * CORES + i %...]
    all_to_all x3, waiting for transfers between devices: 0.7 us -> 3.49 us  [exchange(): return lax.all_to_all(value, 'grp', 0, 0, tiled=True)]
    pallas_call x2 -> x3, Pallas kernels: 5.93 us -> 7.82 us  [pack_lines(): pl.pallas_call(kernel, out_shape=[shape] * len(messages), in_specs=[SMEM,...]
  transfers between devices with their start and end apart: 24 -> 24, of which waited for: 10 -> 10; matrix products, arithmetic and copies ran while one was open for 12% -> 12% of each run, Pallas kernels for 31% -> 32%
where the time goes in v7:
time: 230 us; the launch traced here: 228 us
  waiting for transfers between devices  90.8 us (39%)
  Pallas kernels  74.8 us (33%)
  starting transfers between devices  29.2 us (13%)
  local copies, waits for them, and re-layouts  18.5 us (8%)
  other arithmetic  13.5 us (6%)
    ppermute x15, waiting for transfers between devices, send_lines(): lax.ppermute(blocks[s], 'pen', [(i, plan.to(i // CORES, s) * CORES + i %...  85.8 us
    pallas_call x3, Pallas kernels, home_step(): pl.pallas_call(kernel, out_shape=jax.ShapeDtypeStruct((3, 1, rows, depth)...  28 us
    pallas_call x2, Pallas kernels, line_slopes(): pl.pallas_call(kernel, out_shape=shapes, in_specs=[SMEM, VMEM, VMEM] + [H...  20.1 us
    ppermute x15, starting transfers between devices, send_lines(): lax.ppermute(blocks[s], 'pen', [(i, plan.to(i // CORES, s) * CORES + i %...  13.8 us
    all_to_all x3, starting transfers between devices, exchange(): return lax.all_to_all(value, 'grp', 0, 0, tiled=True)  12.5 us
    another operation x2, local copies, waits for them, and re-layouts, cut_depth(): return jnp.moveaxis(value.reshape(*value.shape[:-1], grps, width), -2, 0)  11.2 us
    pallas_call x1, Pallas kernels, depth_terms(): pl.pallas_call(kernel, grid=(rows // step,), out_shape=[jax.ShapeDtypeStr...  10.2 us
    pallas_call x3, Pallas kernels, pack_lines(): pl.pallas_call(kernel, out_shape=[shape] * len(messages), in_specs=[SMEM,...  7.82 us
  transfers between devices with their start and end apart: 24, of which 10 were waited for; matrix products, arithmetic and copies ran while one was open for 12% of the time, Pallas kernels for 32%

profile of v7, /device:TPU:9, one launch (start us, length us, event | category | flops | bytes accessed | tf_op | source)
XLA Modules:
  0.0 227.9 jit_solution(6139936988337669193)
XLA Ops:
  0.6 2.1 pack_lines.3
  2.7 2.4 %collective-permute-start = (f32[6,192,128]{2,1,0:T(8,128)}, f32[6,192,128]{2,1,0:T(8,128)S(1)}, u32[]{:S(2)}, u32[]{:S(2)}) collective-permute-start(f32[6,192,128]{2,1,0:T(8,128)} %pack_lines.3), channel_id=1, source_target_pairs={{0,4},{1,5},{2,6},{3,7},{4,0},{5,1},{6,2},{7,3},{8,12},{9,13},{10,... | collective-permute-start | bytes 1769480 | tf_op jit(solution)/shard_map/ppermute | solution.py:495
  5.1 2.8 %pack_lines.4 = (f32[6,192,128]{2,1,0:T(8,128)}, f32[6,192,128]{2,1,0:T(8,128)}, f32[6,192,128]{2,1,0:T(8,128)}) custom-call(s32[1]{0:T(128)} %bitcast.me_ref, f32[4,1,192,1536]{3,2,1,0:T(8,128)} %flow_ref.10), custom_call_target="tpu_custom_call" | custom-call | bytes 23592 | tf_op jit(solution)/shard_map/pack_lines/pallas_call | solution.py:135
  8.3 6.2 %reshape_squeeze.3 = f32[4,192,4,384]{3,2,1,0:T(4,128)} reshape(f32[4,1,192,1536]{3,2,1,0:T(8,128)} %flow_ref.10) | data formatting | bytes 9437184 | tf_op jit(solution)/shard_map/reshape;squeeze | solution.py:506
  14.5 5.0 %copy.36 = f32[4,192,4,384]{3,1,0,2:T(8,128)} copy(f32[4,192,4,384]{3,2,1,0:T(4,128)} %reshape_squeeze.3) | data formatting | bytes 9437184 | tf_op jit(solution)/shard_map/reshape;squeeze | solution.py:506
  19.5 5.1 %all-to-all-start = ((f32[4,4,192,384]{3,2,1,0:T(8,128)}), f32[4,4,192,384]{3,2,1,0:T(8,128)}, u32[]{:S(2)}, u32[]{:S(2)}) async-start(f32[4,4,192,384]{3,2,1,0:T(8,128)} %bitcast.18), calls=%async_computation | async-start | bytes 9437184 | tf_op jit(solution)/shard_map/all_to_all | solution.py:509
  26.7 6.9 %sort.23 = (s32[8192]{0:T(1024)S(1)}, f32[8192]{0:T(1024)}, s32[8192]{0:T(1024)}) sort(s32[8192]{0:T(1024)S(1)} %fusion.5, f32[8192]{0:T(1024)S(1)} %reshape.61, s32[8192]{0:T(1024)S(1)} %iota.19), dimensions={0}, to_apply=%region_0.1 | sort | flops 106496 | bytes 196608 | tf_op jit(solution)/shard_map/sort | solution.py:278
  36.6 3.0 %pack_lines.5 = (f32[6,192,128]{2,1,0:T(8,128)}, f32[6,192,128]{2,1,0:T(8,128)}, f32[6,192,128]{2,1,0:T(8,128)}, f32[6,192,128]{2,1,0:T(8,128)}) custom-call(s32[1]{0:T(128)} %bitcast.me_ref, f32[4,1,192,1536]{3,2,1,0:T(8,128)} %flow_ref.10), custom_call_target="tpu_custom_call" | custom-call | bytes 23592 | tf_op jit(solution)/shard_map/pack_lines/pallas_call | solution.py:135
  39.6 4.5 %collective-permute-done.1.rest_1_ = f32[6,192,128]{2,1,0:T(8,128)S(1)} collective-permute-done((f32[6,192,128]{2,1,0:T(8,128)}, f32[6,192,128]{2,1,0:T(8,128)S(1)}, u32[]{:S(2)}, u32[]{:S(2)}) %collective-permute-start.1) | collective-permute-done | bytes 589856 | tf_op jit(solution)/shard_map/ppermute | solution.py:495
  44.1 12.2 %collective-permute-done.2.rest_3_ = f32[6,192,128]{2,1,0:T(8,128)S(1)} collective-permute-done((f32[6,192,128]{2,1,0:T(8,128)}, f32[6,192,128]{2,1,0:T(8,128)S(1)}, u32[]{:S(2)}, u32[]{:S(2)}) %collective-permute-start.2) | collective-permute-done | bytes 589856 | tf_op jit(solution)/shard_map/ppermute | solution.py:495
  57.1 3.3 %collective-permute-start.4 = (f32[6,192,128]{2,1,0:T(8,128)}, f32[6,192,128]{2,1,0:T(8,128)}, u32[]{:S(2)}, u32[]{:S(2)}) collective-permute-start(f32[6,192,128]{2,1,0:T(8,128)} %get-tuple-element.108), channel_id=1, source_target_pairs={{0,2},{1,3},{2,0},{3,1},{4,6},{5,7},{6,4},{7,5},{8,10},{9,11},{10,... | collective-permute-start | bytes 1769480 | tf_op jit(solution)/shard_map/ppermute | solution.py:495
  60.4 1.3 fusion.18
  62.5 10.0 %line_slopes.2 = (f32[6,192,128]{2,1,0:T(8,128)}, f32[6,192,128]{2,1,0:T(8,128)}, f32[6,192,128]{2,1,0:T(8,128)}, f32[6,192,128]{2,1,0:T(8,128)}) custom-call(s32[1]{0:T(128)} %bitcast.me_ref, bf16[2,768,768]{2,1,0:T(8,128)(2,1)} %constant.112.clone.high_ref, bf16[2,768,768]{2,1,0:T(8,128)(2,1)} %constant.113.clone.low_ref, ...), custom_call_target="tpu_custom_call" | custom-call | flops 27179088 | bytes 117964 | tf_op jit(solution)/shard_map/line_slopes/pallas_call | solution.py:195
  73.6 3.5 %all-to-all-done.in_ref = f32[4,4,192,384]{3,2,1,0:T(8,128)} async-done(((f32[4,4,192,384]{3,2,1,0:T(8,128)}), f32[4,4,192,384]{3,2,1,0:T(8,128)}, u32[]{:S(2)}, u32[]{:S(2)}) %all-to-all-start) | async-done | bytes 4718624 | tf_op jit(solution)/shard_map/all_to_all | solution.py:509
  77.1 5.7 %slab_terms.1 = (f32[4,3,192,384]{3,2,1,0:T(8,128)}, f32[4,192,384]{2,1,0:T(8,128)}) custom-call(f32[4,4,192,384]{3,2,1,0:T(8,128)} %all-to-all-done.in_ref), custom_call_target="tpu_custom_call" | custom-call | flops 188743 | bytes 94371 | tf_op jit(solution)/shard_map/slab_terms/pallas_call | solution.py:260
  82.8 3.9 %all-to-all-start.1 = ((f32[4,3,192,384]{3,2,1,0:T(8,128)}), f32[4,3,192,384]{3,2,1,0:T(8,128)S(1)}, u32[]{:S(2)}, u32[]{:S(2)}) async-start(f32[4,3,192,384]{3,2,1,0:T(8,128)} %get-tuple-element.141), calls=%async_computation.1 | async-start | bytes 7077888 | tf_op jit(solution)/shard_map/all_to_all | solution.py:509
  86.7 24.3 %collective-permute-done.5.rest_3_ = f32[6,192,128]{2,1,0:T(8,128)} collective-permute-done((f32[6,192,128]{2,1,0:T(8,128)}, f32[6,192,128]{2,1,0:T(8,128)}, u32[]{:S(2)}, u32[]{:S(2)}) %collective-permute-start.5) | collective-permute-done | bytes 589856 | tf_op jit(solution)/shard_map/ppermute | solution.py:495
  115.5 10.1 %line_slopes.3 = (f32[3,192,128]{2,1,0:T(8,128)}, f32[3,192,128]{2,1,0:T(8,128)}, f32[3,192,128]{2,1,0:T(8,128)}, f32[3,192,128]{2,1,0:T(8,128)}, f32[3,192,128]...) custom-call(s32[1]{0:T(128)} %bitcast.me_ref, ...), custom_call_target="tpu_custom_call" | custom-call | flops 17666408448 | bytes 76677120 | tf_op jit(solution)/shard_map/line_slopes/pallas_call | solution.py:195
  125.5 10.2 %depth_terms.1 = (f32[3,192,1536]{2,1,0:T(8,128)}, f32[192,1536]{1,0:T(8,128)}) custom-call(f32[4,1,192,1536]{3,2,1,0:T(8,128)} %flow_ref.10, bf16[2,768,768]{2,1,0:T(8,128)(2,1)} %constant.112.clone.high_ref, bf16[2,768,768]{2,1,0:T(8,128)(2,1)} %constant.113.clone.low_ref), custom_call_target="tpu_custom_call" | custom-call | flops 54358180 | bytes 141557 | tf_op jit(solution)/shard_map/depth_terms/pallas_call | solution.py:233
  136.6 1.5 copy-done
  138.1 2.4 %sub.64.base_ref = f32[3,192,1536]{2,1,0:T(8,128)} subtract(f32[3,192,1536]{2,1,0:T(8,128)S(1)} %copy-done, f32[3,192,1536]{2,1,0:T(8,128)S(1)} %bitcast.19) | non-fusion elementwise | flops 884736 | bytes 10616832 | tf_op jit(solution)/shard_map/sub | solution.py:543
  140.6 23.0 %collective-permute-done.11.rest_8_.rest_12_.rest_3_ = f32[6,192,128]{2,1,0:T(8,128)} collective-permute-done((f32[6,192,128]{2,1,0:T(8,128)}, f32[6,192,128]{2,1,0:T(8,128)}, u32[]{:S(2)}, u32[]{:S(2)}) %collective-permute-start.11) | collective-permute-done | bytes 589856 | tf_op jit(solution)/shard_map/ppermute | solution.py:495
  163.6 3.4 %collective-permute-start.16 = (f32[3,192,128]{2,1,0:T(8,128)S(1)}, f32[3,192,128]{2,1,0:T(8,128)S(1)}, u32[]{:S(2)}, u32[]{:S(2)}) collective-permute-start(f32[3,192,128]{2,1,0:T(8,128)S(1)} %copy-done.18), channel_id=1, source_target_pairs={{0,2},{1,3},{2,0},{3,1},{4,6},{5,7},{6,4},{7,5},{8,10},{9,11},{10,... | collective-permute-start | bytes 884744 | tf_op jit(solution)/shard_map/ppermute | solution.py:495
  167.7 9.9 %home_step.3.rest_9_ = f32[3,1,192,1536]{3,2,1,0:T(8,128)} custom-call(s32[1]{0:T(128)} %bitcast.me_ref, s32[44]{0:T(128)} %copy-done.13, s32[44]{0:T(128)} %compare_select_fusion.tile_ref, f32[4,1,192,1536]{3,2,1,0:T(8,128)} %flow_ref.10, f32[3,192,1536]{2,1,0:T(8,128)} %sub.64.base_ref, s32[32,1,256]{2,1,0:T(1,128)} %bitcast.29, s32[32,1,256]{2,1,0:T(1,128)} %bitcast.26, ...), custom_call_target="tpu_custom_call" | custom-call | flops 44291848 | bytes 58982 | tf_op jit(solution)/shard_map/home_step/pallas_call | solution.py:461
  177.6 2.2 collective-permute-done.16.rest_6_
  179.9 12.2 %collective-permute-done.17.rest_8_ = f32[3,192,128]{2,1,0:T(8,128)S(1)} collective-permute-done((f32[3,192,128]{2,1,0:T(8,128)S(1)}, f32[3,192,128]{2,1,0:T(8,128)S(1)}, u32[]{:S(2)}, u32[]{:S(2)}) %collective-permute-start.17) | collective-permute-done | bytes 294944 | tf_op jit(solution)/shard_map/ppermute | solution.py:495
  192.5 2.2 collective-permute-start.20
  194.7 9.1 %home_step.4.rest_9_ = f32[3,1,192,1536]{3,2,1,0:T(8,128)} custom-call(s32[1]{0:T(128)} %bitcast.me_ref, s32[44]{0:T(128)} %copy-done.13, s32[44]{0:T(128)} %compare_select_fusion.tile_ref, f32[4,1,192,1536]{3,2,1,0:T(8,128)} %flow_ref.10, f32[3,192,1536]{2,1,0:T(8,128)} %sub.64.base_ref, s32[32,1,256]{2,1,0:T(1,128)} %bitcast.30, ...), custom_call_target="tpu_custom_call", output_to_operand_aliasing={{}: (14, {})} | custom-call | flops 44291848 | bytes 58982 | tf_op jit(solution)/shard_map/home_step/pallas_call | solution.py:461
  203.8 2.9 %home_divergence.1 = f32[4,192,384]{2,1,0:T(8,128)} custom-call(s32[1]{0:T(128)} %bitcast.me_ref, f32[192,1536]{1,0:T(8,128)} %get-tuple-element.176.slope_ref, f32[6,192,128]{2,1,0:T(8,128)} %get-tuple-element.157.rest_5_.rest_9_.rest_0_, f32[6,192,128]{2,1,0:T(8,128)} %collective-permute-done.10.rest_6_.rest_10_.rest_1_, ...), custom_call_target="tpu_custom_call" | custom-call | bytes 35389 | tf_op jit(solution)/shard_map/home_divergence/pallas_call | solution.py:331
  206.7 3.5 %all-to-all-start.2 = ((f32[4,192,384]{2,1,0:T(8,128)}), f32[4,192,384]{2,1,0:T(8,128)S(1)}, u32[]{:S(2)}, u32[]{:S(2)}) async-start(f32[4,192,384]{2,1,0:T(8,128)} %home_divergence.1), calls=%async_computation.2 | async-start | bytes 2359296 | tf_op jit(solution)/shard_map/all_to_all | solution.py:509
  210.3 7.3 %collective-permute-done.20.rest_8_ = f32[3,192,128]{2,1,0:T(8,128)} collective-permute-done((f32[3,192,128]{2,1,0:T(8,128)S(1)}, f32[3,192,128]{2,1,0:T(8,128)}, u32[]{:S(2)}, u32[]{:S(2)}) %collective-permute-start.20) | collective-permute-done | bytes 294944 | tf_op jit(solution)/shard_map/ppermute | solution.py:495
  217.6 9.1 %home_step.5 = f32[3,1,192,1536]{3,2,1,0:T(8,128)} custom-call(s32[1]{0:T(128)} %bitcast.me_ref, s32[44]{0:T(128)} %copy-done.13, s32[44]{0:T(128)} %compare_select_fusion.tile_ref, f32[4,1,192,1536]{3,2,1,0:T(8,128)} %flow_ref.10, f32[3,192,1536]{2,1,0:T(8,128)} %sub.64.base_ref, s32[32,1,256]{2,1,0:T(1,128)} %bitcast.31, ...), custom_call_target="tpu_custom_call", output_to_operand_aliasing={{}: (14, {})} | custom-call | flops 44291850240 | bytes 58982400 | tf_op jit(solution)/shard_map/home_step/pallas_call | solution.py:461
  (102 shorter events, 15.6 us)
Async XLA Ops:
  2.7 36.8 %collective-permute-start = (f32[6,192,128]{2,1,0:T(8,128)}, f32[6,192,128]{2,1,0:T(8,128)S(1)}, u32[]{:S(2)}, u32[]{:S(2)}) collective-permute-start(f32[6,192,128]{2,1,0:T(8,128)} %pack_lines.3), channel_id=1, source_target_pairs={{0,4},{1,5},{2,6},{3,7},{4,0},{5,1},{6,2},{7,3},{8,12},{9,13},{10,... | collective-permute-start | bytes 1769480 | tf_op jit(solution)/shard_map/ppermute | solution.py:495
  7.9 36.2 %collective-permute-start.1 = (f32[6,192,128]{2,1,0:T(8,128)}, f32[6,192,128]{2,1,0:T(8,128)S(1)}, u32[]{:S(2)}, u32[]{:S(2)}) collective-permute-start(f32[6,192,128]{2,1,0:T(8,128)} %get-tuple-element.93), channel_id=1, source_target_pairs={{0,2},{1,3},{2,0},{3,1},{4,6},{5,7},{6,4},{7,5},{8,10},{9,11},{10,... | collective-permute-start | bytes 1769480 | tf_op jit(solution)/shard_map/ppermute | solution.py:495
  8.1 48.2 %collective-permute-start.2 = (f32[6,192,128]{2,1,0:T(8,128)}, f32[6,192,128]{2,1,0:T(8,128)S(1)}, u32[]{:S(2)}, u32[]{:S(2)}) collective-permute-start(f32[6,192,128]{2,1,0:T(8,128)} %get-tuple-element.94), channel_id=1, source_target_pairs={{0,6},{1,7},{2,4},{3,5},{4,2},{5,3},{6,0},{7,1},{8,14},{9,15},{10,... | collective-permute-start | bytes 1769480 | tf_op jit(solution)/shard_map/ppermute | solution.py:495
  19.5 57.6 %all-to-all-start = ((f32[4,4,192,384]{3,2,1,0:T(8,128)}), f32[4,4,192,384]{3,2,1,0:T(8,128)}, u32[]{:S(2)}, u32[]{:S(2)}) async-start(f32[4,4,192,384]{3,2,1,0:T(8,128)} %bitcast.18), calls=%async_computation | async-start | bytes 9437184 | tf_op jit(solution)/shard_map/all_to_all | solution.py:509
  39.6 22.1 %copy-start.1 = (f32[6,192,128]{2,1,0:T(8,128)}, f32[6,192,128]{2,1,0:T(8,128)S(1)}, u32[]{:S(2)}) copy-start(f32[6,192,128]{2,1,0:T(8,128)S(1)} %collective-permute-done.rest_2_) | copy-start | bytes 1769476
  56.4 4.0 %collective-permute-start.7 = (f32[18,192,128]{2,1,0:T(8,128)S(1)}, f32[18,192,128]{2,1,0:T(8,128)S(1)}, u32[]{:S(2)}, u32[]{:S(2)}) collective-permute-start(f32[18,192,128]{2,1,0:T(8,128)S(1)} %pad_maximum_fusion), channel_id=1, source_target_pairs={{0,1},{1,0},{2,3},{3,2},{4,5},{5,4},{6,7},{7,6},{8,9},{9,8},{10,11... | collective-permute-start | bytes 5308424 | tf_op jit(solution)/shard_map/ppermute | solution.py:499
  57.0 4.7 %collective-permute-start.6 = (f32[6,192,128]{2,1,0:T(8,128)S(1)}, f32[6,192,128]{2,1,0:T(8,128)S(1)}, u32[]{:S(2)}, u32[]{:S(2)}) collective-permute-start(f32[6,192,128]{2,1,0:T(8,128)S(1)} %copy-done.5), channel_id=1, source_target_pairs={{0,1},{1,0},{2,3},{3,2},{4,5},{5,4},{6,7},{7,6},{8,9},{9,8},{10,11... | collective-permute-start | bytes 1769480 | tf_op jit(solution)/shard_map/ppermute | solution.py:499
  57.1 29.6 %collective-permute-start.3 = (f32[6,192,128]{2,1,0:T(8,128)}, f32[6,192,128]{2,1,0:T(8,128)}, u32[]{:S(2)}, u32[]{:S(2)}) collective-permute-start(f32[6,192,128]{2,1,0:T(8,128)} %get-tuple-element.107), channel_id=1, source_target_pairs={{0,4},{1,5},{2,6},{3,7},{4,0},{5,1},{6,2},{7,3},{8,12},{9,13},{10,... | collective-permute-start | bytes 1769480 | tf_op jit(solution)/shard_map/ppermute | solution.py:495
  57.1 29.6 %collective-permute-start.4 = (f32[6,192,128]{2,1,0:T(8,128)}, f32[6,192,128]{2,1,0:T(8,128)}, u32[]{:S(2)}, u32[]{:S(2)}) collective-permute-start(f32[6,192,128]{2,1,0:T(8,128)} %get-tuple-element.108), channel_id=1, source_target_pairs={{0,2},{1,3},{2,0},{3,1},{4,6},{5,7},{6,4},{7,5},{8,10},{9,11},{10,... | collective-permute-start | bytes 1769480 | tf_op jit(solution)/shard_map/ppermute | solution.py:495
  60.4 50.7 %collective-permute-start.5 = (f32[6,192,128]{2,1,0:T(8,128)}, f32[6,192,128]{2,1,0:T(8,128)}, u32[]{:S(2)}, u32[]{:S(2)}) collective-permute-start(f32[6,192,128]{2,1,0:T(8,128)} %get-tuple-element.109), channel_id=1, source_target_pairs={{0,6},{1,7},{2,4},{3,5},{4,2},{5,3},{6,0},{7,1},{8,14},{9,15},{10,... | collective-permute-start | bytes 1769480 | tf_op jit(solution)/shard_map/ppermute | solution.py:495
  72.6 38.5 %collective-permute-start.8 = (f32[6,192,128]{2,1,0:T(8,128)}, f32[6,192,128]{2,1,0:T(8,128)}, u32[]{:S(2)}, u32[]{:S(2)}) collective-permute-start(f32[6,192,128]{2,1,0:T(8,128)} %get-tuple-element.126.rest_0_), channel_id=1, source_target_pairs={{0,1},{1,0},{2,3},{3,2},{4,5},{5,4},{6,7},{7,6},{8,9},{9,8},{10,11... | collective-permute-start | bytes 1769480 | tf_op jit(solution)/shard_map/ppermute | solution.py:499
  82.8 53.0 %all-to-all-start.1 = ((f32[4,3,192,384]{3,2,1,0:T(8,128)}), f32[4,3,192,384]{3,2,1,0:T(8,128)S(1)}, u32[]{:S(2)}, u32[]{:S(2)}) async-start(f32[4,3,192,384]{3,2,1,0:T(8,128)} %get-tuple-element.141), calls=%async_computation.1 | async-start | bytes 7077888 | tf_op jit(solution)/shard_map/all_to_all | solution.py:509
  111.1 2.7 %collective-permute-start.12 = (f32[6,192,128]{2,1,0:T(8,128)}, f32[6,192,128]{2,1,0:T(8,128)}, u32[]{:S(2)}, u32[]{:S(2)}) collective-permute-start(f32[6,192,128]{2,1,0:T(8,128)} %collective-permute-done.4.rest_1_), channel_id=1, source_target_pairs={{0,1},{1,0},{2,3},{3,2},{4,5},{5,4},{6,7},{7,6},{8,9},{9,8},{10,11... | collective-permute-start | bytes 1769480 | tf_op jit(solution)/shard_map/ppermute | solution.py:499
  111.8 3.2 %collective-permute-start.13 = (f32[6,192,128]{2,1,0:T(8,128)}, f32[6,192,128]{2,1,0:T(8,128)}, u32[]{:S(2)}, u32[]{:S(2)}) collective-permute-start(f32[6,192,128]{2,1,0:T(8,128)} %collective-permute-done.3.rest_2_), channel_id=1, source_target_pairs={{0,1},{1,0},{2,3},{3,2},{4,5},{5,4},{6,7},{7,6},{8,9},{9,8},{10,11... | collective-permute-start | bytes 1769480 | tf_op jit(solution)/shard_map/ppermute | solution.py:499
  111.8 3.7 %collective-permute-start.14 = (f32[6,192,128]{2,1,0:T(8,128)}, f32[6,192,128]{2,1,0:T(8,128)}, u32[]{:S(2)}, u32[]{:S(2)}) collective-permute-start(f32[6,192,128]{2,1,0:T(8,128)} %collective-permute-done.5.rest_3_), channel_id=1, source_target_pairs={{0,1},{1,0},{2,3},{3,2},{4,5},{5,4},{6,7},{7,6},{8,9},{9,8},{10,11... | collective-permute-start | bytes 1769480 | tf_op jit(solution)/shard_map/ppermute | solution.py:499
  112.3 28.2 %collective-permute-start.9 = (f32[6,192,128]{2,1,0:T(8,128)}, f32[6,192,128]{2,1,0:T(8,128)}, u32[]{:S(2)}, u32[]{:S(2)}) collective-permute-start(f32[6,192,128]{2,1,0:T(8,128)} %get-tuple-element.123), channel_id=1, source_target_pairs={{0,4},{1,5},{2,6},{3,7},{4,0},{5,1},{6,2},{7,3},{8,12},{9,13},{10,... | collective-permute-start | bytes 1769480 | tf_op jit(solution)/shard_map/ppermute | solution.py:495
  112.3 28.2 %collective-permute-start.10 = (f32[6,192,128]{2,1,0:T(8,128)}, f32[6,192,128]{2,1,0:T(8,128)}, u32[]{:S(2)}, u32[]{:S(2)}) collective-permute-start(f32[6,192,128]{2,1,0:T(8,128)} %get-tuple-element.124), channel_id=1, source_target_pairs={{0,2},{1,3},{2,0},{3,1},{4,6},{5,7},{6,4},{7,5},{8,10},{9,11},{10,... | collective-permute-start | bytes 1769480 | tf_op jit(solution)/shard_map/ppermute | solution.py:495
  113.8 49.8 %collective-permute-start.11 = (f32[6,192,128]{2,1,0:T(8,128)}, f32[6,192,128]{2,1,0:T(8,128)}, u32[]{:S(2)}, u32[]{:S(2)}) collective-permute-start(f32[6,192,128]{2,1,0:T(8,128)} %get-tuple-element.125), channel_id=1, source_target_pairs={{0,6},{1,7},{2,4},{3,5},{4,2},{5,3},{6,0},{7,1},{8,14},{9,15},{10,... | collective-permute-start | bytes 1769480 | tf_op jit(solution)/shard_map/ppermute | solution.py:495
  138.1 25.5 %copy-start.19 = (f32[3,192,128]{2,1,0:T(8,128)S(1)}, f32[3,192,128]{2,1,0:T(8,128)}, u32[]{:S(2)}) copy-start(f32[3,192,128]{2,1,0:T(8,128)} %get-tuple-element.150) | copy-start | bytes 884740
  138.1 25.5 %copy-start.18 = (f32[3,192,128]{2,1,0:T(8,128)S(1)}, f32[3,192,128]{2,1,0:T(8,128)}, u32[]{:S(2)}) copy-start(f32[3,192,128]{2,1,0:T(8,128)} %get-tuple-element.151) | copy-start | bytes 884740
  138.1 28.8 %copy-start.17 = (f32[3,192,128]{2,1,0:T(8,128)S(1)}, f32[3,192,128]{2,1,0:T(8,128)}, u32[]{:S(2)}) copy-start(f32[3,192,128]{2,1,0:T(8,128)} %get-tuple-element.152) | copy-start | bytes 884740
  138.1 28.9 %copy-start.12 = (s32[1,192,12]{1,0,2:T(1,128)S(1)}, s32[1,192,12]{1,0,2:T(1,128)}, u32[]{:S(2)}) copy-start(s32[1,192,12]{1,0,2:T(1,128)} %param.9) | copy-start | bytes 27652
  163.6 14.1 %collective-permute-start.15 = (f32[3,192,128]{2,1,0:T(8,128)S(1)}, f32[3,192,128]{2,1,0:T(8,128)S(1)}, u32[]{:S(2)}, u32[]{:S(2)}) collective-permute-start(f32[3,192,128]{2,1,0:T(8,128)S(1)} %copy-done.19), channel_id=1, source_target_pairs={{0,4},{1,5},{2,6},{3,7},{4,0},{5,1},{6,2},{7,3},{8,12},{9,13},{10,... | collective-permute-start | bytes 884744 | tf_op jit(solution)/shard_map/ppermute | solution.py:495
  163.6 16.3 %collective-permute-start.16 = (f32[3,192,128]{2,1,0:T(8,128)S(1)}, f32[3,192,128]{2,1,0:T(8,128)S(1)}, u32[]{:S(2)}, u32[]{:S(2)}) collective-permute-start(f32[3,192,128]{2,1,0:T(8,128)S(1)} %copy-done.18), channel_id=1, source_target_pairs={{0,2},{1,3},{2,0},{3,1},{4,6},{5,7},{6,4},{7,5},{8,10},{9,11},{10,... | collective-permute-start | bytes 884744 | tf_op jit(solution)/shard_map/ppermute | solution.py:495
  166.9 25.1 %collective-permute-start.17 = (f32[3,192,128]{2,1,0:T(8,128)S(1)}, f32[3,192,128]{2,1,0:T(8,128)S(1)}, u32[]{:S(2)}, u32[]{:S(2)}) collective-permute-start(f32[3,192,128]{2,1,0:T(8,128)S(1)} %copy-done.17), channel_id=1, source_target_pairs={{0,6},{1,7},{2,4},{3,5},{4,2},{5,3},{6,0},{7,1},{8,14},{9,15},{10,... | collective-permute-start | bytes 884744 | tf_op jit(solution)/shard_map/ppermute | solution.py:495
  167.7 24.4 %copy-start.16 = (f32[3,192,128]{2,1,0:T(8,128)S(1)}, f32[3,192,128]{2,1,0:T(8,128)}, u32[]{:S(2)}) copy-start(f32[3,192,128]{2,1,0:T(8,128)} %get-tuple-element.162) | copy-start | bytes 884740
  167.7 24.4 %copy-start.15 = (f32[3,192,128]{2,1,0:T(8,128)S(1)}, f32[3,192,128]{2,1,0:T(8,128)}, u32[]{:S(2)}) copy-start(f32[3,192,128]{2,1,0:T(8,128)} %get-tuple-element.163) | copy-start | bytes 884740
  167.7 24.8 %copy-start.14 = (f32[3,192,128]{2,1,0:T(8,128)S(1)}, f32[3,192,128]{2,1,0:T(8,128)}, u32[]{:S(2)}) copy-start(f32[3,192,128]{2,1,0:T(8,128)} %get-tuple-element.164) | copy-start | bytes 884740
  192.1 18.2 %collective-permute-start.18 = (f32[3,192,128]{2,1,0:T(8,128)S(1)}, f32[3,192,128]{2,1,0:T(8,128)S(1)}, u32[]{:S(2)}, u32[]{:S(2)}) collective-permute-start(f32[3,192,128]{2,1,0:T(8,128)S(1)} %copy-done.16), channel_id=1, source_target_pairs={{0,4},{1,5},{2,6},{3,7},{4,0},{5,1},{6,2},{7,3},{8,12},{9,13},{10,... | collective-permute-start | bytes 884744 | tf_op jit(solution)/shard_map/ppermute | solution.py:495
  192.1 18.2 %collective-permute-start.19 = (f32[3,192,128]{2,1,0:T(8,128)S(1)}, f32[3,192,128]{2,1,0:T(8,128)}, u32[]{:S(2)}, u32[]{:S(2)}) collective-permute-start(f32[3,192,128]{2,1,0:T(8,128)S(1)} %copy-done.15), channel_id=1, source_target_pairs={{0,2},{1,3},{2,0},{3,1},{4,6},{5,7},{6,4},{7,5},{8,10},{9,11},{10,... | collective-permute-start | bytes 884744 | tf_op jit(solution)/shard_map/ppermute | solution.py:495
  192.5 25.1 %collective-permute-start.20 = (f32[3,192,128]{2,1,0:T(8,128)S(1)}, f32[3,192,128]{2,1,0:T(8,128)}, u32[]{:S(2)}, u32[]{:S(2)}) collective-permute-start(f32[3,192,128]{2,1,0:T(8,128)S(1)} %copy-done.14), channel_id=1, source_target_pairs={{0,6},{1,7},{2,4},{3,5},{4,2},{5,3},{6,0},{7,1},{8,14},{9,15},{10,... | collective-permute-start | bytes 884744 | tf_op jit(solution)/shard_map/ppermute | solution.py:495
  206.7 20.0 %all-to-all-start.2 = ((f32[4,192,384]{2,1,0:T(8,128)}), f32[4,192,384]{2,1,0:T(8,128)S(1)}, u32[]{:S(2)}, u32[]{:S(2)}) async-start(f32[4,192,384]{2,1,0:T(8,128)} %home_divergence.1), calls=%async_computation.2 | async-start | bytes 2359296 | tf_op jit(solution)/shard_map/all_to_all | solution.py:509
  (13 other events, 138.1 us)

commit v8 on v7

--- a/solution.py
+++ b/solution.py
@@ -487,7 +487,7 @@
         return lax.optimization_barrier((value, others))[0]
 
     chips = plan.chips
-    shifts = [2, 1, 3] if chips == 4 else list(range(1, chips))
+    shifts = [2, 3, 1] if chips == 4 else list(range(1, chips))
 
     def send_lines(blocks):
         got = {0: blocks[0]}

time: 230 us -> 230 us (level)
  starting transfers between devices: 29.2 us -> 32.2 us
  waiting for transfers between devices: 90.8 us -> 87.8 us
    ppermute x15, waiting for transfers between devices: 85.8 us -> 82.5 us  [send_lines(): lax.ppermute(blocks[s], 'pen', [(i, plan.to(i // CORES, s) * CORES + i %...]
    ppermute x15, starting transfers between devices: 13.8 us -> 16.4 us  [send_lines(): lax.ppermute(blocks[s], 'pen', [(i, plan.to(i // CORES, s) * CORES + i %...]
  transfers between devices with their start and end apart: 24 -> 24, of which waited for: 10 -> 12; matrix products, arithmetic and copies ran while one was open for 12% -> 12% of each run, Pallas kernels for 32% -> 32%
where the time goes in v8:
time: 230 us; the launch traced here: 228 us
  waiting for transfers between devices  87.8 us (38%)
  Pallas kernels  74.8 us (33%)
  starting transfers between devices  32.2 us (14%)
  local copies, waits for them, and re-layouts  18.5 us (8%)
  other arithmetic  13.5 us (6%)
    ppermute x15, waiting for transfers between devices, send_lines(): lax.ppermute(blocks[s], 'pen', [(i, plan.to(i // CORES, s) * CORES + i %...  82.5 us
    pallas_call x3, Pallas kernels, home_step(): pl.pallas_call(kernel, out_shape=jax.ShapeDtypeStruct((3, 1, rows, depth)...  28 us
    pallas_call x2, Pallas kernels, line_slopes(): pl.pallas_call(kernel, out_shape=shapes, in_specs=[SMEM, VMEM, VMEM] + [H...  20.1 us
    ppermute x15, starting transfers between devices, send_lines(): lax.ppermute(blocks[s], 'pen', [(i, plan.to(i // CORES, s) * CORES + i %...  16.4 us
    all_to_all x3, starting transfers between devices, exchange(): return lax.all_to_all(value, 'grp', 0, 0, tiled=True)  12.5 us
    another operation x2, local copies, waits for them, and re-layouts, cut_depth(): return jnp.moveaxis(value.reshape(*value.shape[:-1], grps, width), -2, 0)  11.2 us
    pallas_call x1, Pallas kernels, depth_terms(): pl.pallas_call(kernel, grid=(rows // step,), out_shape=[jax.ShapeDtypeStr...  10.2 us
    pallas_call x3, Pallas kernels, pack_lines(): pl.pallas_call(kernel, out_shape=[shape] * len(messages), in_specs=[SMEM,...  7.83 us
  transfers between devices with their start and end apart: 24, of which 12 were waited for; matrix products, arithmetic and copies ran while one was open for 12% of the time, Pallas kernels for 32%

profile of v8, /device:TPU:9, one launch (start us, length us, event | category | flops | bytes accessed | tf_op | source)
XLA Modules:
  0.0 227.8 jit_solution(17415924428735863137)
XLA Ops:
  2.7 2.4 %collective-permute-start = (f32[6,192,128]{2,1,0:T(8,128)}, f32[6,192,128]{2,1,0:T(8,128)S(1)}, u32[]{:S(2)}, u32[]{:S(2)}) collective-permute-start(f32[6,192,128]{2,1,0:T(8,128)} %pack_lines.3), channel_id=1, source_target_pairs={{0,4},{1,5},{2,6},{3,7},{4,0},{5,1},{6,2},{7,3},{8,12},{9,13},{10,... | collective-permute-start | bytes 1769480 | tf_op jit(solution)/shard_map/ppermute | solution.py:495
  5.1 2.8 %pack_lines.4 = (f32[6,192,128]{2,1,0:T(8,128)}, f32[6,192,128]{2,1,0:T(8,128)}, f32[6,192,128]{2,1,0:T(8,128)}) custom-call(s32[1]{0:T(128)} %bitcast.me_ref, f32[4,1,192,1536]{3,2,1,0:T(8,128)} %flow_ref.10), custom_call_target="tpu_custom_call" | custom-call | bytes 23592 | tf_op jit(solution)/shard_map/pack_lines/pallas_call | solution.py:135
  9.2 6.2 %reshape_squeeze.3 = f32[4,192,4,384]{3,2,1,0:T(4,128)} reshape(f32[4,1,192,1536]{3,2,1,0:T(8,128)} %flow_ref.10) | data formatting | bytes 9437184 | tf_op jit(solution)/shard_map/reshape;squeeze | solution.py:506
  15.4 5.0 %copy.36 = f32[4,192,4,384]{3,1,0,2:T(8,128)} copy(f32[4,192,4,384]{3,2,1,0:T(4,128)} %reshape_squeeze.3) | data formatting | bytes 9437184 | tf_op jit(solution)/shard_map/reshape;squeeze | solution.py:506
  20.4 5.1 %all-to-all-start = ((f32[4,4,192,384]{3,2,1,0:T(8,128)}), f32[4,4,192,384]{3,2,1,0:T(8,128)}, u32[]{:S(2)}, u32[]{:S(2)}) async-start(f32[4,4,192,384]{3,2,1,0:T(8,128)} %bitcast.18), calls=%async_computation | async-start | bytes 9437184 | tf_op jit(solution)/shard_map/all_to_all | solution.py:509
  27.6 6.9 %sort.23 = (s32[8192]{0:T(1024)S(1)}, f32[8192]{0:T(1024)}, s32[8192]{0:T(1024)}) sort(s32[8192]{0:T(1024)S(1)} %fusion.5, f32[8192]{0:T(1024)S(1)} %reshape.61, s32[8192]{0:T(1024)S(1)} %iota.19), dimensions={0}, to_apply=%region_0.1 | sort | flops 106496 | bytes 196608 | tf_op jit(solution)/shard_map/sort | solution.py:278
  37.5 3.0 %pack_lines.5 = (f32[6,192,128]{2,1,0:T(8,128)}, f32[6,192,128]{2,1,0:T(8,128)}, f32[6,192,128]{2,1,0:T(8,128)}, f32[6,192,128]{2,1,0:T(8,128)}) custom-call(s32[1]{0:T(128)} %bitcast.me_ref, f32[4,1,192,1536]{3,2,1,0:T(8,128)} %flow_ref.10), custom_call_target="tpu_custom_call" | custom-call | bytes 23592 | tf_op jit(solution)/shard_map/pack_lines/pallas_call | solution.py:135
  40.5 3.2 %collective-permute-done.rest_2_ = f32[6,192,128]{2,1,0:T(8,128)S(1)} collective-permute-done((f32[6,192,128]{2,1,0:T(8,128)}, f32[6,192,128]{2,1,0:T(8,128)S(1)}, u32[]{:S(2)}, u32[]{:S(2)}) %collective-permute-start) | collective-permute-done | bytes 589856 | tf_op jit(solution)/shard_map/ppermute | solution.py:495
  43.7 12.6 %collective-permute-done.1.rest_3_ = f32[6,192,128]{2,1,0:T(8,128)S(1)} collective-permute-done((f32[6,192,128]{2,1,0:T(8,128)}, f32[6,192,128]{2,1,0:T(8,128)S(1)}, u32[]{:S(2)}, u32[]{:S(2)}) %collective-permute-start.1) | collective-permute-done | bytes 589856 | tf_op jit(solution)/shard_map/ppermute | solution.py:495
  57.1 2.1 collective-permute-start.4
  62.8 10.0 %line_slopes.2 = (f32[6,192,128]{2,1,0:T(8,128)}, f32[6,192,128]{2,1,0:T(8,128)}, f32[6,192,128]{2,1,0:T(8,128)}, f32[6,192,128]{2,1,0:T(8,128)}) custom-call(s32[1]{0:T(128)} %bitcast.me_ref, bf16[2,768,768]{2,1,0:T(8,128)(2,1)} %constant.112.clone.high_ref, bf16[2,768,768]{2,1,0:T(8,128)(2,1)} %constant.113.clone.low_ref, ...), custom_call_target="tpu_custom_call" | custom-call | flops 27179088 | bytes 117964 | tf_op jit(solution)/shard_map/line_slopes/pallas_call | solution.py:195
  74.1 3.8 %all-to-all-done.in_ref = f32[4,4,192,384]{3,2,1,0:T(8,128)} async-done(((f32[4,4,192,384]{3,2,1,0:T(8,128)}), f32[4,4,192,384]{3,2,1,0:T(8,128)}, u32[]{:S(2)}, u32[]{:S(2)}) %all-to-all-start) | async-done | bytes 4718624 | tf_op jit(solution)/shard_map/all_to_all | solution.py:509
  78.0 5.7 %slab_terms.1 = (f32[4,3,192,384]{3,2,1,0:T(8,128)}, f32[4,192,384]{2,1,0:T(8,128)}) custom-call(f32[4,4,192,384]{3,2,1,0:T(8,128)} %all-to-all-done.in_ref), custom_call_target="tpu_custom_call" | custom-call | flops 188743 | bytes 94371 | tf_op jit(solution)/shard_map/slab_terms/pallas_call | solution.py:260
  83.7 3.9 %all-to-all-start.1 = ((f32[4,3,192,384]{3,2,1,0:T(8,128)}), f32[4,3,192,384]{3,2,1,0:T(8,128)S(1)}, u32[]{:S(2)}, u32[]{:S(2)}) async-start(f32[4,3,192,384]{3,2,1,0:T(8,128)} %get-tuple-element.141), calls=%async_computation.1 | async-start | bytes 7077888 | tf_op jit(solution)/shard_map/all_to_all | solution.py:509
  87.6 7.7 %collective-permute-done.3.rest_2_ = f32[6,192,128]{2,1,0:T(8,128)} collective-permute-done((f32[6,192,128]{2,1,0:T(8,128)}, f32[6,192,128]{2,1,0:T(8,128)}, u32[]{:S(2)}, u32[]{:S(2)}) %collective-permute-start.3) | collective-permute-done | bytes 589856 | tf_op jit(solution)/shard_map/ppermute | solution.py:495
  95.3 15.7 %collective-permute-done.4.rest_3_ = f32[6,192,128]{2,1,0:T(8,128)} collective-permute-done((f32[6,192,128]{2,1,0:T(8,128)}, f32[6,192,128]{2,1,0:T(8,128)}, u32[]{:S(2)}, u32[]{:S(2)}) %collective-permute-start.4) | collective-permute-done | bytes 589856 | tf_op jit(solution)/shard_map/ppermute | solution.py:495
  113.8 2.1 collective-permute-start.11
  115.9 10.1 %line_slopes.3 = (f32[3,192,128]{2,1,0:T(8,128)}, f32[3,192,128]{2,1,0:T(8,128)}, f32[3,192,128]{2,1,0:T(8,128)}, f32[3,192,128]{2,1,0:T(8,128)}, f32[3,192,128]...) custom-call(s32[1]{0:T(128)} %bitcast.me_ref, ...), custom_call_target="tpu_custom_call" | custom-call | flops 17666408448 | bytes 76677120 | tf_op jit(solution)/shard_map/line_slopes/pallas_call | solution.py:195
  125.9 10.2 %depth_terms.1 = (f32[3,192,1536]{2,1,0:T(8,128)}, f32[192,1536]{1,0:T(8,128)}) custom-call(f32[4,1,192,1536]{3,2,1,0:T(8,128)} %flow_ref.10, bf16[2,768,768]{2,1,0:T(8,128)(2,1)} %constant.112.clone.high_ref, bf16[2,768,768]{2,1,0:T(8,128)(2,1)} %constant.113.clone.low_ref), custom_call_target="tpu_custom_call" | custom-call | flops 54358180 | bytes 141557 | tf_op jit(solution)/shard_map/depth_terms/pallas_call | solution.py:233
  138.5 2.4 %sub.64.base_ref = f32[3,192,1536]{2,1,0:T(8,128)} subtract(f32[3,192,1536]{2,1,0:T(8,128)S(1)} %copy-done, f32[3,192,1536]{2,1,0:T(8,128)S(1)} %bitcast.19) | non-fusion elementwise | flops 884736 | bytes 10616832 | tf_op jit(solution)/shard_map/sub | solution.py:543
  141.0 9.9 %collective-permute-done.9.rest_7_.rest_11_.rest_2_ = f32[6,192,128]{2,1,0:T(8,128)} collective-permute-done((f32[6,192,128]{2,1,0:T(8,128)}, f32[6,192,128]{2,1,0:T(8,128)}, u32[]{:S(2)}, u32[]{:S(2)}) %collective-permute-start.9) | collective-permute-done | bytes 589856 | tf_op jit(solution)/shard_map/ppermute | solution.py:495
  150.9 12.7 %collective-permute-done.10.rest_8_.rest_12_.rest_3_ = f32[6,192,128]{2,1,0:T(8,128)} collective-permute-done((f32[6,192,128]{2,1,0:T(8,128)}, f32[6,192,128]{2,1,0:T(8,128)}, u32[]{:S(2)}, u32[]{:S(2)}) %collective-permute-start.10) | collective-permute-done | bytes 589856 | tf_op jit(solution)/shard_map/ppermute | solution.py:495
  163.6 2.2 collective-permute-start.16
  167.9 9.9 %home_step.3.rest_9_ = f32[3,1,192,1536]{3,2,1,0:T(8,128)} custom-call(s32[1]{0:T(128)} %bitcast.me_ref, s32[44]{0:T(128)} %copy-done.13, s32[44]{0:T(128)} %compare_select_fusion.tile_ref, f32[4,1,192,1536]{3,2,1,0:T(8,128)} %flow_ref.10, f32[3,192,1536]{2,1,0:T(8,128)} %sub.64.base_ref, s32[32,1,256]{2,1,0:T(1,128)} %bitcast.29, s32[32,1,256]{2,1,0:T(1,128)} %bitcast.26, ...), custom_call_target="tpu_custom_call" | custom-call | flops 44291848 | bytes 58982 | tf_op jit(solution)/shard_map/home_step/pallas_call | solution.py:461
  177.8 4.5 %collective-permute-done.15.rest_7_ = f32[3,192,128]{2,1,0:T(8,128)S(1)} collective-permute-done((f32[3,192,128]{2,1,0:T(8,128)S(1)}, f32[3,192,128]{2,1,0:T(8,128)S(1)}, u32[]{:S(2)}, u32[]{:S(2)}) %collective-permute-start.15) | collective-permute-done | bytes 294944 | tf_op jit(solution)/shard_map/ppermute | solution.py:495
  182.3 9.7 %collective-permute-done.16.rest_8_ = f32[3,192,128]{2,1,0:T(8,128)S(1)} collective-permute-done((f32[3,192,128]{2,1,0:T(8,128)S(1)}, f32[3,192,128]{2,1,0:T(8,128)S(1)}, u32[]{:S(2)}, u32[]{:S(2)}) %collective-permute-start.16) | collective-permute-done | bytes 294944 | tf_op jit(solution)/shard_map/ppermute | solution.py:495
  192.1 3.4 %collective-permute-start.20 = (f32[3,192,128]{2,1,0:T(8,128)S(1)}, f32[3,192,128]{2,1,0:T(8,128)}, u32[]{:S(2)}, u32[]{:S(2)}) collective-permute-start(f32[3,192,128]{2,1,0:T(8,128)S(1)} %copy-done.14), channel_id=1, source_target_pairs={{0,2},{1,3},{2,0},{3,1},{4,6},{5,7},{6,4},{7,5},{8,10},{9,11},{10,... | collective-permute-start | bytes 884744 | tf_op jit(solution)/shard_map/ppermute | solution.py:495
  195.6 9.1 %home_step.4.rest_9_ = f32[3,1,192,1536]{3,2,1,0:T(8,128)} custom-call(s32[1]{0:T(128)} %bitcast.me_ref, s32[44]{0:T(128)} %copy-done.13, s32[44]{0:T(128)} %compare_select_fusion.tile_ref, f32[4,1,192,1536]{3,2,1,0:T(8,128)} %flow_ref.10, f32[3,192,1536]{2,1,0:T(8,128)} %sub.64.base_ref, s32[32,1,256]{2,1,0:T(1,128)} %bitcast.30, ...), custom_call_target="tpu_custom_call", output_to_operand_aliasing={{}: (14, {})} | custom-call | flops 44291848 | bytes 58982 | tf_op jit(solution)/shard_map/home_step/pallas_call | solution.py:461
  204.7 2.9 %home_divergence.1 = f32[4,192,384]{2,1,0:T(8,128)} custom-call(s32[1]{0:T(128)} %bitcast.me_ref, f32[192,1536]{1,0:T(8,128)} %get-tuple-element.176.slope_ref, f32[6,192,128]{2,1,0:T(8,128)} %get-tuple-element.157.rest_5_.rest_9_.rest_0_, f32[6,192,128]{2,1,0:T(8,128)} %collective-permute-done.11.rest_6_.rest_10_.rest_1_, ...), custom_call_target="tpu_custom_call" | custom-call | bytes 35389 | tf_op jit(solution)/shard_map/home_divergence/pallas_call | solution.py:331
  207.6 3.5 %all-to-all-start.2 = ((f32[4,192,384]{2,1,0:T(8,128)}), f32[4,192,384]{2,1,0:T(8,128)S(1)}, u32[]{:S(2)}, u32[]{:S(2)}) async-start(f32[4,192,384]{2,1,0:T(8,128)} %home_divergence.1), calls=%async_computation.2 | async-start | bytes 2359296 | tf_op jit(solution)/shard_map/all_to_all | solution.py:509
  211.3 6.3 %collective-permute-done.19.rest_8_ = f32[3,192,128]{2,1,0:T(8,128)} collective-permute-done((f32[3,192,128]{2,1,0:T(8,128)S(1)}, f32[3,192,128]{2,1,0:T(8,128)}, u32[]{:S(2)}, u32[]{:S(2)}) %collective-permute-start.19) | collective-permute-done | bytes 294944 | tf_op jit(solution)/shard_map/ppermute | solution.py:495
  217.6 9.1 %home_step.5 = f32[3,1,192,1536]{3,2,1,0:T(8,128)} custom-call(s32[1]{0:T(128)} %bitcast.me_ref, s32[44]{0:T(128)} %copy-done.13, s32[44]{0:T(128)} %compare_select_fusion.tile_ref, f32[4,1,192,1536]{3,2,1,0:T(8,128)} %flow_ref.10, f32[3,192,1536]{2,1,0:T(8,128)} %sub.64.base_ref, s32[32,1,256]{2,1,0:T(1,128)} %bitcast.31, ...), custom_call_target="tpu_custom_call", output_to_operand_aliasing={{}: (14, {})} | custom-call | flops 44291850240 | bytes 58982400 | tf_op jit(solution)/shard_map/home_step/pallas_call | solution.py:461
  (102 shorter events, 22.5 us)
Async XLA Ops:
  2.7 41.0 %collective-permute-start = (f32[6,192,128]{2,1,0:T(8,128)}, f32[6,192,128]{2,1,0:T(8,128)S(1)}, u32[]{:S(2)}, u32[]{:S(2)}) collective-permute-start(f32[6,192,128]{2,1,0:T(8,128)} %pack_lines.3), channel_id=1, source_target_pairs={{0,4},{1,5},{2,6},{3,7},{4,0},{5,1},{6,2},{7,3},{8,12},{9,13},{10,... | collective-permute-start | bytes 1769480 | tf_op jit(solution)/shard_map/ppermute | solution.py:495
  7.9 48.4 %collective-permute-start.1 = (f32[6,192,128]{2,1,0:T(8,128)}, f32[6,192,128]{2,1,0:T(8,128)S(1)}, u32[]{:S(2)}, u32[]{:S(2)}) collective-permute-start(f32[6,192,128]{2,1,0:T(8,128)} %get-tuple-element.93), channel_id=1, source_target_pairs={{0,6},{1,7},{2,4},{3,5},{4,2},{5,3},{6,0},{7,1},{8,14},{9,15},{10,... | collective-permute-start | bytes 1769480 | tf_op jit(solution)/shard_map/ppermute | solution.py:495
  8.0 48.3 %collective-permute-start.2 = (f32[6,192,128]{2,1,0:T(8,128)}, f32[6,192,128]{2,1,0:T(8,128)S(1)}, u32[]{:S(2)}, u32[]{:S(2)}) collective-permute-start(f32[6,192,128]{2,1,0:T(8,128)} %get-tuple-element.94), channel_id=1, source_target_pairs={{0,2},{1,3},{2,0},{3,1},{4,6},{5,7},{6,4},{7,5},{8,10},{9,11},{10,... | collective-permute-start | bytes 1769480 | tf_op jit(solution)/shard_map/ppermute | solution.py:495
  20.4 57.6 %all-to-all-start = ((f32[4,4,192,384]{3,2,1,0:T(8,128)}), f32[4,4,192,384]{3,2,1,0:T(8,128)}, u32[]{:S(2)}, u32[]{:S(2)}) async-start(f32[4,4,192,384]{3,2,1,0:T(8,128)} %bitcast.18), calls=%async_computation | async-start | bytes 9437184 | tf_op jit(solution)/shard_map/all_to_all | solution.py:509
  35.6 20.8 %copy-start.13 = (s32[44]{0:T(128)}, s32[44]{0:T(128)S(1)}, u32[]{:S(2)}) copy-start(s32[44]{0:T(128)S(1)} %broadcast_minimum_fusion.chunk_ref) | copy-start | bytes 532
  56.5 4.2 %collective-permute-start.7 = (f32[18,192,128]{2,1,0:T(8,128)S(1)}, f32[18,192,128]{2,1,0:T(8,128)S(1)}, u32[]{:S(2)}, u32[]{:S(2)}) collective-permute-start(f32[18,192,128]{2,1,0:T(8,128)S(1)} %pad_maximum_fusion), channel_id=1, source_target_pairs={{0,1},{1,0},{2,3},{3,2},{4,5},{5,4},{6,7},{7,6},{8,9},{9,8},{10,11... | collective-permute-start | bytes 5308424 | tf_op jit(solution)/shard_map/ppermute | solution.py:499
  57.0 4.9 %collective-permute-start.6 = (f32[6,192,128]{2,1,0:T(8,128)S(1)}, f32[6,192,128]{2,1,0:T(8,128)S(1)}, u32[]{:S(2)}, u32[]{:S(2)}) collective-permute-start(f32[6,192,128]{2,1,0:T(8,128)S(1)} %copy-done.5), channel_id=1, source_target_pairs={{0,1},{1,0},{2,3},{3,2},{4,5},{5,4},{6,7},{7,6},{8,9},{9,8},{10,11... | collective-permute-start | bytes 1769480 | tf_op jit(solution)/shard_map/ppermute | solution.py:499
  57.1 38.2 %collective-permute-start.3 = (f32[6,192,128]{2,1,0:T(8,128)}, f32[6,192,128]{2,1,0:T(8,128)}, u32[]{:S(2)}, u32[]{:S(2)}) collective-permute-start(f32[6,192,128]{2,1,0:T(8,128)} %get-tuple-element.107), channel_id=1, source_target_pairs={{0,4},{1,5},{2,6},{3,7},{4,0},{5,1},{6,2},{7,3},{8,12},{9,13},{10,... | collective-permute-start | bytes 1769480 | tf_op jit(solution)/shard_map/ppermute | solution.py:495
  57.1 54.0 %collective-permute-start.4 = (f32[6,192,128]{2,1,0:T(8,128)}, f32[6,192,128]{2,1,0:T(8,128)}, u32[]{:S(2)}, u32[]{:S(2)}) collective-permute-start(f32[6,192,128]{2,1,0:T(8,128)} %get-tuple-element.108), channel_id=1, source_target_pairs={{0,6},{1,7},{2,4},{3,5},{4,2},{5,3},{6,0},{7,1},{8,14},{9,15},{10,... | collective-permute-start | bytes 1769480 | tf_op jit(solution)/shard_map/ppermute | solution.py:495
  59.2 51.8 %collective-permute-start.5 = (f32[6,192,128]{2,1,0:T(8,128)}, f32[6,192,128]{2,1,0:T(8,128)}, u32[]{:S(2)}, u32[]{:S(2)}) collective-permute-start(f32[6,192,128]{2,1,0:T(8,128)} %get-tuple-element.109), channel_id=1, source_target_pairs={{0,2},{1,3},{2,0},{3,1},{4,6},{5,7},{6,4},{7,5},{8,10},{9,11},{10,... | collective-permute-start | bytes 1769480 | tf_op jit(solution)/shard_map/ppermute | solution.py:495
  72.8 38.3 %collective-permute-start.8 = (f32[6,192,128]{2,1,0:T(8,128)}, f32[6,192,128]{2,1,0:T(8,128)}, u32[]{:S(2)}, u32[]{:S(2)}) collective-permute-start(f32[6,192,128]{2,1,0:T(8,128)} %get-tuple-element.126.rest_0_), channel_id=1, source_target_pairs={{0,1},{1,0},{2,3},{3,2},{4,5},{5,4},{6,7},{7,6},{8,9},{9,8},{10,11... | collective-permute-start | bytes 1769480 | tf_op jit(solution)/shard_map/ppermute | solution.py:499
  83.7 52.5 %all-to-all-start.1 = ((f32[4,3,192,384]{3,2,1,0:T(8,128)}), f32[4,3,192,384]{3,2,1,0:T(8,128)S(1)}, u32[]{:S(2)}, u32[]{:S(2)}) async-start(f32[4,3,192,384]{3,2,1,0:T(8,128)} %get-tuple-element.141), calls=%async_computation.1 | async-start | bytes 7077888 | tf_op jit(solution)/shard_map/all_to_all | solution.py:509
  111.1 2.7 %collective-permute-start.12 = (f32[6,192,128]{2,1,0:T(8,128)}, f32[6,192,128]{2,1,0:T(8,128)}, u32[]{:S(2)}, u32[]{:S(2)}) collective-permute-start(f32[6,192,128]{2,1,0:T(8,128)} %collective-permute-done.5.rest_1_), channel_id=1, source_target_pairs={{0,1},{1,0},{2,3},{3,2},{4,5},{5,4},{6,7},{7,6},{8,9},{9,8},{10,11... | collective-permute-start | bytes 1769480 | tf_op jit(solution)/shard_map/ppermute | solution.py:499
  111.8 4.1 %collective-permute-start.13 = (f32[6,192,128]{2,1,0:T(8,128)}, f32[6,192,128]{2,1,0:T(8,128)}, u32[]{:S(2)}, u32[]{:S(2)}) collective-permute-start(f32[6,192,128]{2,1,0:T(8,128)} %collective-permute-done.3.rest_2_), channel_id=1, source_target_pairs={{0,1},{1,0},{2,3},{3,2},{4,5},{5,4},{6,7},{7,6},{8,9},{9,8},{10,11... | collective-permute-start | bytes 1769480 | tf_op jit(solution)/shard_map/ppermute | solution.py:499
  111.9 4.0 %collective-permute-start.14 = (f32[6,192,128]{2,1,0:T(8,128)}, f32[6,192,128]{2,1,0:T(8,128)}, u32[]{:S(2)}, u32[]{:S(2)}) collective-permute-start(f32[6,192,128]{2,1,0:T(8,128)} %collective-permute-done.4.rest_3_), channel_id=1, source_target_pairs={{0,1},{1,0},{2,3},{3,2},{4,5},{5,4},{6,7},{7,6},{8,9},{9,8},{10,11... | collective-permute-start | bytes 1769480 | tf_op jit(solution)/shard_map/ppermute | solution.py:499
  112.3 38.5 %collective-permute-start.9 = (f32[6,192,128]{2,1,0:T(8,128)}, f32[6,192,128]{2,1,0:T(8,128)}, u32[]{:S(2)}, u32[]{:S(2)}) collective-permute-start(f32[6,192,128]{2,1,0:T(8,128)} %get-tuple-element.123), channel_id=1, source_target_pairs={{0,4},{1,5},{2,6},{3,7},{4,0},{5,1},{6,2},{7,3},{8,12},{9,13},{10,... | collective-permute-start | bytes 1769480 | tf_op jit(solution)/shard_map/ppermute | solution.py:495
  112.3 51.2 %collective-permute-start.10 = (f32[6,192,128]{2,1,0:T(8,128)}, f32[6,192,128]{2,1,0:T(8,128)}, u32[]{:S(2)}, u32[]{:S(2)}) collective-permute-start(f32[6,192,128]{2,1,0:T(8,128)} %get-tuple-element.124), channel_id=1, source_target_pairs={{0,6},{1,7},{2,4},{3,5},{4,2},{5,3},{6,0},{7,1},{8,14},{9,15},{10,... | collective-permute-start | bytes 1769480 | tf_op jit(solution)/shard_map/ppermute | solution.py:495
  113.8 49.8 %collective-permute-start.11 = (f32[6,192,128]{2,1,0:T(8,128)}, f32[6,192,128]{2,1,0:T(8,128)}, u32[]{:S(2)}, u32[]{:S(2)}) collective-permute-start(f32[6,192,128]{2,1,0:T(8,128)} %get-tuple-element.125), channel_id=1, source_target_pairs={{0,2},{1,3},{2,0},{3,1},{4,6},{5,7},{6,4},{7,5},{8,10},{9,11},{10,... | collective-permute-start | bytes 1769480 | tf_op jit(solution)/shard_map/ppermute | solution.py:495
  138.5 25.1 %copy-start.19 = (f32[3,192,128]{2,1,0:T(8,128)S(1)}, f32[3,192,128]{2,1,0:T(8,128)}, u32[]{:S(2)}) copy-start(f32[3,192,128]{2,1,0:T(8,128)} %get-tuple-element.150) | copy-start | bytes 884740
  138.5 25.1 %copy-start.18 = (f32[3,192,128]{2,1,0:T(8,128)S(1)}, f32[3,192,128]{2,1,0:T(8,128)}, u32[]{:S(2)}) copy-start(f32[3,192,128]{2,1,0:T(8,128)} %get-tuple-element.151) | copy-start | bytes 884740
  138.5 27.3 %copy-start.17 = (f32[3,192,128]{2,1,0:T(8,128)S(1)}, f32[3,192,128]{2,1,0:T(8,128)}, u32[]{:S(2)}) copy-start(f32[3,192,128]{2,1,0:T(8,128)} %get-tuple-element.152) | copy-start | bytes 884740
  138.5 28.6 %copy-start.12 = (s32[1,192,12]{1,0,2:T(1,128)S(1)}, s32[1,192,12]{1,0,2:T(1,128)}, u32[]{:S(2)}) copy-start(s32[1,192,12]{1,0,2:T(1,128)} %param.9) | copy-start | bytes 27652
  163.6 18.7 %collective-permute-start.15 = (f32[3,192,128]{2,1,0:T(8,128)S(1)}, f32[3,192,128]{2,1,0:T(8,128)S(1)}, u32[]{:S(2)}, u32[]{:S(2)}) collective-permute-start(f32[3,192,128]{2,1,0:T(8,128)S(1)} %copy-done.19), channel_id=1, source_target_pairs={{0,4},{1,5},{2,6},{3,7},{4,0},{5,1},{6,2},{7,3},{8,12},{9,13},{10,... | collective-permute-start | bytes 884744 | tf_op jit(solution)/shard_map/ppermute | solution.py:495
  163.6 28.4 %collective-permute-start.16 = (f32[3,192,128]{2,1,0:T(8,128)S(1)}, f32[3,192,128]{2,1,0:T(8,128)S(1)}, u32[]{:S(2)}, u32[]{:S(2)}) collective-permute-start(f32[3,192,128]{2,1,0:T(8,128)S(1)} %copy-done.18), channel_id=1, source_target_pairs={{0,6},{1,7},{2,4},{3,5},{4,2},{5,3},{6,0},{7,1},{8,14},{9,15},{10,... | collective-permute-start | bytes 884744 | tf_op jit(solution)/shard_map/ppermute | solution.py:495
  165.8 26.2 %collective-permute-start.17 = (f32[3,192,128]{2,1,0:T(8,128)S(1)}, f32[3,192,128]{2,1,0:T(8,128)S(1)}, u32[]{:S(2)}, u32[]{:S(2)}) collective-permute-start(f32[3,192,128]{2,1,0:T(8,128)S(1)} %copy-done.17), channel_id=1, source_target_pairs={{0,2},{1,3},{2,0},{3,1},{4,6},{5,7},{6,4},{7,5},{8,10},{9,11},{10,... | collective-permute-start | bytes 884744 | tf_op jit(solution)/shard_map/ppermute | solution.py:495
  167.9 24.1 %copy-start.16 = (f32[3,192,128]{2,1,0:T(8,128)S(1)}, f32[3,192,128]{2,1,0:T(8,128)}, u32[]{:S(2)}) copy-start(f32[3,192,128]{2,1,0:T(8,128)} %get-tuple-element.162) | copy-start | bytes 884740
  167.9 24.2 %copy-start.15 = (f32[3,192,128]{2,1,0:T(8,128)S(1)}, f32[3,192,128]{2,1,0:T(8,128)}, u32[]{:S(2)}) copy-start(f32[3,192,128]{2,1,0:T(8,128)} %get-tuple-element.163) | copy-start | bytes 884740
  167.9 24.3 %copy-start.14 = (f32[3,192,128]{2,1,0:T(8,128)S(1)}, f32[3,192,128]{2,1,0:T(8,128)}, u32[]{:S(2)}) copy-start(f32[3,192,128]{2,1,0:T(8,128)} %get-tuple-element.164) | copy-start | bytes 884740
  192.0 19.3 %collective-permute-start.18 = (f32[3,192,128]{2,1,0:T(8,128)S(1)}, f32[3,192,128]{2,1,0:T(8,128)S(1)}, u32[]{:S(2)}, u32[]{:S(2)}) collective-permute-start(f32[3,192,128]{2,1,0:T(8,128)S(1)} %copy-done.16), channel_id=1, source_target_pairs={{0,4},{1,5},{2,6},{3,7},{4,0},{5,1},{6,2},{7,3},{8,12},{9,13},{10,... | collective-permute-start | bytes 884744 | tf_op jit(solution)/shard_map/ppermute | solution.py:495
  192.1 25.6 %collective-permute-start.19 = (f32[3,192,128]{2,1,0:T(8,128)S(1)}, f32[3,192,128]{2,1,0:T(8,128)}, u32[]{:S(2)}, u32[]{:S(2)}) collective-permute-start(f32[3,192,128]{2,1,0:T(8,128)S(1)} %copy-done.15), channel_id=1, source_target_pairs={{0,6},{1,7},{2,4},{3,5},{4,2},{5,3},{6,0},{7,1},{8,14},{9,15},{10,... | collective-permute-start | bytes 884744 | tf_op jit(solution)/shard_map/ppermute | solution.py:495
  192.1 25.5 %collective-permute-start.20 = (f32[3,192,128]{2,1,0:T(8,128)S(1)}, f32[3,192,128]{2,1,0:T(8,128)}, u32[]{:S(2)}, u32[]{:S(2)}) collective-permute-start(f32[3,192,128]{2,1,0:T(8,128)S(1)} %copy-done.14), channel_id=1, source_target_pairs={{0,2},{1,3},{2,0},{3,1},{4,6},{5,7},{6,4},{7,5},{8,10},{9,11},{10,... | collective-permute-start | bytes 884744 | tf_op jit(solution)/shard_map/ppermute | solution.py:495
  207.6 19.1 %all-to-all-start.2 = ((f32[4,192,384]{2,1,0:T(8,128)}), f32[4,192,384]{2,1,0:T(8,128)S(1)}, u32[]{:S(2)}, u32[]{:S(2)}) async-start(f32[4,192,384]{2,1,0:T(8,128)} %home_divergence.1), calls=%async_computation.2 | async-start | bytes 2359296 | tf_op jit(solution)/shard_map/all_to_all | solution.py:509
  (13 other events, 106.0 us)
